TPU v7x, 32 devices: a whole 2x2x4 slice. The times are simulated.
32 devices in a mesh: states: 16 (over z, y, x), act: 2 (over core).
Axes of the slice: x: 2, y: 2, z: 4, core: 2. Of those that a mesh axis runs over, the one named last changes fastest.
Arguments:
- transitions: float32 [4, 256, 2, 128, 128], P('act', 'states'), may hold values from 7.8125e-05 to 0.01953125
- columns: int32 [4, 256, 2], P(None, 'states'), may hold values from 0 to 255, as said below
- targets: int32 [32768, 128], P('states'), may hold values 0 or 1
Outputs:
- values: float32 [32768, 128], P('states')
Inputs may be any that keep to these rules, and one draw needn't show every extreme that they name: columns[a, b, t] = (b + d) mod 256 with |d| <= 8; both d = 8 and d = -8 occur in every draw.
All inputs are finite; a program needn't handle non-finite values. No bound on the sum of `targets` on one device may be relied on, other than what follows from the above.
Results may differ from a plain program's by a relative error of at most 0.0003.
Values sent between devices are 32-bit elements; how exact they have to be, the bound alone decides.
No kernel may reach another device: no remote copies, remote signals or barrier semaphores. Data moves between devices by JAX's collectives and lax.ppermute only.
A program may use at most 64 MiB of HBM per device.

v0:
```python
import jax
import jax.numpy as jnp
from jax import lax
from jax.sharding import PartitionSpec as P

REACH = 8
SWEEPS = 12


def extended(cells, sides, width):
    for axis, dim in sides:
        count = lax.axis_size(axis)
        head = lax.slice_in_dim(cells, 0, width, axis=dim)
        tail = lax.slice_in_dim(cells, cells.shape[dim] - width, cells.shape[dim], axis=dim)
        cells = jnp.concatenate(
            [
                lax.ppermute(tail, axis, [(i, (i + 1) % count) for i in range(count)]),
                cells,
                lax.ppermute(head, axis, [((i + 1) % count, i) for i in range(count)]),
            ],
            axis=dim,
        )
    return cells


def extend(panel, width_rows):
    return extended(panel, (("states", 0),), width_rows)


def products(padded, tiles, column_ids, first_block, total_blocks, tile_rows, target_sets):
    blocks = padded.reshape(-1, tile_rows, target_sets)
    local_index = (column_ids - first_block + REACH) % total_blocks
    picked = blocks[local_index]
    values = jnp.einsum("arbij,arbjk->arik", tiles, picked, precision=lax.Precision.HIGHEST)
    return jnp.max(values, axis=0)


def per_device(transitions, columns, targets):
    acts_here = transitions.shape[0]
    row_blocks = transitions.shape[1]
    tile_rows = transitions.shape[3]
    target_sets = targets.shape[1]
    total_blocks = row_blocks * lax.axis_size("states")
    first_block = lax.axis_index("states") * row_blocks
    width_rows = REACH * tile_rows
    target_hit = targets == 1
    panel = targets.astype(jnp.float32)
    own_columns = lax.dynamic_slice_in_dim(columns, lax.axis_index("act") * acts_here, acts_here, 0)

    def action_sweep(sweep_index, current):
        padded = extend(current, width_rows)
        largest = products(
            padded, transitions, own_columns, first_block, total_blocks, tile_rows, target_sets
        )
        merged = lax.pmax(largest, "act")
        return jnp.where(target_hit, jnp.float32(1.0), merged.reshape(-1, target_sets))

    panel = lax.fori_loop(0, SWEEPS, action_sweep, panel)
    return panel


def solution(mesh):
    return jax.shard_map(
        per_device,
        mesh=mesh,
        in_specs=(P("act", "states", None, None, None), P(None, "states", None), P("states", None)),
        out_specs=P("states", None),
        check_vma=False,
    )
```

profile of v0, /device:TPU:0, one launch (start us, length us, event | category | flops | bytes accessed | tf_op | source)
XLA Modules:
  0.0 783.1 jit_solution(12247602693530813975)
XLA Ops:
  9.9 765.4 %while.12 = (s32[]{:T(128)}, f32[2048,128]{1,0:T(8,128)S(1)}, s32[]{:T(128)}, s32[2,16,2]{1,2,0:T(2,128)S(1)}, f32[2,16,2,128,128]{4,3,2,1,0:T(8,128)}, /*index=5*/pred[2048,128]{1,0:T(8,128)(4,1)S(1)}, s32[]{:T(128)}) while((s32[]{:T(128)}, f32[2048,128]{1,0:T(8,128)S(1)}, s32[]{:T(128)}, s32[2,16,2]{1,2,0:T(2,128)S(1)}, ...), condition=%wide.region_3.4_spmd, body=%wide.region_0.3_spmd.sunk | while | flops 1612449792 | bytes 41162980 | solution.py:58
  10.0 7.0 collective-permute-start
  17.2 11.0 %collective-permute-done = f32[1024,128]{1,0:T(8,128)S(1)} collective-permute-done((f32[1024,128]{1,0:T(8,128)S(1)}, f32[1024,128]{1,0:T(8,128)S(1)}, u32[]{:S(2)}, u32[]{:S(2)}) %collective-permute-start) | collective-permute-done | bytes 524320 | tf_op jit(solution)/shard_map/while/body/eval_jaxpr/ppermute | solution.py:19
  29.0 8.3 %collective-permute-done.1 = f32[1024,128]{1,0:T(8,128)} collective-permute-done((f32[1024,128]{1,0:T(8,128)S(1)}, f32[1024,128]{1,0:T(8,128)}, u32[]{:S(2)}, u32[]{:S(2)}) %collective-permute-start.1) | collective-permute-done | bytes 524320 | tf_op jit(solution)/shard_map/while/body/eval_jaxpr/ppermute | solution.py:17
  38.6 2.8 gather_fusion
  41.4 10.3 %bitcast_reduce_fusion.2 = f32[16,128,128]{2,1,0:T(8,128)S(1)} fusion(f32[2,16,2,128,128]{4,3,2,1,0:T(8,128)} %bitcast.33, f32[2,16,2,128,128]{4,3,2,1,0:T(8,128)} %get-tuple-element.157), kind=kOutput, calls=%fused_computation.2.clone.1 | convolution fusion | flops 1610874880 | bytes 9437184 | tf_op jit(solution)/shard_map/while/body/eval_jaxpr/arbij,arbjk->arik/dot_general | solution.py:34
  53.1 20.2 %all-reduce.2.cloned.1.call-done = f32[2048,128]{1,0:T(8,128)} async-done(((f32[2048,128]{1,0:T(8,128)}), f32[2048,128]{1,0:T(8,128)}) %all-reduce.2.cloned.1.call-update) | async-done | bytes 1048592 | tf_op jit(solution)/shard_map/while/body/eval_jaxpr/pmax | solution.py:55
  74.7 5.5 collective-permute-start
  80.4 11.4 %collective-permute-done = f32[1024,128]{1,0:T(8,128)S(1)} collective-permute-done((f32[1024,128]{1,0:T(8,128)S(1)}, f32[1024,128]{1,0:T(8,128)S(1)}, u32[]{:S(2)}, u32[]{:S(2)}) %collective-permute-start) | collective-permute-done | bytes 524320 | tf_op jit(solution)/shard_map/while/body/eval_jaxpr/ppermute | solution.py:19
  92.6 8.6 %collective-permute-done.1 = f32[1024,128]{1,0:T(8,128)} collective-permute-done((f32[1024,128]{1,0:T(8,128)S(1)}, f32[1024,128]{1,0:T(8,128)}, u32[]{:S(2)}, u32[]{:S(2)}) %collective-permute-start.1) | collective-permute-done | bytes 524320 | tf_op jit(solution)/shard_map/while/body/eval_jaxpr/ppermute | solution.py:17
  105.3 10.3 %bitcast_reduce_fusion.2 = f32[16,128,128]{2,1,0:T(8,128)S(1)} fusion(f32[2,16,2,128,128]{4,3,2,1,0:T(8,128)} %bitcast.33, f32[2,16,2,128,128]{4,3,2,1,0:T(8,128)} %get-tuple-element.157), kind=kOutput, calls=%fused_computation.2.clone.1 | convolution fusion | flops 1610874880 | bytes 9437184 | tf_op jit(solution)/shard_map/while/body/eval_jaxpr/arbij,arbjk->arik/dot_general | solution.py:34
  117.0 20.0 %all-reduce.2.cloned.1.call-done = f32[2048,128]{1,0:T(8,128)} async-done(((f32[2048,128]{1,0:T(8,128)}), f32[2048,128]{1,0:T(8,128)}) %all-reduce.2.cloned.1.call-update) | async-done | bytes 1048592 | tf_op jit(solution)/shard_map/while/body/eval_jaxpr/pmax | solution.py:55
  138.4 5.5 collective-permute-start
  144.1 11.4 %collective-permute-done = f32[1024,128]{1,0:T(8,128)S(1)} collective-permute-done((f32[1024,128]{1,0:T(8,128)S(1)}, f32[1024,128]{1,0:T(8,128)S(1)}, u32[]{:S(2)}, u32[]{:S(2)}) %collective-permute-start) | collective-permute-done | bytes 524320 | tf_op jit(solution)/shard_map/while/body/eval_jaxpr/ppermute | solution.py:19
  156.3 8.6 %collective-permute-done.1 = f32[1024,128]{1,0:T(8,128)} collective-permute-done((f32[1024,128]{1,0:T(8,128)S(1)}, f32[1024,128]{1,0:T(8,128)}, u32[]{:S(2)}, u32[]{:S(2)}) %collective-permute-start.1) | collective-permute-done | bytes 524320 | tf_op jit(solution)/shard_map/while/body/eval_jaxpr/ppermute | solution.py:17
  169.0 10.3 %bitcast_reduce_fusion.2 = f32[16,128,128]{2,1,0:T(8,128)S(1)} fusion(f32[2,16,2,128,128]{4,3,2,1,0:T(8,128)} %bitcast.33, f32[2,16,2,128,128]{4,3,2,1,0:T(8,128)} %get-tuple-element.157), kind=kOutput, calls=%fused_computation.2.clone.1 | convolution fusion | flops 1610874880 | bytes 9437184 | tf_op jit(solution)/shard_map/while/body/eval_jaxpr/arbij,arbjk->arik/dot_general | solution.py:34
  180.7 20.0 %all-reduce.2.cloned.1.call-done = f32[2048,128]{1,0:T(8,128)} async-done(((f32[2048,128]{1,0:T(8,128)}), f32[2048,128]{1,0:T(8,128)}) %all-reduce.2.cloned.1.call-update) | async-done | bytes 1048592 | tf_op jit(solution)/shard_map/while/body/eval_jaxpr/pmax | solution.py:55
  202.1 5.5 collective-permute-start
  207.8 11.4 %collective-permute-done = f32[1024,128]{1,0:T(8,128)S(1)} collective-permute-done((f32[1024,128]{1,0:T(8,128)S(1)}, f32[1024,128]{1,0:T(8,128)S(1)}, u32[]{:S(2)}, u32[]{:S(2)}) %collective-permute-start) | collective-permute-done | bytes 524320 | tf_op jit(solution)/shard_map/while/body/eval_jaxpr/ppermute | solution.py:19
  220.0 8.6 %collective-permute-done.1 = f32[1024,128]{1,0:T(8,128)} collective-permute-done((f32[1024,128]{1,0:T(8,128)S(1)}, f32[1024,128]{1,0:T(8,128)}, u32[]{:S(2)}, u32[]{:S(2)}) %collective-permute-start.1) | collective-permute-done | bytes 524320 | tf_op jit(solution)/shard_map/while/body/eval_jaxpr/ppermute | solution.py:17
  232.7 10.3 %bitcast_reduce_fusion.2 = f32[16,128,128]{2,1,0:T(8,128)S(1)} fusion(f32[2,16,2,128,128]{4,3,2,1,0:T(8,128)} %bitcast.33, f32[2,16,2,128,128]{4,3,2,1,0:T(8,128)} %get-tuple-element.157), kind=kOutput, calls=%fused_computation.2.clone.1 | convolution fusion | flops 1610874880 | bytes 9437184 | tf_op jit(solution)/shard_map/while/body/eval_jaxpr/arbij,arbjk->arik/dot_general | solution.py:34
  244.4 20.0 %all-reduce.2.cloned.1.call-done = f32[2048,128]{1,0:T(8,128)} async-done(((f32[2048,128]{1,0:T(8,128)}), f32[2048,128]{1,0:T(8,128)}) %all-reduce.2.cloned.1.call-update) | async-done | bytes 1048592 | tf_op jit(solution)/shard_map/while/body/eval_jaxpr/pmax | solution.py:55
  265.8 5.5 collective-permute-start
  271.5 11.4 %collective-permute-done = f32[1024,128]{1,0:T(8,128)S(1)} collective-permute-done((f32[1024,128]{1,0:T(8,128)S(1)}, f32[1024,128]{1,0:T(8,128)S(1)}, u32[]{:S(2)}, u32[]{:S(2)}) %collective-permute-start) | collective-permute-done | bytes 524320 | tf_op jit(solution)/shard_map/while/body/eval_jaxpr/ppermute | solution.py:19
  283.7 8.6 %collective-permute-done.1 = f32[1024,128]{1,0:T(8,128)} collective-permute-done((f32[1024,128]{1,0:T(8,128)S(1)}, f32[1024,128]{1,0:T(8,128)}, u32[]{:S(2)}, u32[]{:S(2)}) %collective-permute-start.1) | collective-permute-done | bytes 524320 | tf_op jit(solution)/shard_map/while/body/eval_jaxpr/ppermute | solution.py:17
  296.4 10.3 %bitcast_reduce_fusion.2 = f32[16,128,128]{2,1,0:T(8,128)S(1)} fusion(f32[2,16,2,128,128]{4,3,2,1,0:T(8,128)} %bitcast.33, f32[2,16,2,128,128]{4,3,2,1,0:T(8,128)} %get-tuple-element.157), kind=kOutput, calls=%fused_computation.2.clone.1 | convolution fusion | flops 1610874880 | bytes 9437184 | tf_op jit(solution)/shard_map/while/body/eval_jaxpr/arbij,arbjk->arik/dot_general | solution.py:34
  308.1 20.0 %all-reduce.2.cloned.1.call-done = f32[2048,128]{1,0:T(8,128)} async-done(((f32[2048,128]{1,0:T(8,128)}), f32[2048,128]{1,0:T(8,128)}) %all-reduce.2.cloned.1.call-update) | async-done | bytes 1048592 | tf_op jit(solution)/shard_map/while/body/eval_jaxpr/pmax | solution.py:55
  329.5 5.5 collective-permute-start
  335.2 11.4 %collective-permute-done = f32[1024,128]{1,0:T(8,128)S(1)} collective-permute-done((f32[1024,128]{1,0:T(8,128)S(1)}, f32[1024,128]{1,0:T(8,128)S(1)}, u32[]{:S(2)}, u32[]{:S(2)}) %collective-permute-start) | collective-permute-done | bytes 524320 | tf_op jit(solution)/shard_map/while/body/eval_jaxpr/ppermute | solution.py:19
  347.4 8.6 %collective-permute-done.1 = f32[1024,128]{1,0:T(8,128)} collective-permute-done((f32[1024,128]{1,0:T(8,128)S(1)}, f32[1024,128]{1,0:T(8,128)}, u32[]{:S(2)}, u32[]{:S(2)}) %collective-permute-start.1) | collective-permute-done | bytes 524320 | tf_op jit(solution)/shard_map/while/body/eval_jaxpr/ppermute | solution.py:17
  360.1 10.3 %bitcast_reduce_fusion.2 = f32[16,128,128]{2,1,0:T(8,128)S(1)} fusion(f32[2,16,2,128,128]{4,3,2,1,0:T(8,128)} %bitcast.33, f32[2,16,2,128,128]{4,3,2,1,0:T(8,128)} %get-tuple-element.157), kind=kOutput, calls=%fused_computation.2.clone.1 | convolution fusion | flops 1610874880 | bytes 9437184 | tf_op jit(solution)/shard_map/while/body/eval_jaxpr/arbij,arbjk->arik/dot_general | solution.py:34
  371.8 20.0 %all-reduce.2.cloned.1.call-done = f32[2048,128]{1,0:T(8,128)} async-done(((f32[2048,128]{1,0:T(8,128)}), f32[2048,128]{1,0:T(8,128)}) %all-reduce.2.cloned.1.call-update) | async-done | bytes 1048592 | tf_op jit(solution)/shard_map/while/body/eval_jaxpr/pmax | solution.py:55
  393.2 5.5 collective-permute-start
  398.9 11.4 %collective-permute-done = f32[1024,128]{1,0:T(8,128)S(1)} collective-permute-done((f32[1024,128]{1,0:T(8,128)S(1)}, f32[1024,128]{1,0:T(8,128)S(1)}, u32[]{:S(2)}, u32[]{:S(2)}) %collective-permute-start) | collective-permute-done | bytes 524320 | tf_op jit(solution)/shard_map/while/body/eval_jaxpr/ppermute | solution.py:19
  411.1 8.6 %collective-permute-done.1 = f32[1024,128]{1,0:T(8,128)} collective-permute-done((f32[1024,128]{1,0:T(8,128)S(1)}, f32[1024,128]{1,0:T(8,128)}, u32[]{:S(2)}, u32[]{:S(2)}) %collective-permute-start.1) | collective-permute-done | bytes 524320 | tf_op jit(solution)/shard_map/while/body/eval_jaxpr/ppermute | solution.py:17
  423.8 10.3 %bitcast_reduce_fusion.2 = f32[16,128,128]{2,1,0:T(8,128)S(1)} fusion(f32[2,16,2,128,128]{4,3,2,1,0:T(8,128)} %bitcast.33, f32[2,16,2,128,128]{4,3,2,1,0:T(8,128)} %get-tuple-element.157), kind=kOutput, calls=%fused_computation.2.clone.1 | convolution fusion | flops 1610874880 | bytes 9437184 | tf_op jit(solution)/shard_map/while/body/eval_jaxpr/arbij,arbjk->arik/dot_general | solution.py:34
  435.5 20.0 %all-reduce.2.cloned.1.call-done = f32[2048,128]{1,0:T(8,128)} async-done(((f32[2048,128]{1,0:T(8,128)}), f32[2048,128]{1,0:T(8,128)}) %all-reduce.2.cloned.1.call-update) | async-done | bytes 1048592 | tf_op jit(solution)/shard_map/while/body/eval_jaxpr/pmax | solution.py:55
  456.9 5.5 collective-permute-start
  462.6 11.4 %collective-permute-done = f32[1024,128]{1,0:T(8,128)S(1)} collective-permute-done((f32[1024,128]{1,0:T(8,128)S(1)}, f32[1024,128]{1,0:T(8,128)S(1)}, u32[]{:S(2)}, u32[]{:S(2)}) %collective-permute-start) | collective-permute-done | bytes 524320 | tf_op jit(solution)/shard_map/while/body/eval_jaxpr/ppermute | solution.py:19
  474.8 8.6 %collective-permute-done.1 = f32[1024,128]{1,0:T(8,128)} collective-permute-done((f32[1024,128]{1,0:T(8,128)S(1)}, f32[1024,128]{1,0:T(8,128)}, u32[]{:S(2)}, u32[]{:S(2)}) %collective-permute-start.1) | collective-permute-done | bytes 524320 | tf_op jit(solution)/shard_map/while/body/eval_jaxpr/ppermute | solution.py:17
  487.5 10.3 %bitcast_reduce_fusion.2 = f32[16,128,128]{2,1,0:T(8,128)S(1)} fusion(f32[2,16,2,128,128]{4,3,2,1,0:T(8,128)} %bitcast.33, f32[2,16,2,128,128]{4,3,2,1,0:T(8,128)} %get-tuple-element.157), kind=kOutput, calls=%fused_computation.2.clone.1 | convolution fusion | flops 1610874880 | bytes 9437184 | tf_op jit(solution)/shard_map/while/body/eval_jaxpr/arbij,arbjk->arik/dot_general | solution.py:34
  499.2 20.0 %all-reduce.2.cloned.1.call-done = f32[2048,128]{1,0:T(8,128)} async-done(((f32[2048,128]{1,0:T(8,128)}), f32[2048,128]{1,0:T(8,128)}) %all-reduce.2.cloned.1.call-update) | async-done | bytes 1048592 | tf_op jit(solution)/shard_map/while/body/eval_jaxpr/pmax | solution.py:55
  520.6 5.5 collective-permute-start
  526.3 11.4 %collective-permute-done = f32[1024,128]{1,0:T(8,128)S(1)} collective-permute-done((f32[1024,128]{1,0:T(8,128)S(1)}, f32[1024,128]{1,0:T(8,128)S(1)}, u32[]{:S(2)}, u32[]{:S(2)}) %collective-permute-start) | collective-permute-done | bytes 524320 | tf_op jit(solution)/shard_map/while/body/eval_jaxpr/ppermute | solution.py:19
  538.5 8.6 %collective-permute-done.1 = f32[1024,128]{1,0:T(8,128)} collective-permute-done((f32[1024,128]{1,0:T(8,128)S(1)}, f32[1024,128]{1,0:T(8,128)}, u32[]{:S(2)}, u32[]{:S(2)}) %collective-permute-start.1) | collective-permute-done | bytes 524320 | tf_op jit(solution)/shard_map/while/body/eval_jaxpr/ppermute | solution.py:17
  551.2 10.3 %bitcast_reduce_fusion.2 = f32[16,128,128]{2,1,0:T(8,128)S(1)} fusion(f32[2,16,2,128,128]{4,3,2,1,0:T(8,128)} %bitcast.33, f32[2,16,2,128,128]{4,3,2,1,0:T(8,128)} %get-tuple-element.157), kind=kOutput, calls=%fused_computation.2.clone.1 | convolution fusion | flops 1610874880 | bytes 9437184 | tf_op jit(solution)/shard_map/while/body/eval_jaxpr/arbij,arbjk->arik/dot_general | solution.py:34
  562.9 20.0 %all-reduce.2.cloned.1.call-done = f32[2048,128]{1,0:T(8,128)} async-done(((f32[2048,128]{1,0:T(8,128)}), f32[2048,128]{1,0:T(8,128)}) %all-reduce.2.cloned.1.call-update) | async-done | bytes 1048592 | tf_op jit(solution)/shard_map/while/body/eval_jaxpr/pmax | solution.py:55
  584.3 5.5 collective-permute-start
  590.0 11.4 %collective-permute-done = f32[1024,128]{1,0:T(8,128)S(1)} collective-permute-done((f32[1024,128]{1,0:T(8,128)S(1)}, f32[1024,128]{1,0:T(8,128)S(1)}, u32[]{:S(2)}, u32[]{:S(2)}) %collective-permute-start) | collective-permute-done | bytes 524320 | tf_op jit(solution)/shard_map/while/body/eval_jaxpr/ppermute | solution.py:19
  602.2 8.6 %collective-permute-done.1 = f32[1024,128]{1,0:T(8,128)} collective-permute-done((f32[1024,128]{1,0:T(8,128)S(1)}, f32[1024,128]{1,0:T(8,128)}, u32[]{:S(2)}, u32[]{:S(2)}) %collective-permute-start.1) | collective-permute-done | bytes 524320 | tf_op jit(solution)/shard_map/while/body/eval_jaxpr/ppermute | solution.py:17
  614.9 10.3 %bitcast_reduce_fusion.2 = f32[16,128,128]{2,1,0:T(8,128)S(1)} fusion(f32[2,16,2,128,128]{4,3,2,1,0:T(8,128)} %bitcast.33, f32[2,16,2,128,128]{4,3,2,1,0:T(8,128)} %get-tuple-element.157), kind=kOutput, calls=%fused_computation.2.clone.1 | convolution fusion | flops 1610874880 | bytes 9437184 | tf_op jit(solution)/shard_map/while/body/eval_jaxpr/arbij,arbjk->arik/dot_general | solution.py:34
  626.6 20.0 %all-reduce.2.cloned.1.call-done = f32[2048,128]{1,0:T(8,128)} async-done(((f32[2048,128]{1,0:T(8,128)}), f32[2048,128]{1,0:T(8,128)}) %all-reduce.2.cloned.1.call-update) | async-done | bytes 1048592 | tf_op jit(solution)/shard_map/while/body/eval_jaxpr/pmax | solution.py:55
  648.0 5.5 collective-permute-start
  653.7 11.4 %collective-permute-done = f32[1024,128]{1,0:T(8,128)S(1)} collective-permute-done((f32[1024,128]{1,0:T(8,128)S(1)}, f32[1024,128]{1,0:T(8,128)S(1)}, u32[]{:S(2)}, u32[]{:S(2)}) %collective-permute-start) | collective-permute-done | bytes 524320 | tf_op jit(solution)/shard_map/while/body/eval_jaxpr/ppermute | solution.py:19
  665.9 8.6 %collective-permute-done.1 = f32[1024,128]{1,0:T(8,128)} collective-permute-done((f32[1024,128]{1,0:T(8,128)S(1)}, f32[1024,128]{1,0:T(8,128)}, u32[]{:S(2)}, u32[]{:S(2)}) %collective-permute-start.1) | collective-permute-done | bytes 524320 | tf_op jit(solution)/shard_map/while/body/eval_jaxpr/ppermute | solution.py:17
  675.9 2.8 gather_fusion
  678.6 10.3 %bitcast_reduce_fusion.2 = f32[16,128,128]{2,1,0:T(8,128)S(1)} fusion(f32[2,16,2,128,128]{4,3,2,1,0:T(8,128)} %bitcast.33, f32[2,16,2,128,128]{4,3,2,1,0:T(8,128)} %get-tuple-element.157), kind=kOutput, calls=%fused_computation.2.clone.1 | convolution fusion | flops 1610874880 | bytes 9437184 | tf_op jit(solution)/shard_map/while/body/eval_jaxpr/arbij,arbjk->arik/dot_general | solution.py:34
  690.3 20.0 %all-reduce.2.cloned.1.call-done = f32[2048,128]{1,0:T(8,128)} async-done(((f32[2048,128]{1,0:T(8,128)}), f32[2048,128]{1,0:T(8,128)}) %all-reduce.2.cloned.1.call-update) | async-done | bytes 1048592 | tf_op jit(solution)/shard_map/while/body/eval_jaxpr/pmax | solution.py:55
  711.8 5.5 collective-permute-start
  717.4 11.4 %collective-permute-done = f32[1024,128]{1,0:T(8,128)S(1)} collective-permute-done((f32[1024,128]{1,0:T(8,128)S(1)}, f32[1024,128]{1,0:T(8,128)S(1)}, u32[]{:S(2)}, u32[]{:S(2)}) %collective-permute-start) | collective-permute-done | bytes 524320 | tf_op jit(solution)/shard_map/while/body/eval_jaxpr/ppermute | solution.py:19
  729.6 8.6 %collective-permute-done.1 = f32[1024,128]{1,0:T(8,128)} collective-permute-done((f32[1024,128]{1,0:T(8,128)S(1)}, f32[1024,128]{1,0:T(8,128)}, u32[]{:S(2)}, u32[]{:S(2)}) %collective-permute-start.1) | collective-permute-done | bytes 524320 | tf_op jit(solution)/shard_map/while/body/eval_jaxpr/ppermute | solution.py:17
  739.6 2.8 gather_fusion
  742.3 10.3 %bitcast_reduce_fusion.2 = f32[16,128,128]{2,1,0:T(8,128)S(1)} fusion(f32[2,16,2,128,128]{4,3,2,1,0:T(8,128)} %bitcast.33, f32[2,16,2,128,128]{4,3,2,1,0:T(8,128)} %get-tuple-element.157), kind=kOutput, calls=%fused_computation.2.clone.1 | convolution fusion | flops 1610874880 | bytes 9437184 | tf_op jit(solution)/shard_map/while/body/eval_jaxpr/arbij,arbjk->arik/dot_general | solution.py:34
  754.0 20.0 %all-reduce.2.cloned.1.call-done = f32[2048,128]{1,0:T(8,128)} async-done(((f32[2048,128]{1,0:T(8,128)}), f32[2048,128]{1,0:T(8,128)}) %all-reduce.2.cloned.1.call-update) | async-done | bytes 1048592 | tf_op jit(solution)/shard_map/while/body/eval_jaxpr/pmax | solution.py:55
  (172 shorter events, 90.4 us)
Async XLA Ops:
  6.5 0.7 copy-start
  9.9 63.4 %all-reduce.2.cloned.1.call-start = ((), (), s32[]{:S(2)}) async-start(), calls=%async_computation | async-start | bytes 2097152 | tf_op jit(solution)/shard_map/while/body/eval_jaxpr/pmax | solution.py:55
  10.0 18.2 %collective-permute-start = (f32[1024,128]{1,0:T(8,128)S(1)}, f32[1024,128]{1,0:T(8,128)S(1)}, u32[]{:S(2)}, u32[]{:S(2)}) collective-permute-start(f32[1024,128]{1,0:T(8,128)S(1)} %get-tuple-element.137), channel_id=1, source_target_pairs={{2,0},{4,2},{6,4},{8,6},{10,8},{12,10},{14,12},{16,14},{18,16},{20... | collective-permute-start | bytes 1572872 | tf_op jit(solution)/shard_map/while/body/eval_jaxpr/ppermute | solution.py:19
  17.0 20.3 %collective-permute-start.1 = (f32[1024,128]{1,0:T(8,128)S(1)}, f32[1024,128]{1,0:T(8,128)}, u32[]{:S(2)}, u32[]{:S(2)}) collective-permute-start(f32[1024,128]{1,0:T(8,128)S(1)} %get-tuple-element.138), channel_id=1, source_target_pairs={{0,2},{2,4},{4,6},{6,8},{8,10},{10,12},{12,14},{14,16},{16,18},{18... | collective-permute-start | bytes 1572872 | tf_op jit(solution)/shard_map/while/body/eval_jaxpr/ppermute | solution.py:17
  28.2 0.8 copy-start.2
  74.6 62.4 %all-reduce.2.cloned.1.call-start = ((), (), s32[]{:S(2)}) async-start(), calls=%async_computation | async-start | bytes 2097152 | tf_op jit(solution)/shard_map/while/body/eval_jaxpr/pmax | solution.py:55
  74.7 17.1 %collective-permute-start = (f32[1024,128]{1,0:T(8,128)S(1)}, f32[1024,128]{1,0:T(8,128)S(1)}, u32[]{:S(2)}, u32[]{:S(2)}) collective-permute-start(f32[1024,128]{1,0:T(8,128)S(1)} %get-tuple-element.137), channel_id=1, source_target_pairs={{2,0},{4,2},{6,4},{8,6},{10,8},{12,10},{14,12},{16,14},{18,16},{20... | collective-permute-start | bytes 1572872 | tf_op jit(solution)/shard_map/while/body/eval_jaxpr/ppermute | solution.py:19
  80.2 21.0 %collective-permute-start.1 = (f32[1024,128]{1,0:T(8,128)S(1)}, f32[1024,128]{1,0:T(8,128)}, u32[]{:S(2)}, u32[]{:S(2)}) collective-permute-start(f32[1024,128]{1,0:T(8,128)S(1)} %get-tuple-element.138), channel_id=1, source_target_pairs={{0,2},{2,4},{4,6},{6,8},{8,10},{10,12},{12,14},{14,16},{16,18},{18... | collective-permute-start | bytes 1572872 | tf_op jit(solution)/shard_map/while/body/eval_jaxpr/ppermute | solution.py:17
  91.8 0.8 copy-start.2
  138.3 62.4 %all-reduce.2.cloned.1.call-start = ((), (), s32[]{:S(2)}) async-start(), calls=%async_computation | async-start | bytes 2097152 | tf_op jit(solution)/shard_map/while/body/eval_jaxpr/pmax | solution.py:55
  138.4 17.1 %collective-permute-start = (f32[1024,128]{1,0:T(8,128)S(1)}, f32[1024,128]{1,0:T(8,128)S(1)}, u32[]{:S(2)}, u32[]{:S(2)}) collective-permute-start(f32[1024,128]{1,0:T(8,128)S(1)} %get-tuple-element.137), channel_id=1, source_target_pairs={{2,0},{4,2},{6,4},{8,6},{10,8},{12,10},{14,12},{16,14},{18,16},{20... | collective-permute-start | bytes 1572872 | tf_op jit(solution)/shard_map/while/body/eval_jaxpr/ppermute | solution.py:19
  143.9 21.0 %collective-permute-start.1 = (f32[1024,128]{1,0:T(8,128)S(1)}, f32[1024,128]{1,0:T(8,128)}, u32[]{:S(2)}, u32[]{:S(2)}) collective-permute-start(f32[1024,128]{1,0:T(8,128)S(1)} %get-tuple-element.138), channel_id=1, source_target_pairs={{0,2},{2,4},{4,6},{6,8},{8,10},{10,12},{12,14},{14,16},{16,18},{18... | collective-permute-start | bytes 1572872 | tf_op jit(solution)/shard_map/while/body/eval_jaxpr/ppermute | solution.py:17
  155.5 0.8 copy-start.2
  202.0 62.4 %all-reduce.2.cloned.1.call-start = ((), (), s32[]{:S(2)}) async-start(), calls=%async_computation | async-start | bytes 2097152 | tf_op jit(solution)/shard_map/while/body/eval_jaxpr/pmax | solution.py:55
  202.1 17.1 %collective-permute-start = (f32[1024,128]{1,0:T(8,128)S(1)}, f32[1024,128]{1,0:T(8,128)S(1)}, u32[]{:S(2)}, u32[]{:S(2)}) collective-permute-start(f32[1024,128]{1,0:T(8,128)S(1)} %get-tuple-element.137), channel_id=1, source_target_pairs={{2,0},{4,2},{6,4},{8,6},{10,8},{12,10},{14,12},{16,14},{18,16},{20... | collective-permute-start | bytes 1572872 | tf_op jit(solution)/shard_map/while/body/eval_jaxpr/ppermute | solution.py:19
  207.6 21.0 %collective-permute-start.1 = (f32[1024,128]{1,0:T(8,128)S(1)}, f32[1024,128]{1,0:T(8,128)}, u32[]{:S(2)}, u32[]{:S(2)}) collective-permute-start(f32[1024,128]{1,0:T(8,128)S(1)} %get-tuple-element.138), channel_id=1, source_target_pairs={{0,2},{2,4},{4,6},{6,8},{8,10},{10,12},{12,14},{14,16},{16,18},{18... | collective-permute-start | bytes 1572872 | tf_op jit(solution)/shard_map/while/body/eval_jaxpr/ppermute | solution.py:17
  219.2 0.8 copy-start.2
  265.7 62.4 %all-reduce.2.cloned.1.call-start = ((), (), s32[]{:S(2)}) async-start(), calls=%async_computation | async-start | bytes 2097152 | tf_op jit(solution)/shard_map/while/body/eval_jaxpr/pmax | solution.py:55
  265.8 17.1 %collective-permute-start = (f32[1024,128]{1,0:T(8,128)S(1)}, f32[1024,128]{1,0:T(8,128)S(1)}, u32[]{:S(2)}, u32[]{:S(2)}) collective-permute-start(f32[1024,128]{1,0:T(8,128)S(1)} %get-tuple-element.137), channel_id=1, source_target_pairs={{2,0},{4,2},{6,4},{8,6},{10,8},{12,10},{14,12},{16,14},{18,16},{20... | collective-permute-start | bytes 1572872 | tf_op jit(solution)/shard_map/while/body/eval_jaxpr/ppermute | solution.py:19
  271.3 21.0 %collective-permute-start.1 = (f32[1024,128]{1,0:T(8,128)S(1)}, f32[1024,128]{1,0:T(8,128)}, u32[]{:S(2)}, u32[]{:S(2)}) collective-permute-start(f32[1024,128]{1,0:T(8,128)S(1)} %get-tuple-element.138), channel_id=1, source_target_pairs={{0,2},{2,4},{4,6},{6,8},{8,10},{10,12},{12,14},{14,16},{16,18},{18... | collective-permute-start | bytes 1572872 | tf_op jit(solution)/shard_map/while/body/eval_jaxpr/ppermute | solution.py:17
  282.9 0.8 copy-start.2
  329.4 62.4 %all-reduce.2.cloned.1.call-start = ((), (), s32[]{:S(2)}) async-start(), calls=%async_computation | async-start | bytes 2097152 | tf_op jit(solution)/shard_map/while/body/eval_jaxpr/pmax | solution.py:55
  329.5 17.1 %collective-permute-start = (f32[1024,128]{1,0:T(8,128)S(1)}, f32[1024,128]{1,0:T(8,128)S(1)}, u32[]{:S(2)}, u32[]{:S(2)}) collective-permute-start(f32[1024,128]{1,0:T(8,128)S(1)} %get-tuple-element.137), channel_id=1, source_target_pairs={{2,0},{4,2},{6,4},{8,6},{10,8},{12,10},{14,12},{16,14},{18,16},{20... | collective-permute-start | bytes 1572872 | tf_op jit(solution)/shard_map/while/body/eval_jaxpr/ppermute | solution.py:19
  335.0 21.0 %collective-permute-start.1 = (f32[1024,128]{1,0:T(8,128)S(1)}, f32[1024,128]{1,0:T(8,128)}, u32[]{:S(2)}, u32[]{:S(2)}) collective-permute-start(f32[1024,128]{1,0:T(8,128)S(1)} %get-tuple-element.138), channel_id=1, source_target_pairs={{0,2},{2,4},{4,6},{6,8},{8,10},{10,12},{12,14},{14,16},{16,18},{18... | collective-permute-start | bytes 1572872 | tf_op jit(solution)/shard_map/while/body/eval_jaxpr/ppermute | solution.py:17
  346.6 0.8 copy-start.2
  393.1 62.4 %all-reduce.2.cloned.1.call-start = ((), (), s32[]{:S(2)}) async-start(), calls=%async_computation | async-start | bytes 2097152 | tf_op jit(solution)/shard_map/while/body/eval_jaxpr/pmax | solution.py:55
  393.2 17.1 %collective-permute-start = (f32[1024,128]{1,0:T(8,128)S(1)}, f32[1024,128]{1,0:T(8,128)S(1)}, u32[]{:S(2)}, u32[]{:S(2)}) collective-permute-start(f32[1024,128]{1,0:T(8,128)S(1)} %get-tuple-element.137), channel_id=1, source_target_pairs={{2,0},{4,2},{6,4},{8,6},{10,8},{12,10},{14,12},{16,14},{18,16},{20... | collective-permute-start | bytes 1572872 | tf_op jit(solution)/shard_map/while/body/eval_jaxpr/ppermute | solution.py:19
  398.7 21.0 %collective-permute-start.1 = (f32[1024,128]{1,0:T(8,128)S(1)}, f32[1024,128]{1,0:T(8,128)}, u32[]{:S(2)}, u32[]{:S(2)}) collective-permute-start(f32[1024,128]{1,0:T(8,128)S(1)} %get-tuple-element.138), channel_id=1, source_target_pairs={{0,2},{2,4},{4,6},{6,8},{8,10},{10,12},{12,14},{14,16},{16,18},{18... | collective-permute-start | bytes 1572872 | tf_op jit(solution)/shard_map/while/body/eval_jaxpr/ppermute | solution.py:17
  410.3 0.8 copy-start.2
  456.8 62.4 %all-reduce.2.cloned.1.call-start = ((), (), s32[]{:S(2)}) async-start(), calls=%async_computation | async-start | bytes 2097152 | tf_op jit(solution)/shard_map/while/body/eval_jaxpr/pmax | solution.py:55
  456.9 17.1 %collective-permute-start = (f32[1024,128]{1,0:T(8,128)S(1)}, f32[1024,128]{1,0:T(8,128)S(1)}, u32[]{:S(2)}, u32[]{:S(2)}) collective-permute-start(f32[1024,128]{1,0:T(8,128)S(1)} %get-tuple-element.137), channel_id=1, source_target_pairs={{2,0},{4,2},{6,4},{8,6},{10,8},{12,10},{14,12},{16,14},{18,16},{20... | collective-permute-start | bytes 1572872 | tf_op jit(solution)/shard_map/while/body/eval_jaxpr/ppermute | solution.py:19
  462.4 21.0 %collective-permute-start.1 = (f32[1024,128]{1,0:T(8,128)S(1)}, f32[1024,128]{1,0:T(8,128)}, u32[]{:S(2)}, u32[]{:S(2)}) collective-permute-start(f32[1024,128]{1,0:T(8,128)S(1)} %get-tuple-element.138), channel_id=1, source_target_pairs={{0,2},{2,4},{4,6},{6,8},{8,10},{10,12},{12,14},{14,16},{16,18},{18... | collective-permute-start | bytes 1572872 | tf_op jit(solution)/shard_map/while/body/eval_jaxpr/ppermute | solution.py:17
  474.0 0.8 copy-start.2
  520.5 62.4 %all-reduce.2.cloned.1.call-start = ((), (), s32[]{:S(2)}) async-start(), calls=%async_computation | async-start | bytes 2097152 | tf_op jit(solution)/shard_map/while/body/eval_jaxpr/pmax | solution.py:55
  520.6 17.1 %collective-permute-start = (f32[1024,128]{1,0:T(8,128)S(1)}, f32[1024,128]{1,0:T(8,128)S(1)}, u32[]{:S(2)}, u32[]{:S(2)}) collective-permute-start(f32[1024,128]{1,0:T(8,128)S(1)} %get-tuple-element.137), channel_id=1, source_target_pairs={{2,0},{4,2},{6,4},{8,6},{10,8},{12,10},{14,12},{16,14},{18,16},{20... | collective-permute-start | bytes 1572872 | tf_op jit(solution)/shard_map/while/body/eval_jaxpr/ppermute | solution.py:19
  526.1 21.0 %collective-permute-start.1 = (f32[1024,128]{1,0:T(8,128)S(1)}, f32[1024,128]{1,0:T(8,128)}, u32[]{:S(2)}, u32[]{:S(2)}) collective-permute-start(f32[1024,128]{1,0:T(8,128)S(1)} %get-tuple-element.138), channel_id=1, source_target_pairs={{0,2},{2,4},{4,6},{6,8},{8,10},{10,12},{12,14},{14,16},{16,18},{18... | collective-permute-start | bytes 1572872 | tf_op jit(solution)/shard_map/while/body/eval_jaxpr/ppermute | solution.py:17
  537.7 0.8 copy-start.2
  584.2 62.4 %all-reduce.2.cloned.1.call-start = ((), (), s32[]{:S(2)}) async-start(), calls=%async_computation | async-start | bytes 2097152 | tf_op jit(solution)/shard_map/while/body/eval_jaxpr/pmax | solution.py:55
  584.3 17.1 %collective-permute-start = (f32[1024,128]{1,0:T(8,128)S(1)}, f32[1024,128]{1,0:T(8,128)S(1)}, u32[]{:S(2)}, u32[]{:S(2)}) collective-permute-start(f32[1024,128]{1,0:T(8,128)S(1)} %get-tuple-element.137), channel_id=1, source_target_pairs={{2,0},{4,2},{6,4},{8,6},{10,8},{12,10},{14,12},{16,14},{18,16},{20... | collective-permute-start | bytes 1572872 | tf_op jit(solution)/shard_map/while/body/eval_jaxpr/ppermute | solution.py:19
  589.8 21.0 %collective-permute-start.1 = (f32[1024,128]{1,0:T(8,128)S(1)}, f32[1024,128]{1,0:T(8,128)}, u32[]{:S(2)}, u32[]{:S(2)}) collective-permute-start(f32[1024,128]{1,0:T(8,128)S(1)} %get-tuple-element.138), channel_id=1, source_target_pairs={{0,2},{2,4},{4,6},{6,8},{8,10},{10,12},{12,14},{14,16},{16,18},{18... | collective-permute-start | bytes 1572872 | tf_op jit(solution)/shard_map/while/body/eval_jaxpr/ppermute | solution.py:17
  601.5 0.8 copy-start.2
  647.9 62.4 %all-reduce.2.cloned.1.call-start = ((), (), s32[]{:S(2)}) async-start(), calls=%async_computation | async-start | bytes 2097152 | tf_op jit(solution)/shard_map/while/body/eval_jaxpr/pmax | solution.py:55
  648.0 17.1 %collective-permute-start = (f32[1024,128]{1,0:T(8,128)S(1)}, f32[1024,128]{1,0:T(8,128)S(1)}, u32[]{:S(2)}, u32[]{:S(2)}) collective-permute-start(f32[1024,128]{1,0:T(8,128)S(1)} %get-tuple-element.137), channel_id=1, source_target_pairs={{2,0},{4,2},{6,4},{8,6},{10,8},{12,10},{14,12},{16,14},{18,16},{20... | collective-permute-start | bytes 1572872 | tf_op jit(solution)/shard_map/while/body/eval_jaxpr/ppermute | solution.py:19
  653.5 21.0 %collective-permute-start.1 = (f32[1024,128]{1,0:T(8,128)S(1)}, f32[1024,128]{1,0:T(8,128)}, u32[]{:S(2)}, u32[]{:S(2)}) collective-permute-start(f32[1024,128]{1,0:T(8,128)S(1)} %get-tuple-element.138), channel_id=1, source_target_pairs={{0,2},{2,4},{4,6},{6,8},{8,10},{10,12},{12,14},{14,16},{16,18},{18... | collective-permute-start | bytes 1572872 | tf_op jit(solution)/shard_map/while/body/eval_jaxpr/ppermute | solution.py:17
  665.2 0.8 copy-start.2
  711.6 62.4 %all-reduce.2.cloned.1.call-start = ((), (), s32[]{:S(2)}) async-start(), calls=%async_computation | async-start | bytes 2097152 | tf_op jit(solution)/shard_map/while/body/eval_jaxpr/pmax | solution.py:55
  711.8 17.1 %collective-permute-start = (f32[1024,128]{1,0:T(8,128)S(1)}, f32[1024,128]{1,0:T(8,128)S(1)}, u32[]{:S(2)}, u32[]{:S(2)}) collective-permute-start(f32[1024,128]{1,0:T(8,128)S(1)} %get-tuple-element.137), channel_id=1, source_target_pairs={{2,0},{4,2},{6,4},{8,6},{10,8},{12,10},{14,12},{16,14},{18,16},{20... | collective-permute-start | bytes 1572872 | tf_op jit(solution)/shard_map/while/body/eval_jaxpr/ppermute | solution.py:19
  717.2 21.0 %collective-permute-start.1 = (f32[1024,128]{1,0:T(8,128)S(1)}, f32[1024,128]{1,0:T(8,128)}, u32[]{:S(2)}, u32[]{:S(2)}) collective-permute-start(f32[1024,128]{1,0:T(8,128)S(1)} %get-tuple-element.138), channel_id=1, source_target_pairs={{0,2},{2,4},{4,6},{6,8},{8,10},{10,12},{12,14},{14,16},{16,18},{18... | collective-permute-start | bytes 1572872 | tf_op jit(solution)/shard_map/while/body/eval_jaxpr/ppermute | solution.py:17
  728.9 0.8 copy-start.2
  775.3 1.0 copy-start.1
Sparse Core Ops, SparseCore 0:
  53.2 20.0 all-reduce.1
  117.1 19.7 all-reduce.1
  180.8 19.7 all-reduce.1
  244.5 19.7 all-reduce.1
  308.2 19.7 all-reduce.1
  371.9 19.7 all-reduce.1
  435.6 19.7 all-reduce.1
  499.3 19.7 all-reduce.1
  563.0 19.7 all-reduce.1
  626.7 19.7 all-reduce.1
  690.4 19.7 all-reduce.1
  754.1 19.7 all-reduce.1
where the time goes:
time: 784 us; the launch traced here: 783 us
  waiting for transfers between devices  479 us (61%)
  matrix products  124 us (16%)
  starting transfers between devices  67.7 us (9%)
  local copies, waits for them, and re-layouts  63.1 us (8%)
  other arithmetic  34.9 us (4%)
  between operations  13.4 us (2%)
    pmax x12, waiting for transfers between devices, action_sweep(): merged = lax.pmax(largest, 'act')  240 us
    ppermute x12, waiting for transfers between devices, extended(): lax.ppermute(head, axis, [((i + 1) % count, i) for i in range(count)])  136 us
    dot_general x12, matrix products, products(): jnp.einsum('arbij,arbjk->arik', tiles, picked, precision=lax.Precision.HI...  124 us
    ppermute x12, waiting for transfers between devices, extended(): lax.ppermute(tail, axis, [(i, (i + 1) % count) for i in range(count)])  103 us
    ppermute x12, starting transfers between devices, extended(): lax.ppermute(head, axis, [((i + 1) % count, i) for i in range(count)])  67.2 us
    gather x12, local copies, waits for them, and re-layouts, products(): picked = blocks[local_index]  33 us
    concatenate x12, other arithmetic, extended(): jnp.concatenate([lax.ppermute(tail, axis, [(i, (i + 1) % count) for i in...  16 us
    select_n x12, other arithmetic, action_sweep(): jnp.where(target_hit, jnp.float32(1.0), merged.reshape(-1, target_sets))  15.9 us
  transfers between devices with their start and end apart: 36, of which 36 were waited for; matrix products, arithmetic and copies ran while one was open for 0% of the time, Pallas kernels for 0%

commit v1 on v0

v1 whole, which is shorter than its diff:
```python
import functools

import jax
import jax.numpy as jnp
from jax import lax
from jax.experimental import pallas as pl
from jax.experimental.pallas import tpu as pltpu
from jax.sharding import PartitionSpec as P

REACH = 8
SWEEPS = 12
CHUNKS = 2
AXES = ("states", "act")
VMEM = pltpu.VMEM
SMEM = pltpu.SMEM


def in_vmem(x):
    return pltpu.with_memory_space_constraint(x, VMEM)


def split(x):
    high = x.astype(jnp.bfloat16)
    return high, (x - high.astype(jnp.float32)).astype(jnp.bfloat16)


def turn_targets(own_ref, out_refs):
    blocks, width, lanes = out_refs[0].shape
    for b in range(blocks):
        turned = own_ref[b * lanes : (b + 1) * lanes, :].astype(jnp.float32).T
        for c, out_ref in enumerate(out_refs):
            out_ref[b] = turned[c * width : (c + 1) * width, :]


def start_kernel(own_ref, sib_ref, *out_refs):
    turn_targets(own_ref, out_refs[:CHUNKS])
    turn_targets(sib_ref, out_refs[CHUNKS:])


def tiles_kernel(tiles_ref, out_ref):
    actions = tiles_ref.shape[0]
    lanes = tiles_ref.shape[-1]
    for a in range(actions):
        for t in range(2):
            high, low = split(tiles_ref[a, 0, t].T)
            out_ref[0, a, t * lanes : (t + 1) * lanes, :lanes] = high
            out_ref[0, a, t * lanes : (t + 1) * lanes, lanes:] = low


def sweep_kernel(slot_ref, first_ref, second_ref, own_ref, sib_ref, ici_ref, target_ref, out_ref, parts_ref):
    blocks, width, lanes = own_ref.shape
    for n, ref in enumerate((own_ref, sib_ref, ici_ref)):
        for b in range(blocks):
            high, low = split(ref[b])
            parts_ref[n * blocks + b, :width] = high
            parts_ref[n * blocks + b, width:] = low
    for b in range(blocks):
        largest = None
        for n, tiles_ref in enumerate((first_ref, second_ref)):
            for a in range(tiles_ref.shape[1]):
                at = (n * tiles_ref.shape[1] + a) * blocks * 2 + b * 2
                left = jnp.concatenate([parts_ref[slot_ref[at]], parts_ref[slot_ref[at + 1]]], axis=1)
                both = jnp.dot(left, tiles_ref[b, a], preferred_element_type=jnp.float32)
                q = (both[:width, :lanes] + both[:width, lanes:]) + (both[width:, :lanes] + both[width:, lanes:])
                largest = q if largest is None else jnp.maximum(largest, q)
        out_ref[b] = jnp.where(target_ref[b] == 1.0, 1.0, largest)


def finish_kernel(core_ref, *refs):
    own_refs, sib_refs, out_ref = refs[:CHUNKS], refs[CHUNKS:-1], refs[-1]
    blocks, width, lanes = own_refs[0].shape
    core = core_ref[0]
    for part, group in ((core, own_refs), (1 - core, sib_refs)):
        for b in range(blocks):
            panel = jnp.concatenate([ref[b] for ref in group], axis=0)
            out_ref[pl.ds(pl.multiple_of(part * (blocks * lanes) + b * lanes, lanes), lanes), :] = panel.T


def per_device(transitions, columns, targets):
    acts_here, row_blocks, _, lanes, _ = transitions.shape
    sets = targets.shape[1]
    width = sets // CHUNKS
    blocks = row_blocks // 2
    rows = blocks * lanes
    states = lax.axis_size("states")
    total_blocks = row_blocks * states
    devices = 2 * states
    core = lax.axis_index("act")
    first_block = lax.axis_index("states") * row_blocks + core * blocks

    to_sib = [(i, i ^ 1) for i in range(devices)]
    to_ici = [(i, (i + 1) % devices if i % 2 else (i - 1) % devices) for i in range(devices)]

    chunk = jax.ShapeDtypeStruct((blocks, width, lanes), jnp.float32)
    whole = pl.BlockSpec(memory_space=VMEM)
    scalars = pl.BlockSpec(memory_space=SMEM)

    half = lambda which: pl.BlockSpec((rows, sets), lambda i, core_ref: (which(core_ref[0]), 0))
    core_arr = core.astype(jnp.int32).reshape(1)
    started = pl.pallas_call(
        lambda core_ref, own_ref, sib_ref, *outs: start_kernel(own_ref, sib_ref, *outs),
        out_shape=[chunk] * (2 * CHUNKS),
        grid_spec=pltpu.PrefetchScalarGridSpec(
            num_scalar_prefetch=1,
            grid=(1,),
            in_specs=[half(lambda c: c), half(lambda c: 1 - c)],
            out_specs=[pl.BlockSpec((blocks, width, lanes), lambda i, core_ref: (0, 0, 0))] * (2 * CHUNKS),
        ),
        name="start",
    )(core_arr, targets, targets)
    zero, sib = list(started[:CHUNKS]), list(started[CHUNKS:])
    ici = [lax.ppermute(v, AXES, to_ici) for v in zero]

    given = lax.dynamic_slice_in_dim(transitions, (1 - core) * blocks, blocks, 1)
    taken = lax.ppermute(given, AXES, to_sib)

    def right_sides(tiles, offset):
        return pl.pallas_call(
            lambda offset_ref, tiles_ref, out_ref: tiles_kernel(tiles_ref, out_ref),
            out_shape=jax.ShapeDtypeStruct((blocks, acts_here, 2 * lanes, 2 * lanes), jnp.bfloat16),
            grid_spec=pltpu.PrefetchScalarGridSpec(
                num_scalar_prefetch=1,
                grid=(blocks,),
                in_specs=[pl.BlockSpec((acts_here, 1, 2, lanes, lanes), lambda i, offset_ref: (0, offset_ref[0] + i, 0, 0, 0))],
                out_specs=pl.BlockSpec((1, acts_here, 2 * lanes, 2 * lanes), lambda i, offset_ref: (i, 0, 0, 0)),
            ),
            name="tiles",
        )(offset, tiles)

    first = right_sides(transitions, core_arr * blocks)
    second = right_sides(taken, jnp.zeros((1,), jnp.int32))

    mine = lax.dynamic_slice_in_dim(columns, core * blocks, blocks, 1)
    mine = jnp.concatenate(
        [lax.dynamic_slice_in_dim(mine, core * acts_here, acts_here, 0), lax.dynamic_slice_in_dim(mine, (1 - core) * acts_here, acts_here, 0)]
    )
    place = (mine - first_block + blocks) % total_blocks
    left = place + jnp.where(core == 0, 2 * blocks, blocks)
    right = place - 2 * blocks + jnp.where(core == 0, blocks, 2 * blocks)
    slots = jnp.where(place < blocks, left, jnp.where(place < 2 * blocks, place - blocks, right)).reshape(-1)

    def sweep(own, sib, ici, zero):
        return pl.pallas_call(
            sweep_kernel,
            out_shape=chunk,
            in_specs=[scalars] + [whole] * 6,
            out_specs=whole,
            scratch_shapes=[pltpu.VMEM((3 * blocks, 2 * width, lanes), jnp.bfloat16)],
            name="sweep",
            compiler_params=pltpu.CompilerParams(vmem_limit_bytes=24 << 20),
            cost_estimate=pl.CostEstimate(
                flops=2 * 2 * acts_here * blocks * (2 * width) * (2 * lanes) ** 2,
                bytes_accessed=4 * 5 * blocks * width * lanes + 8 * acts_here * blocks * (2 * lanes) ** 2,
                transcendentals=0,
            ),
        )(slots, first, second, own, sib, ici, zero)

    own = list(zero)
    for step in range(SWEEPS):
        for c in range(CHUNKS):
            own[c] = sweep(own[c], sib[c], ici[c], zero[c])
            if step < SWEEPS - 1:
                ici[c] = lax.ppermute(own[c], AXES, to_ici)
            sib[c] = lax.ppermute(own[c], AXES, to_sib)

    return pl.pallas_call(
        finish_kernel,
        out_shape=jax.ShapeDtypeStruct((2 * rows, sets), jnp.float32),
        in_specs=[scalars] + [whole] * (2 * CHUNKS),
        out_specs=whole,
        name="finish",
    )(core_arr, *own, *sib)


def solution(mesh):
    return jax.shard_map(
        per_device,
        mesh=mesh,
        in_specs=(P("act", "states", None, None, None), P(None, "states", None), P("states", None)),
        out_specs=P("states", None),
        check_vma=False,
    )
```

time: 784 us -> 163 us (0.21)
  waiting for transfers between devices: 479 us -> 8.75 us
  matrix products: 124 us -> 0 us
  local copies, waits for them, and re-layouts: 63.1 us -> 5.78 us
  Pallas kernels: 0 us -> 50.3 us
  other arithmetic: 34.9 us -> 0.02 us
  starting transfers between devices: 67.7 us -> 97.7 us
  between operations: 13.4 us -> 0.42 us
    pmax x12 -> x0, waiting for transfers between devices: 240 us -> none  [action_sweep(): merged = lax.pmax(largest, 'act')]
    ppermute x24 -> x49, waiting for transfers between devices: 239 us -> 8.75 us  [the longest x22 7.34 us: per_device(): ici[c] = lax.ppermute(own[c], AXES, to_ici)]
    dot_general x12 -> x0, matrix products: 124 us -> none  [products(): jnp.einsum('arbij,arbjk->arik', tiles, picked, precision=lax.Precision.HI...]
    pallas_call x0 -> x28, Pallas kernels: none -> 50.3 us  [the longest x24 33.2 us: sweep(): pl.pallas_call(sweep_kernel, out_shape=chunk, in_specs=[scalars] + [whole...]
    gather x12 -> x0, local copies, waits for them, and re-layouts: 33 us -> none  [products(): picked = blocks[local_index]]
    ppermute x24 -> x49, starting transfers between devices: 67.2 us -> 97.7 us  [the longest x22 85.3 us: per_device(): ici[c] = lax.ppermute(own[c], AXES, to_ici)]
    select_n x24 -> x1, other arithmetic: 16.1 us -> 0.01 us  [per_device(): jnp.where(place < blocks, left, jnp.where(place < 2 * blocks, place - blo...]
    concatenate x12 -> x0, other arithmetic: 16 us -> none  [extended(): jnp.concatenate([lax.ppermute(tail, axis, [(i, (i + 1) % count) for i in...]
  transfers between devices with their start and end apart: 36 -> 49, of which waited for: 36 -> 12; matrix products, arithmetic and copies ran while one was open for 0% -> 0% of each run, Pallas kernels for 0% -> 29%
where the time goes in v1:
time: 163 us
  starting transfers between devices  97.7 us (60%)
  Pallas kernels  50.3 us (31%)
  waiting for transfers between devices  8.75 us (5%)
  local copies, waits for them, and re-layouts  5.78 us (4%)
    ppermute x22, starting transfers between devices, per_device(): ici[c] = lax.ppermute(own[c], AXES, to_ici)  85.3 us
    pallas_call x24, Pallas kernels, sweep(): pl.pallas_call(sweep_kernel, out_shape=chunk, in_specs=[scalars] + [whole...  33.2 us
    pallas_call x2, Pallas kernels, right_sides(): pl.pallas_call(lambda offset_ref, tiles_ref, out_ref: tiles_kernel(tiles_...  12.3 us
    ppermute x22, waiting for transfers between devices, per_device(): ici[c] = lax.ppermute(own[c], AXES, to_ici)  7.34 us
    ppermute x2, starting transfers between devices, per_device(): ici = [lax.ppermute(v, AXES, to_ici) for v in zero]  6.63 us
    ppermute x24, starting transfers between devices, per_device(): sib[c] = lax.ppermute(own[c], AXES, to_sib)  5.23 us
  transfers between devices with their start and end apart: 49, of which 12 were waited for; matrix products, arithmetic and copies ran while one was open for 0% of the time, Pallas kernels for 29%

profile of v1, /device:TPU:0, one launch (start us, length us, event | category | flops | bytes accessed | tf_op | source)
XLA Modules:
  0.0 163.0 jit_solution(2724293167799975361)
XLA Ops:
  0.0 3.2 %constant_dynamic-slice_fusion = f32[2,8,2,128,128]{4,3,2,1,0:T(8,128)} fusion(f32[2,16,2,128,128]{4,3,2,1,0:T(8,128)} %tiles_ref.1, s32[]{:T(128)S(6)} %select_n.53), kind=kLoop, calls=%fused_computation.7 | loop fusion | bytes 4194308 | tf_op jit(solution)/shard_map/dynamic_slice | solution.py:114
  3.2 0.5 collective-permute-start
  3.6 2.3 %start.1 = (f32[8,64,128]{2,1,0:T(8,128)}, f32[8,64,128]{2,1,0:T(8,128)}, f32[8,64,128]{2,1,0:T(8,128)}, f32[8,64,128]{2,1,0:T(8,128)}) custom-call(s32[1]{0:T(128)} %bitcast.core_ref, s32[2048,128]{1,0:T(8,128)} %sib_ref.1, s32[2048,128]{1,0:T(8,128)} %sib_ref.1), custom_call_target="tpu_custom_call" | custom-call | tf_op jit(solution)/shard_map/start/pallas_call | solution.py:100
  6.0 6.6 %collective-permute-start.24 = (f32[8,64,128]{2,1,0:T(8,128)}, f32[8,64,128]{2,1,0:T(8,128)S(1)}, u32[]{:S(2)}, u32[]{:S(2)}) collective-permute-start(f32[8,64,128]{2,1,0:T(8,128)} %get-tuple-element.11.own_ref.target_ref), channel_id=1, source_target_pairs={{0,31},{1,2},{2,1},{3,4},{4,3},{5,6},{6,5},{7,8},{8,7},{9,10},{10,... | collective-permute-start | bytes 786440 | tf_op jit(solution)/shard_map/ppermute | solution.py:112
  12.9 6.1 %tiles.2.first_ref = bf16[8,2,256,256]{3,2,1,0:T(8,128)(2,1)} custom-call(s32[1]{0:T(128)S(6)} %mul.23.offset_ref, f32[2,16,2,128,128]{4,3,2,1,0:T(8,128)} %tiles_ref.1), custom_call_target="tpu_custom_call" | custom-call | tf_op jit(solution)/shard_map/tiles/pallas_call | solution.py:118
  19.0 6.2 %tiles.3.second_ref = bf16[8,2,256,256]{3,2,1,0:T(8,128)(2,1)} custom-call(s32[1]{0:T(128)} %constant.73.clone.1.offset_ref, f32[2,8,2,128,128]{4,3,2,1,0:T(8,128)} %collective-permute-done.tiles_ref), custom_call_target="tpu_custom_call" | custom-call | tf_op jit(solution)/shard_map/tiles/pallas_call | solution.py:118
  25.3 1.6 copy-done.1
  26.9 1.4 sweep.36.own_ref
  28.3 5.4 %collective-permute-start.26 = (f32[8,64,128]{2,1,0:T(8,128)S(1)}, f32[8,64,128]{2,1,0:T(8,128)S(1)}, u32[]{:S(2)}, u32[]{:S(2)}) collective-permute-start(f32[8,64,128]{2,1,0:T(8,128)S(1)} %sweep.36.own_ref), channel_id=1, source_target_pairs={{0,31},{1,2},{2,1},{3,4},{4,3},{5,6},{6,5},{7,8},{8,7},{9,10},{10,... | collective-permute-start | bytes 786440 | tf_op jit(solution)/shard_map/ppermute | solution.py:163
  33.7 1.4 sweep.24.own_ref
  35.2 0.4 collective-permute-start.3
  35.6 2.3 %collective-permute-done.26.ici_ref = f32[8,64,128]{2,1,0:T(8,128)S(1)} collective-permute-done((f32[8,64,128]{2,1,0:T(8,128)S(1)}, f32[8,64,128]{2,1,0:T(8,128)S(1)}, u32[]{:S(2)}, u32[]{:S(2)}) %collective-permute-start.26) | collective-permute-done | bytes 262176 | tf_op jit(solution)/shard_map/ppermute | solution.py:163
  37.9 1.4 sweep.37.own_ref
  39.4 5.3 %collective-permute-start.28 = (f32[8,64,128]{2,1,0:T(8,128)S(1)}, f32[8,64,128]{2,1,0:T(8,128)S(1)}, u32[]{:S(2)}, u32[]{:S(2)}) collective-permute-start(f32[8,64,128]{2,1,0:T(8,128)S(1)} %sweep.37.own_ref), channel_id=1, source_target_pairs={{0,31},{1,2},{2,1},{3,4},{4,3},{5,6},{6,5},{7,8},{8,7},{9,10},{10,... | collective-permute-start | bytes 786440 | tf_op jit(solution)/shard_map/ppermute | solution.py:163
  44.8 1.4 sweep.25.own_ref
  46.2 3.1 %collective-permute-start.5 = (f32[8,64,128]{2,1,0:T(8,128)S(1)}, f32[8,64,128]{2,1,0:T(8,128)S(1)}, u32[]{:S(2)}, u32[]{:S(2)}) collective-permute-start(f32[8,64,128]{2,1,0:T(8,128)S(1)} %sweep.25.own_ref), channel_id=1, source_target_pairs={{0,31},{1,2},{2,1},{3,4},{4,3},{5,6},{6,5},{7,8},{8,7},{9,10},{10,... | collective-permute-start | bytes 786440 | tf_op jit(solution)/shard_map/ppermute | solution.py:163
  49.3 1.4 sweep.38.own_ref
  50.7 0.5 collective-permute-start.29
  51.2 4.6 %collective-permute-start.30 = (f32[8,64,128]{2,1,0:T(8,128)S(1)}, f32[8,64,128]{2,1,0:T(8,128)S(1)}, u32[]{:S(2)}, u32[]{:S(2)}) collective-permute-start(f32[8,64,128]{2,1,0:T(8,128)S(1)} %sweep.38.own_ref), channel_id=1, source_target_pairs={{0,31},{1,2},{2,1},{3,4},{4,3},{5,6},{6,5},{7,8},{8,7},{9,10},{10,... | collective-permute-start | bytes 786440 | tf_op jit(solution)/shard_map/ppermute | solution.py:163
  55.8 1.4 sweep.26.own_ref
  57.2 3.3 %collective-permute-start.7 = (f32[8,64,128]{2,1,0:T(8,128)S(1)}, f32[8,64,128]{2,1,0:T(8,128)S(1)}, u32[]{:S(2)}, u32[]{:S(2)}) collective-permute-start(f32[8,64,128]{2,1,0:T(8,128)S(1)} %sweep.26.own_ref), channel_id=1, source_target_pairs={{0,31},{1,2},{2,1},{3,4},{4,3},{5,6},{6,5},{7,8},{8,7},{9,10},{10,... | collective-permute-start | bytes 786440 | tf_op jit(solution)/shard_map/ppermute | solution.py:163
  60.7 1.4 sweep.39.own_ref
  62.4 4.3 %collective-permute-start.32 = (f32[8,64,128]{2,1,0:T(8,128)S(1)}, f32[8,64,128]{2,1,0:T(8,128)S(1)}, u32[]{:S(2)}, u32[]{:S(2)}) collective-permute-start(f32[8,64,128]{2,1,0:T(8,128)S(1)} %sweep.39.own_ref), channel_id=1, source_target_pairs={{0,31},{1,2},{2,1},{3,4},{4,3},{5,6},{6,5},{7,8},{8,7},{9,10},{10,... | collective-permute-start | bytes 786440 | tf_op jit(solution)/shard_map/ppermute | solution.py:163
  66.8 1.4 sweep.27.own_ref
  68.3 4.3 %collective-permute-start.9 = (f32[8,64,128]{2,1,0:T(8,128)S(1)}, f32[8,64,128]{2,1,0:T(8,128)S(1)}, u32[]{:S(2)}, u32[]{:S(2)}) collective-permute-start(f32[8,64,128]{2,1,0:T(8,128)S(1)} %sweep.27.own_ref), channel_id=1, source_target_pairs={{0,31},{1,2},{2,1},{3,4},{4,3},{5,6},{6,5},{7,8},{8,7},{9,10},{10,... | collective-permute-start | bytes 786440 | tf_op jit(solution)/shard_map/ppermute | solution.py:163
  72.6 1.4 sweep.40.own_ref
  73.9 0.4 collective-permute-start.33
  74.4 3.4 %collective-permute-start.34 = (f32[8,64,128]{2,1,0:T(8,128)S(1)}, f32[8,64,128]{2,1,0:T(8,128)S(1)}, u32[]{:S(2)}, u32[]{:S(2)}) collective-permute-start(f32[8,64,128]{2,1,0:T(8,128)S(1)} %sweep.40.own_ref), channel_id=1, source_target_pairs={{0,31},{1,2},{2,1},{3,4},{4,3},{5,6},{6,5},{7,8},{8,7},{9,10},{10,... | collective-permute-start | bytes 786440 | tf_op jit(solution)/shard_map/ppermute | solution.py:163
  77.8 1.4 sweep.28.own_ref
  79.3 4.5 %collective-permute-start.11 = (f32[8,64,128]{2,1,0:T(8,128)S(1)}, f32[8,64,128]{2,1,0:T(8,128)S(1)}, u32[]{:S(2)}, u32[]{:S(2)}) collective-permute-start(f32[8,64,128]{2,1,0:T(8,128)S(1)} %sweep.28.own_ref), channel_id=1, source_target_pairs={{0,31},{1,2},{2,1},{3,4},{4,3},{5,6},{6,5},{7,8},{8,7},{9,10},{10,... | collective-permute-start | bytes 786440 | tf_op jit(solution)/shard_map/ppermute | solution.py:163
  83.8 1.4 sweep.41.own_ref
  85.3 4.1 %collective-permute-start.36 = (f32[8,64,128]{2,1,0:T(8,128)S(1)}, f32[8,64,128]{2,1,0:T(8,128)S(1)}, u32[]{:S(2)}, u32[]{:S(2)}) collective-permute-start(f32[8,64,128]{2,1,0:T(8,128)S(1)} %sweep.41.own_ref), channel_id=1, source_target_pairs={{0,31},{1,2},{2,1},{3,4},{4,3},{5,6},{6,5},{7,8},{8,7},{9,10},{10,... | collective-permute-start | bytes 786440 | tf_op jit(solution)/shard_map/ppermute | solution.py:163
  89.4 1.4 sweep.29.own_ref
  90.8 0.4 collective-permute-start.12
  91.2 3.6 %collective-permute-start.13 = (f32[8,64,128]{2,1,0:T(8,128)S(1)}, f32[8,64,128]{2,1,0:T(8,128)S(1)}, u32[]{:S(2)}, u32[]{:S(2)}) collective-permute-start(f32[8,64,128]{2,1,0:T(8,128)S(1)} %sweep.29.own_ref), channel_id=1, source_target_pairs={{0,31},{1,2},{2,1},{3,4},{4,3},{5,6},{6,5},{7,8},{8,7},{9,10},{10,... | collective-permute-start | bytes 786440 | tf_op jit(solution)/shard_map/ppermute | solution.py:163
  94.9 1.6 sweep.42.own_ref
  96.5 4.3 %collective-permute-start.38 = (f32[8,64,128]{2,1,0:T(8,128)S(1)}, f32[8,64,128]{2,1,0:T(8,128)S(1)}, u32[]{:S(2)}, u32[]{:S(2)}) collective-permute-start(f32[8,64,128]{2,1,0:T(8,128)S(1)} %sweep.42.own_ref), channel_id=1, source_target_pairs={{0,31},{1,2},{2,1},{3,4},{4,3},{5,6},{6,5},{7,8},{8,7},{9,10},{10,... | collective-permute-start | bytes 786440 | tf_op jit(solution)/shard_map/ppermute | solution.py:163
  100.9 1.4 sweep.30.own_ref
  102.3 3.9 %collective-permute-start.15 = (f32[8,64,128]{2,1,0:T(8,128)S(1)}, f32[8,64,128]{2,1,0:T(8,128)S(1)}, u32[]{:S(2)}, u32[]{:S(2)}) collective-permute-start(f32[8,64,128]{2,1,0:T(8,128)S(1)} %sweep.30.own_ref), channel_id=1, source_target_pairs={{0,31},{1,2},{2,1},{3,4},{4,3},{5,6},{6,5},{7,8},{8,7},{9,10},{10,... | collective-permute-start | bytes 786440 | tf_op jit(solution)/shard_map/ppermute | solution.py:163
  106.3 1.4 sweep.43.own_ref
  107.7 0.4 collective-permute-start.39
  108.1 3.8 %collective-permute-start.40 = (f32[8,64,128]{2,1,0:T(8,128)S(1)}, f32[8,64,128]{2,1,0:T(8,128)S(1)}, u32[]{:S(2)}, u32[]{:S(2)}) collective-permute-start(f32[8,64,128]{2,1,0:T(8,128)S(1)} %sweep.43.own_ref), channel_id=1, source_target_pairs={{0,31},{1,2},{2,1},{3,4},{4,3},{5,6},{6,5},{7,8},{8,7},{9,10},{10,... | collective-permute-start | bytes 786440 | tf_op jit(solution)/shard_map/ppermute | solution.py:163
  111.9 1.4 sweep.31.own_ref
  113.4 4.1 %collective-permute-start.17 = (f32[8,64,128]{2,1,0:T(8,128)S(1)}, f32[8,64,128]{2,1,0:T(8,128)S(1)}, u32[]{:S(2)}, u32[]{:S(2)}) collective-permute-start(f32[8,64,128]{2,1,0:T(8,128)S(1)} %sweep.31.own_ref), channel_id=1, source_target_pairs={{0,31},{1,2},{2,1},{3,4},{4,3},{5,6},{6,5},{7,8},{8,7},{9,10},{10,... | collective-permute-start | bytes 786440 | tf_op jit(solution)/shard_map/ppermute | solution.py:163
  117.6 1.4 sweep.44.own_ref
  119.1 4.1 %collective-permute-start.42 = (f32[8,64,128]{2,1,0:T(8,128)S(1)}, f32[8,64,128]{2,1,0:T(8,128)S(1)}, u32[]{:S(2)}, u32[]{:S(2)}) collective-permute-start(f32[8,64,128]{2,1,0:T(8,128)S(1)} %sweep.44.own_ref), channel_id=1, source_target_pairs={{0,31},{1,2},{2,1},{3,4},{4,3},{5,6},{6,5},{7,8},{8,7},{9,10},{10,... | collective-permute-start | bytes 786440 | tf_op jit(solution)/shard_map/ppermute | solution.py:163
  123.1 1.4 sweep.32.own_ref
  124.5 0.8 collective-permute-start.18
  125.3 3.5 %collective-permute-start.19 = (f32[8,64,128]{2,1,0:T(8,128)S(1)}, f32[8,64,128]{2,1,0:T(8,128)S(1)}, u32[]{:S(2)}, u32[]{:S(2)}) collective-permute-start(f32[8,64,128]{2,1,0:T(8,128)S(1)} %sweep.32.own_ref), channel_id=1, source_target_pairs={{0,31},{1,2},{2,1},{3,4},{4,3},{5,6},{6,5},{7,8},{8,7},{9,10},{10,... | collective-permute-start | bytes 786440 | tf_op jit(solution)/shard_map/ppermute | solution.py:163
  128.8 1.4 sweep.45.own_ref
  130.2 4.1 %collective-permute-start.44 = (f32[8,64,128]{2,1,0:T(8,128)S(1)}, f32[8,64,128]{2,1,0:T(8,128)S(1)}, u32[]{:S(2)}, u32[]{:S(2)}) collective-permute-start(f32[8,64,128]{2,1,0:T(8,128)S(1)} %sweep.45.own_ref), channel_id=1, source_target_pairs={{0,31},{1,2},{2,1},{3,4},{4,3},{5,6},{6,5},{7,8},{8,7},{9,10},{10,... | collective-permute-start | bytes 786440 | tf_op jit(solution)/shard_map/ppermute | solution.py:163
  134.7 1.4 sweep.33.own_ref
  136.2 3.7 %collective-permute-start.21 = (f32[8,64,128]{2,1,0:T(8,128)S(1)}, f32[8,64,128]{2,1,0:T(8,128)S(1)}, u32[]{:S(2)}, u32[]{:S(2)}) collective-permute-start(f32[8,64,128]{2,1,0:T(8,128)S(1)} %sweep.33.own_ref), channel_id=1, source_target_pairs={{0,31},{1,2},{2,1},{3,4},{4,3},{5,6},{6,5},{7,8},{8,7},{9,10},{10,... | collective-permute-start | bytes 786440 | tf_op jit(solution)/shard_map/ppermute | solution.py:163
  140.0 1.4 sweep.46.own_ref
  141.4 0.8 collective-permute-start.45
  142.2 3.4 %collective-permute-start.46 = (f32[8,64,128]{2,1,0:T(8,128)S(1)}, f32[8,64,128]{2,1,0:T(8,128)S(1)}, u32[]{:S(2)}, u32[]{:S(2)}) collective-permute-start(f32[8,64,128]{2,1,0:T(8,128)S(1)} %sweep.46.own_ref), channel_id=1, source_target_pairs={{0,31},{1,2},{2,1},{3,4},{4,3},{5,6},{6,5},{7,8},{8,7},{9,10},{10,... | collective-permute-start | bytes 786440 | tf_op jit(solution)/shard_map/ppermute | solution.py:163
  145.7 1.4 sweep.34.own_ref
  147.2 4.0 %collective-permute-start.23 = (f32[8,64,128]{2,1,0:T(8,128)S(1)}, f32[8,64,128]{2,1,0:T(8,128)S(1)}, u32[]{:S(2)}, u32[]{:S(2)}) collective-permute-start(f32[8,64,128]{2,1,0:T(8,128)S(1)} %sweep.34.own_ref), channel_id=1, source_target_pairs={{0,31},{1,2},{2,1},{3,4},{4,3},{5,6},{6,5},{7,8},{8,7},{9,10},{10,... | collective-permute-start | bytes 786440 | tf_op jit(solution)/shard_map/ppermute | solution.py:163
  151.6 1.4 sweep.47.refs_1_
  153.1 3.6 %collective-permute-done.23.ici_ref = f32[8,64,128]{2,1,0:T(8,128)S(1)} collective-permute-done((f32[8,64,128]{2,1,0:T(8,128)S(1)}, f32[8,64,128]{2,1,0:T(8,128)S(1)}, u32[]{:S(2)}, u32[]{:S(2)}) %collective-permute-start.23) | collective-permute-done | bytes 262176 | tf_op jit(solution)/shard_map/ppermute | solution.py:163
  156.8 1.4 sweep.35.refs_0_
  158.4 1.3 collective-permute-done.47.refs_2_
  159.8 0.7 copy-done.9
  160.5 2.5 %finish.1 = f32[2048,128]{1,0:T(8,128)} custom-call(s32[1]{0:T(128)} %bitcast.core_ref, f32[8,64,128]{2,1,0:T(8,128)} %copy-done.5, f32[8,64,128]{2,1,0:T(8,128)} %copy-done.4, f32[8,64,128]{2,1,0:T(8,128)} %copy-done.9, f32[8,64,128]{2,1,0:T(8,128)} %copy-done.8), custom_call_target="tpu_custom_call" | custom-call | tf_op jit(solution)/shard_map/finish/pallas_call | solution.py:166
  (90 shorter events, 3.8 us)
Async XLA Ops:
  3.2 9.4 %copy-start.10 = (s32[4,16,2]{1,2,0:T(2,128)S(1)}, s32[4,16,2]{1,2,0:T(2,128)}, u32[]{:S(2)}) copy-start(s32[4,16,2]{1,2,0:T(2,128)} %param.4) | copy-start | bytes 1540
  3.2 15.8 %collective-permute-start = (f32[2,8,2,128,128]{4,3,2,1,0:T(8,128)}, f32[2,8,2,128,128]{4,3,2,1,0:T(8,128)}, u32[]{:S(2)}, u32[]{:S(2)}) collective-permute-start(f32[2,8,2,128,128]{4,3,2,1,0:T(8,128)} %constant_dynamic-slice_fusion), channel_id=1, source_target_pairs={{0,1},{1,0},{2,3},{3,2},{4,5},{5,4},{6,7},{7,6},{8,9},{9,8},{10,11... | collective-permute-start | bytes 6291464 | tf_op jit(solution)/shard_map/ppermute | solution.py:115
  6.0 19.3 %collective-permute-start.24 = (f32[8,64,128]{2,1,0:T(8,128)}, f32[8,64,128]{2,1,0:T(8,128)S(1)}, u32[]{:S(2)}, u32[]{:S(2)}) collective-permute-start(f32[8,64,128]{2,1,0:T(8,128)} %get-tuple-element.11.own_ref.target_ref), channel_id=1, source_target_pairs={{0,31},{1,2},{2,1},{3,4},{4,3},{5,6},{6,5},{7,8},{8,7},{9,10},{10,... | collective-permute-start | bytes 786440 | tf_op jit(solution)/shard_map/ppermute | solution.py:112
  12.6 21.1 %collective-permute-start.1 = (f32[8,64,128]{2,1,0:T(8,128)}, f32[8,64,128]{2,1,0:T(8,128)S(1)}, u32[]{:S(2)}, u32[]{:S(2)}) collective-permute-start(f32[8,64,128]{2,1,0:T(8,128)} %get-tuple-element.9.own_ref.target_ref), channel_id=1, source_target_pairs={{0,31},{1,2},{2,1},{3,4},{4,3},{5,6},{6,5},{7,8},{8,7},{9,10},{10,... | collective-permute-start | bytes 786440 | tf_op jit(solution)/shard_map/ppermute | solution.py:112
  19.0 6.3 %copy-start = (bf16[8,2,256,256]{3,2,1,0:T(8,128)(2,1)S(1)}, bf16[8,2,256,256]{3,2,1,0:T(8,128)(2,1)}, u32[]{:S(2)}) copy-start(bf16[8,2,256,256]{3,2,1,0:T(8,128)(2,1)} %tiles.2.first_ref) | copy-start | bytes 6291460
  19.0 6.3 %copy-start.3 = (f32[8,64,128]{2,1,0:T(8,128)S(1)}, f32[8,64,128]{2,1,0:T(8,128)}, u32[]{:S(2)}) copy-start(f32[8,64,128]{2,1,0:T(8,128)} %get-tuple-element.11.own_ref.target_ref) | copy-start | bytes 786436
  19.0 6.3 %copy-start.7 = (f32[8,64,128]{2,1,0:T(8,128)S(1)}, f32[8,64,128]{2,1,0:T(8,128)}, u32[]{:S(2)}) copy-start(f32[8,64,128]{2,1,0:T(8,128)} %get-tuple-element.12.sib_ref) | copy-start | bytes 786436
  25.3 1.6 copy-start.1
  26.9 6.8 %copy-start.2 = (f32[8,64,128]{2,1,0:T(8,128)S(1)}, f32[8,64,128]{2,1,0:T(8,128)}, u32[]{:S(2)}) copy-start(f32[8,64,128]{2,1,0:T(8,128)} %get-tuple-element.9.own_ref.target_ref) | copy-start | bytes 786436
  26.9 6.8 %copy-start.6 = (f32[8,64,128]{2,1,0:T(8,128)S(1)}, f32[8,64,128]{2,1,0:T(8,128)}, u32[]{:S(2)}) copy-start(f32[8,64,128]{2,1,0:T(8,128)} %get-tuple-element.10.sib_ref) | copy-start | bytes 786436
  28.3 7.4 %collective-permute-start.25 = (f32[8,64,128]{2,1,0:T(8,128)S(1)}, f32[8,64,128]{2,1,0:T(8,128)S(1)}, u32[]{:S(2)}, u32[]{:S(2)}) collective-permute-start(f32[8,64,128]{2,1,0:T(8,128)S(1)} %sweep.36.own_ref), channel_id=1, source_target_pairs={{0,1},{1,0},{2,3},{3,2},{4,5},{5,4},{6,7},{7,6},{8,9},{9,8},{10,11... | collective-permute-start | bytes 786440 | tf_op jit(solution)/shard_map/ppermute | solution.py:164
  28.3 9.6 %collective-permute-start.26 = (f32[8,64,128]{2,1,0:T(8,128)S(1)}, f32[8,64,128]{2,1,0:T(8,128)S(1)}, u32[]{:S(2)}, u32[]{:S(2)}) collective-permute-start(f32[8,64,128]{2,1,0:T(8,128)S(1)} %sweep.36.own_ref), channel_id=1, source_target_pairs={{0,31},{1,2},{2,1},{3,4},{4,3},{5,6},{6,5},{7,8},{8,7},{9,10},{10,... | collective-permute-start | bytes 786440 | tf_op jit(solution)/shard_map/ppermute | solution.py:163
  35.1 9.6 %collective-permute-start.2 = (f32[8,64,128]{2,1,0:T(8,128)S(1)}, f32[8,64,128]{2,1,0:T(8,128)S(1)}, u32[]{:S(2)}, u32[]{:S(2)}) collective-permute-start(f32[8,64,128]{2,1,0:T(8,128)S(1)} %sweep.24.own_ref), channel_id=1, source_target_pairs={{0,1},{1,0},{2,3},{3,2},{4,5},{5,4},{6,7},{7,6},{8,9},{9,8},{10,11... | collective-permute-start | bytes 786440 | tf_op jit(solution)/shard_map/ppermute | solution.py:164
  35.2 9.6 %collective-permute-start.3 = (f32[8,64,128]{2,1,0:T(8,128)S(1)}, f32[8,64,128]{2,1,0:T(8,128)S(1)}, u32[]{:S(2)}, u32[]{:S(2)}) collective-permute-start(f32[8,64,128]{2,1,0:T(8,128)S(1)} %sweep.24.own_ref), channel_id=1, source_target_pairs={{0,31},{1,2},{2,1},{3,4},{4,3},{5,6},{6,5},{7,8},{8,7},{9,10},{10,... | collective-permute-start | bytes 786440 | tf_op jit(solution)/shard_map/ppermute | solution.py:163
  39.3 10.0 %collective-permute-start.27 = (f32[8,64,128]{2,1,0:T(8,128)S(1)}, f32[8,64,128]{2,1,0:T(8,128)S(1)}, u32[]{:S(2)}, u32[]{:S(2)}) collective-permute-start(f32[8,64,128]{2,1,0:T(8,128)S(1)} %sweep.37.own_ref), channel_id=1, source_target_pairs={{0,1},{1,0},{2,3},{3,2},{4,5},{5,4},{6,7},{7,6},{8,9},{9,8},{10,11... | collective-permute-start | bytes 786440 | tf_op jit(solution)/shard_map/ppermute | solution.py:164
  39.4 9.9 %collective-permute-start.28 = (f32[8,64,128]{2,1,0:T(8,128)S(1)}, f32[8,64,128]{2,1,0:T(8,128)S(1)}, u32[]{:S(2)}, u32[]{:S(2)}) collective-permute-start(f32[8,64,128]{2,1,0:T(8,128)S(1)} %sweep.37.own_ref), channel_id=1, source_target_pairs={{0,31},{1,2},{2,1},{3,4},{4,3},{5,6},{6,5},{7,8},{8,7},{9,10},{10,... | collective-permute-start | bytes 786440 | tf_op jit(solution)/shard_map/ppermute | solution.py:163
  46.1 9.6 %collective-permute-start.4 = (f32[8,64,128]{2,1,0:T(8,128)S(1)}, f32[8,64,128]{2,1,0:T(8,128)S(1)}, u32[]{:S(2)}, u32[]{:S(2)}) collective-permute-start(f32[8,64,128]{2,1,0:T(8,128)S(1)} %sweep.25.own_ref), channel_id=1, source_target_pairs={{0,1},{1,0},{2,3},{3,2},{4,5},{5,4},{6,7},{7,6},{8,9},{9,8},{10,11... | collective-permute-start | bytes 786440 | tf_op jit(solution)/shard_map/ppermute | solution.py:164
  46.2 9.6 %collective-permute-start.5 = (f32[8,64,128]{2,1,0:T(8,128)S(1)}, f32[8,64,128]{2,1,0:T(8,128)S(1)}, u32[]{:S(2)}, u32[]{:S(2)}) collective-permute-start(f32[8,64,128]{2,1,0:T(8,128)S(1)} %sweep.25.own_ref), channel_id=1, source_target_pairs={{0,31},{1,2},{2,1},{3,4},{4,3},{5,6},{6,5},{7,8},{8,7},{9,10},{10,... | collective-permute-start | bytes 786440 | tf_op jit(solution)/shard_map/ppermute | solution.py:163
  50.7 9.8 %collective-permute-start.29 = (f32[8,64,128]{2,1,0:T(8,128)S(1)}, f32[8,64,128]{2,1,0:T(8,128)S(1)}, u32[]{:S(2)}, u32[]{:S(2)}) collective-permute-start(f32[8,64,128]{2,1,0:T(8,128)S(1)} %sweep.38.own_ref), channel_id=1, source_target_pairs={{0,1},{1,0},{2,3},{3,2},{4,5},{5,4},{6,7},{7,6},{8,9},{9,8},{10,11... | collective-permute-start | bytes 786440 | tf_op jit(solution)/shard_map/ppermute | solution.py:164
  51.2 9.5 %collective-permute-start.30 = (f32[8,64,128]{2,1,0:T(8,128)S(1)}, f32[8,64,128]{2,1,0:T(8,128)S(1)}, u32[]{:S(2)}, u32[]{:S(2)}) collective-permute-start(f32[8,64,128]{2,1,0:T(8,128)S(1)} %sweep.38.own_ref), channel_id=1, source_target_pairs={{0,31},{1,2},{2,1},{3,4},{4,3},{5,6},{6,5},{7,8},{8,7},{9,10},{10,... | collective-permute-start | bytes 786440 | tf_op jit(solution)/shard_map/ppermute | solution.py:163
  57.2 9.6 %collective-permute-start.6 = (f32[8,64,128]{2,1,0:T(8,128)S(1)}, f32[8,64,128]{2,1,0:T(8,128)S(1)}, u32[]{:S(2)}, u32[]{:S(2)}) collective-permute-start(f32[8,64,128]{2,1,0:T(8,128)S(1)} %sweep.26.own_ref), channel_id=1, source_target_pairs={{0,1},{1,0},{2,3},{3,2},{4,5},{5,4},{6,7},{7,6},{8,9},{9,8},{10,11... | collective-permute-start | bytes 786440 | tf_op jit(solution)/shard_map/ppermute | solution.py:164
  57.2 9.6 %collective-permute-start.7 = (f32[8,64,128]{2,1,0:T(8,128)S(1)}, f32[8,64,128]{2,1,0:T(8,128)S(1)}, u32[]{:S(2)}, u32[]{:S(2)}) collective-permute-start(f32[8,64,128]{2,1,0:T(8,128)S(1)} %sweep.26.own_ref), channel_id=1, source_target_pairs={{0,31},{1,2},{2,1},{3,4},{4,3},{5,6},{6,5},{7,8},{8,7},{9,10},{10,... | collective-permute-start | bytes 786440 | tf_op jit(solution)/shard_map/ppermute | solution.py:163
  62.0 10.5 %collective-permute-start.31 = (f32[8,64,128]{2,1,0:T(8,128)S(1)}, f32[8,64,128]{2,1,0:T(8,128)S(1)}, u32[]{:S(2)}, u32[]{:S(2)}) collective-permute-start(f32[8,64,128]{2,1,0:T(8,128)S(1)} %sweep.39.own_ref), channel_id=1, source_target_pairs={{0,1},{1,0},{2,3},{3,2},{4,5},{5,4},{6,7},{7,6},{8,9},{9,8},{10,11... | collective-permute-start | bytes 786440 | tf_op jit(solution)/shard_map/ppermute | solution.py:164
  62.4 10.2 %collective-permute-start.32 = (f32[8,64,128]{2,1,0:T(8,128)S(1)}, f32[8,64,128]{2,1,0:T(8,128)S(1)}, u32[]{:S(2)}, u32[]{:S(2)}) collective-permute-start(f32[8,64,128]{2,1,0:T(8,128)S(1)} %sweep.39.own_ref), channel_id=1, source_target_pairs={{0,31},{1,2},{2,1},{3,4},{4,3},{5,6},{6,5},{7,8},{8,7},{9,10},{10,... | collective-permute-start | bytes 786440 | tf_op jit(solution)/shard_map/ppermute | solution.py:163
  68.2 9.6 %collective-permute-start.8 = (f32[8,64,128]{2,1,0:T(8,128)S(1)}, f32[8,64,128]{2,1,0:T(8,128)S(1)}, u32[]{:S(2)}, u32[]{:S(2)}) collective-permute-start(f32[8,64,128]{2,1,0:T(8,128)S(1)} %sweep.27.own_ref), channel_id=1, source_target_pairs={{0,1},{1,0},{2,3},{3,2},{4,5},{5,4},{6,7},{7,6},{8,9},{9,8},{10,11... | collective-permute-start | bytes 786440 | tf_op jit(solution)/shard_map/ppermute | solution.py:164
  68.3 9.6 %collective-permute-start.9 = (f32[8,64,128]{2,1,0:T(8,128)S(1)}, f32[8,64,128]{2,1,0:T(8,128)S(1)}, u32[]{:S(2)}, u32[]{:S(2)}) collective-permute-start(f32[8,64,128]{2,1,0:T(8,128)S(1)} %sweep.27.own_ref), channel_id=1, source_target_pairs={{0,31},{1,2},{2,1},{3,4},{4,3},{5,6},{6,5},{7,8},{8,7},{9,10},{10,... | collective-permute-start | bytes 786440 | tf_op jit(solution)/shard_map/ppermute | solution.py:163
  73.9 9.9 %collective-permute-start.33 = (f32[8,64,128]{2,1,0:T(8,128)S(1)}, f32[8,64,128]{2,1,0:T(8,128)S(1)}, u32[]{:S(2)}, u32[]{:S(2)}) collective-permute-start(f32[8,64,128]{2,1,0:T(8,128)S(1)} %sweep.40.own_ref), channel_id=1, source_target_pairs={{0,1},{1,0},{2,3},{3,2},{4,5},{5,4},{6,7},{7,6},{8,9},{9,8},{10,11... | collective-permute-start | bytes 786440 | tf_op jit(solution)/shard_map/ppermute | solution.py:164
  74.4 9.5 %collective-permute-start.34 = (f32[8,64,128]{2,1,0:T(8,128)S(1)}, f32[8,64,128]{2,1,0:T(8,128)S(1)}, u32[]{:S(2)}, u32[]{:S(2)}) collective-permute-start(f32[8,64,128]{2,1,0:T(8,128)S(1)} %sweep.40.own_ref), channel_id=1, source_target_pairs={{0,31},{1,2},{2,1},{3,4},{4,3},{5,6},{6,5},{7,8},{8,7},{9,10},{10,... | collective-permute-start | bytes 786440 | tf_op jit(solution)/shard_map/ppermute | solution.py:163
  79.2 10.2 %collective-permute-start.10 = (f32[8,64,128]{2,1,0:T(8,128)S(1)}, f32[8,64,128]{2,1,0:T(8,128)S(1)}, u32[]{:S(2)}, u32[]{:S(2)}) collective-permute-start(f32[8,64,128]{2,1,0:T(8,128)S(1)} %sweep.28.own_ref), channel_id=1, source_target_pairs={{0,1},{1,0},{2,3},{3,2},{4,5},{5,4},{6,7},{7,6},{8,9},{9,8},{10,11... | collective-permute-start | bytes 786440 | tf_op jit(solution)/shard_map/ppermute | solution.py:164
  79.3 10.1 %collective-permute-start.11 = (f32[8,64,128]{2,1,0:T(8,128)S(1)}, f32[8,64,128]{2,1,0:T(8,128)S(1)}, u32[]{:S(2)}, u32[]{:S(2)}) collective-permute-start(f32[8,64,128]{2,1,0:T(8,128)S(1)} %sweep.28.own_ref), channel_id=1, source_target_pairs={{0,31},{1,2},{2,1},{3,4},{4,3},{5,6},{6,5},{7,8},{8,7},{9,10},{10,... | collective-permute-start | bytes 786440 | tf_op jit(solution)/shard_map/ppermute | solution.py:163
  85.2 9.6 %collective-permute-start.35 = (f32[8,64,128]{2,1,0:T(8,128)S(1)}, f32[8,64,128]{2,1,0:T(8,128)S(1)}, u32[]{:S(2)}, u32[]{:S(2)}) collective-permute-start(f32[8,64,128]{2,1,0:T(8,128)S(1)} %sweep.41.own_ref), channel_id=1, source_target_pairs={{0,1},{1,0},{2,3},{3,2},{4,5},{5,4},{6,7},{7,6},{8,9},{9,8},{10,11... | collective-permute-start | bytes 786440 | tf_op jit(solution)/shard_map/ppermute | solution.py:164
  85.3 9.5 %collective-permute-start.36 = (f32[8,64,128]{2,1,0:T(8,128)S(1)}, f32[8,64,128]{2,1,0:T(8,128)S(1)}, u32[]{:S(2)}, u32[]{:S(2)}) collective-permute-start(f32[8,64,128]{2,1,0:T(8,128)S(1)} %sweep.41.own_ref), channel_id=1, source_target_pairs={{0,31},{1,2},{2,1},{3,4},{4,3},{5,6},{6,5},{7,8},{8,7},{9,10},{10,... | collective-permute-start | bytes 786440 | tf_op jit(solution)/shard_map/ppermute | solution.py:163
  90.8 10.1 %collective-permute-start.12 = (f32[8,64,128]{2,1,0:T(8,128)S(1)}, f32[8,64,128]{2,1,0:T(8,128)S(1)}, u32[]{:S(2)}, u32[]{:S(2)}) collective-permute-start(f32[8,64,128]{2,1,0:T(8,128)S(1)} %sweep.29.own_ref), channel_id=1, source_target_pairs={{0,1},{1,0},{2,3},{3,2},{4,5},{5,4},{6,7},{7,6},{8,9},{9,8},{10,11... | collective-permute-start | bytes 786440 | tf_op jit(solution)/shard_map/ppermute | solution.py:164
  91.2 9.6 %collective-permute-start.13 = (f32[8,64,128]{2,1,0:T(8,128)S(1)}, f32[8,64,128]{2,1,0:T(8,128)S(1)}, u32[]{:S(2)}, u32[]{:S(2)}) collective-permute-start(f32[8,64,128]{2,1,0:T(8,128)S(1)} %sweep.29.own_ref), channel_id=1, source_target_pairs={{0,31},{1,2},{2,1},{3,4},{4,3},{5,6},{6,5},{7,8},{8,7},{9,10},{10,... | collective-permute-start | bytes 786440 | tf_op jit(solution)/shard_map/ppermute | solution.py:163
  96.4 9.8 %collective-permute-start.37 = (f32[8,64,128]{2,1,0:T(8,128)S(1)}, f32[8,64,128]{2,1,0:T(8,128)S(1)}, u32[]{:S(2)}, u32[]{:S(2)}) collective-permute-start(f32[8,64,128]{2,1,0:T(8,128)S(1)} %sweep.42.own_ref), channel_id=1, source_target_pairs={{0,1},{1,0},{2,3},{3,2},{4,5},{5,4},{6,7},{7,6},{8,9},{9,8},{10,11... | collective-permute-start | bytes 786440 | tf_op jit(solution)/shard_map/ppermute | solution.py:164
  96.5 9.8 %collective-permute-start.38 = (f32[8,64,128]{2,1,0:T(8,128)S(1)}, f32[8,64,128]{2,1,0:T(8,128)S(1)}, u32[]{:S(2)}, u32[]{:S(2)}) collective-permute-start(f32[8,64,128]{2,1,0:T(8,128)S(1)} %sweep.42.own_ref), channel_id=1, source_target_pairs={{0,31},{1,2},{2,1},{3,4},{4,3},{5,6},{6,5},{7,8},{8,7},{9,10},{10,... | collective-permute-start | bytes 786440 | tf_op jit(solution)/shard_map/ppermute | solution.py:163
  102.3 9.7 %collective-permute-start.14 = (f32[8,64,128]{2,1,0:T(8,128)S(1)}, f32[8,64,128]{2,1,0:T(8,128)S(1)}, u32[]{:S(2)}, u32[]{:S(2)}) collective-permute-start(f32[8,64,128]{2,1,0:T(8,128)S(1)} %sweep.30.own_ref), channel_id=1, source_target_pairs={{0,1},{1,0},{2,3},{3,2},{4,5},{5,4},{6,7},{7,6},{8,9},{9,8},{10,11... | collective-permute-start | bytes 786440 | tf_op jit(solution)/shard_map/ppermute | solution.py:164
  102.3 9.6 %collective-permute-start.15 = (f32[8,64,128]{2,1,0:T(8,128)S(1)}, f32[8,64,128]{2,1,0:T(8,128)S(1)}, u32[]{:S(2)}, u32[]{:S(2)}) collective-permute-start(f32[8,64,128]{2,1,0:T(8,128)S(1)} %sweep.30.own_ref), channel_id=1, source_target_pairs={{0,31},{1,2},{2,1},{3,4},{4,3},{5,6},{6,5},{7,8},{8,7},{9,10},{10,... | collective-permute-start | bytes 786440 | tf_op jit(solution)/shard_map/ppermute | solution.py:163
  107.7 9.9 %collective-permute-start.39 = (f32[8,64,128]{2,1,0:T(8,128)S(1)}, f32[8,64,128]{2,1,0:T(8,128)S(1)}, u32[]{:S(2)}, u32[]{:S(2)}) collective-permute-start(f32[8,64,128]{2,1,0:T(8,128)S(1)} %sweep.43.own_ref), channel_id=1, source_target_pairs={{0,1},{1,0},{2,3},{3,2},{4,5},{5,4},{6,7},{7,6},{8,9},{9,8},{10,11... | collective-permute-start | bytes 786440 | tf_op jit(solution)/shard_map/ppermute | solution.py:164
  108.1 9.5 %collective-permute-start.40 = (f32[8,64,128]{2,1,0:T(8,128)S(1)}, f32[8,64,128]{2,1,0:T(8,128)S(1)}, u32[]{:S(2)}, u32[]{:S(2)}) collective-permute-start(f32[8,64,128]{2,1,0:T(8,128)S(1)} %sweep.43.own_ref), channel_id=1, source_target_pairs={{0,31},{1,2},{2,1},{3,4},{4,3},{5,6},{6,5},{7,8},{8,7},{9,10},{10,... | collective-permute-start | bytes 786440 | tf_op jit(solution)/shard_map/ppermute | solution.py:163
  113.3 9.8 %collective-permute-start.16 = (f32[8,64,128]{2,1,0:T(8,128)S(1)}, f32[8,64,128]{2,1,0:T(8,128)S(1)}, u32[]{:S(2)}, u32[]{:S(2)}) collective-permute-start(f32[8,64,128]{2,1,0:T(8,128)S(1)} %sweep.31.own_ref), channel_id=1, source_target_pairs={{0,1},{1,0},{2,3},{3,2},{4,5},{5,4},{6,7},{7,6},{8,9},{9,8},{10,11... | collective-permute-start | bytes 786440 | tf_op jit(solution)/shard_map/ppermute | solution.py:164
  113.4 9.7 %collective-permute-start.17 = (f32[8,64,128]{2,1,0:T(8,128)S(1)}, f32[8,64,128]{2,1,0:T(8,128)S(1)}, u32[]{:S(2)}, u32[]{:S(2)}) collective-permute-start(f32[8,64,128]{2,1,0:T(8,128)S(1)} %sweep.31.own_ref), channel_id=1, source_target_pairs={{0,31},{1,2},{2,1},{3,4},{4,3},{5,6},{6,5},{7,8},{8,7},{9,10},{10,... | collective-permute-start | bytes 786440 | tf_op jit(solution)/shard_map/ppermute | solution.py:163
  119.0 9.8 %collective-permute-start.41 = (f32[8,64,128]{2,1,0:T(8,128)S(1)}, f32[8,64,128]{2,1,0:T(8,128)S(1)}, u32[]{:S(2)}, u32[]{:S(2)}) collective-permute-start(f32[8,64,128]{2,1,0:T(8,128)S(1)} %sweep.44.own_ref), channel_id=1, source_target_pairs={{0,1},{1,0},{2,3},{3,2},{4,5},{5,4},{6,7},{7,6},{8,9},{9,8},{10,11... | collective-permute-start | bytes 786440 | tf_op jit(solution)/shard_map/ppermute | solution.py:164
  119.1 9.7 %collective-permute-start.42 = (f32[8,64,128]{2,1,0:T(8,128)S(1)}, f32[8,64,128]{2,1,0:T(8,128)S(1)}, u32[]{:S(2)}, u32[]{:S(2)}) collective-permute-start(f32[8,64,128]{2,1,0:T(8,128)S(1)} %sweep.44.own_ref), channel_id=1, source_target_pairs={{0,31},{1,2},{2,1},{3,4},{4,3},{5,6},{6,5},{7,8},{8,7},{9,10},{10,... | collective-permute-start | bytes 786440 | tf_op jit(solution)/shard_map/ppermute | solution.py:163
  124.5 9.8 %collective-permute-start.18 = (f32[8,64,128]{2,1,0:T(8,128)S(1)}, f32[8,64,128]{2,1,0:T(8,128)S(1)}, u32[]{:S(2)}, u32[]{:S(2)}) collective-permute-start(f32[8,64,128]{2,1,0:T(8,128)S(1)} %sweep.32.own_ref), channel_id=1, source_target_pairs={{0,1},{1,0},{2,3},{3,2},{4,5},{5,4},{6,7},{7,6},{8,9},{9,8},{10,11... | collective-permute-start | bytes 786440 | tf_op jit(solution)/shard_map/ppermute | solution.py:164
  125.3 9.4 %collective-permute-start.19 = (f32[8,64,128]{2,1,0:T(8,128)S(1)}, f32[8,64,128]{2,1,0:T(8,128)S(1)}, u32[]{:S(2)}, u32[]{:S(2)}) collective-permute-start(f32[8,64,128]{2,1,0:T(8,128)S(1)} %sweep.32.own_ref), channel_id=1, source_target_pairs={{0,31},{1,2},{2,1},{3,4},{4,3},{5,6},{6,5},{7,8},{8,7},{9,10},{10,... | collective-permute-start | bytes 786440 | tf_op jit(solution)/shard_map/ppermute | solution.py:163
  130.1 9.8 %collective-permute-start.43 = (f32[8,64,128]{2,1,0:T(8,128)S(1)}, f32[8,64,128]{2,1,0:T(8,128)S(1)}, u32[]{:S(2)}, u32[]{:S(2)}) collective-permute-start(f32[8,64,128]{2,1,0:T(8,128)S(1)} %sweep.45.own_ref), channel_id=1, source_target_pairs={{0,1},{1,0},{2,3},{3,2},{4,5},{5,4},{6,7},{7,6},{8,9},{9,8},{10,11... | collective-permute-start | bytes 786440 | tf_op jit(solution)/shard_map/ppermute | solution.py:164
  130.2 9.8 %collective-permute-start.44 = (f32[8,64,128]{2,1,0:T(8,128)S(1)}, f32[8,64,128]{2,1,0:T(8,128)S(1)}, u32[]{:S(2)}, u32[]{:S(2)}) collective-permute-start(f32[8,64,128]{2,1,0:T(8,128)S(1)} %sweep.45.own_ref), channel_id=1, source_target_pairs={{0,31},{1,2},{2,1},{3,4},{4,3},{5,6},{6,5},{7,8},{8,7},{9,10},{10,... | collective-permute-start | bytes 786440 | tf_op jit(solution)/shard_map/ppermute | solution.py:163
  136.1 9.5 %collective-permute-start.20 = (f32[8,64,128]{2,1,0:T(8,128)S(1)}, f32[8,64,128]{2,1,0:T(8,128)S(1)}, u32[]{:S(2)}, u32[]{:S(2)}) collective-permute-start(f32[8,64,128]{2,1,0:T(8,128)S(1)} %sweep.33.own_ref), channel_id=1, source_target_pairs={{0,1},{1,0},{2,3},{3,2},{4,5},{5,4},{6,7},{7,6},{8,9},{9,8},{10,11... | collective-permute-start | bytes 786440 | tf_op jit(solution)/shard_map/ppermute | solution.py:164
  136.2 9.5 %collective-permute-start.21 = (f32[8,64,128]{2,1,0:T(8,128)S(1)}, f32[8,64,128]{2,1,0:T(8,128)S(1)}, u32[]{:S(2)}, u32[]{:S(2)}) collective-permute-start(f32[8,64,128]{2,1,0:T(8,128)S(1)} %sweep.33.own_ref), channel_id=1, source_target_pairs={{0,31},{1,2},{2,1},{3,4},{4,3},{5,6},{6,5},{7,8},{8,7},{9,10},{10,... | collective-permute-start | bytes 786440 | tf_op jit(solution)/shard_map/ppermute | solution.py:163
  141.4 9.8 %collective-permute-start.45 = (f32[8,64,128]{2,1,0:T(8,128)S(1)}, f32[8,64,128]{2,1,0:T(8,128)S(1)}, u32[]{:S(2)}, u32[]{:S(2)}) collective-permute-start(f32[8,64,128]{2,1,0:T(8,128)S(1)} %sweep.46.own_ref), channel_id=1, source_target_pairs={{0,1},{1,0},{2,3},{3,2},{4,5},{5,4},{6,7},{7,6},{8,9},{9,8},{10,11... | collective-permute-start | bytes 786440 | tf_op jit(solution)/shard_map/ppermute | solution.py:164
  142.2 9.5 %collective-permute-start.46 = (f32[8,64,128]{2,1,0:T(8,128)S(1)}, f32[8,64,128]{2,1,0:T(8,128)S(1)}, u32[]{:S(2)}, u32[]{:S(2)}) collective-permute-start(f32[8,64,128]{2,1,0:T(8,128)S(1)} %sweep.46.own_ref), channel_id=1, source_target_pairs={{0,31},{1,2},{2,1},{3,4},{4,3},{5,6},{6,5},{7,8},{8,7},{9,10},{10,... | collective-permute-start | bytes 786440 | tf_op jit(solution)/shard_map/ppermute | solution.py:163
  147.1 6.0 %collective-permute-start.22 = (f32[8,64,128]{2,1,0:T(8,128)S(1)}, f32[8,64,128]{2,1,0:T(8,128)S(1)}, u32[]{:S(2)}, u32[]{:S(2)}) collective-permute-start(f32[8,64,128]{2,1,0:T(8,128)S(1)} %sweep.34.own_ref), channel_id=1, source_target_pairs={{0,1},{1,0},{2,3},{3,2},{4,5},{5,4},{6,7},{7,6},{8,9},{9,8},{10,11... | collective-permute-start | bytes 786440 | tf_op jit(solution)/shard_map/ppermute | solution.py:164
  147.2 9.6 %collective-permute-start.23 = (f32[8,64,128]{2,1,0:T(8,128)S(1)}, f32[8,64,128]{2,1,0:T(8,128)S(1)}, u32[]{:S(2)}, u32[]{:S(2)}) collective-permute-start(f32[8,64,128]{2,1,0:T(8,128)S(1)} %sweep.34.own_ref), channel_id=1, source_target_pairs={{0,31},{1,2},{2,1},{3,4},{4,3},{5,6},{6,5},{7,8},{8,7},{9,10},{10,... | collective-permute-start | bytes 786440 | tf_op jit(solution)/shard_map/ppermute | solution.py:163
  153.0 5.1 %copy-start.4 = (f32[8,64,128]{2,1,0:T(8,128)}, f32[8,64,128]{2,1,0:T(8,128)S(1)}, u32[]{:S(2)}) copy-start(f32[8,64,128]{2,1,0:T(8,128)S(1)} %sweep.47.refs_1_) | copy-start | bytes 786436
  153.0 5.4 %collective-permute-start.48 = (f32[8,64,128]{2,1,0:T(8,128)S(1)}, f32[8,64,128]{2,1,0:T(8,128)S(1)}, u32[]{:S(2)}, u32[]{:S(2)}) collective-permute-start(f32[8,64,128]{2,1,0:T(8,128)S(1)} %sweep.47.refs_1_), channel_id=1, source_target_pairs={{0,1},{1,0},{2,3},{3,2},{4,5},{5,4},{6,7},{7,6},{8,9},{9,8},{10,11... | collective-permute-start | bytes 786440 | tf_op jit(solution)/shard_map/ppermute | solution.py:164
  158.2 1.6 copy-start.5
  158.2 1.6 collective-permute-start.47
  158.4 1.4 copy-start.8
  159.8 0.7 copy-start.9

commit v2 on v1

v2 whole, which is shorter than its diff:
```python
import functools

import jax
import jax.numpy as jnp
from jax import lax
from jax.experimental import pallas as pl
from jax.experimental.pallas import tpu as pltpu
from jax.sharding import PartitionSpec as P

SWEEPS = 12
CHUNKS = 2
AXES = ("states", "act")
VMEM = pltpu.VMEM
SMEM = pltpu.SMEM
HBM = pltpu.HBM
WHOLE = pl.BlockSpec(memory_space=VMEM)
SCALARS = pl.BlockSpec(memory_space=SMEM)
ANYWHERE = pl.BlockSpec(memory_space=pl.ANY)


def split(x):
    high = x.astype(jnp.bfloat16)
    return high, (x - high.astype(jnp.float32)).astype(jnp.bfloat16)


def unit(rows, repeats=1):
    row = lax.broadcasted_iota(jnp.int32, (rows, rows), 0)
    col = lax.broadcasted_iota(jnp.int32, (rows, rows), 1)
    one = jnp.where(row == col, 1.0, 0.0).astype(jnp.bfloat16)
    return jnp.concatenate([one] * repeats, axis=1)


def times_turned(left, right):
    return lax.dot_general(left, right, (((1,), (1,)), ((), ())), preferred_element_type=jnp.float32)


def turn_targets(held_ref, out_refs):
    blocks, width, lanes = out_refs[0].shape
    one = unit(held_ref.shape[1])
    for b in range(blocks):
        hit = held_ref[b * lanes : (b + 1) * lanes, :].astype(jnp.float32).astype(jnp.bfloat16)
        turned = times_turned(one, hit)
        for c, out_ref in enumerate(out_refs):
            out_ref[b] = turned[c * width : (c + 1) * width, :]


def half_of(ref, part):
    rows = ref.shape[0] // 2
    return ref.at[pl.ds(pl.multiple_of(part * rows, rows), rows)]


def own_kernel(targets_ref, *refs):
    out_refs, (held_ref, sem) = refs[:CHUNKS], refs[CHUNKS:]
    copy = pltpu.make_async_copy(half_of(targets_ref, lax.axis_index("act")), held_ref, sem)
    copy.start()
    copy.wait()
    turn_targets(held_ref, out_refs)


def turn_tiles(tiles_ref, first, out_ref, start):
    blocks, _, side, _ = out_ref.shape
    lanes = side // 2
    one = unit(lanes)
    for b in range(blocks):
        for a in range(tiles_ref.shape[0]):
            for t in range(2):
                both = jnp.concatenate(split(tiles_ref[a, first + b, t]), axis=0)
                out_ref[b, start + a, t * lanes : (t + 1) * lanes] = times_turned(one, both).astype(jnp.bfloat16)


def rest_kernel(columns_ref, targets_ref, tiles_ref, taken_ref, slots_ref, right_ref, *refs):
    out_refs, (held_ref, tiles_held_ref, sems) = refs[:CHUNKS], refs[CHUNKS:]
    core = lax.axis_index("act")
    blocks, acts_here = tiles_held_ref.shape[1], tiles_held_ref.shape[0]
    own_tiles = tiles_ref.at[:, pl.ds(pl.multiple_of(core * blocks, blocks), blocks)]
    copies = [
        pltpu.make_async_copy(half_of(targets_ref, 1 - core), held_ref, sems.at[0]),
        pltpu.make_async_copy(own_tiles, tiles_held_ref, sems.at[1]),
    ]
    for copy in copies:
        copy.start()
    fill_slots(columns_ref, slots_ref)
    turn_tiles(taken_ref, core * blocks, right_ref, acts_here)
    for copy in copies:
        copy.wait()
    turn_targets(held_ref, out_refs)
    turn_tiles(tiles_held_ref, 0, right_ref, 0)


def fill_slots(columns_ref, out_ref):
    actions, _, row_blocks = columns_ref.shape
    blocks, half = row_blocks // 2, actions // 2
    total = row_blocks * lax.axis_size("states")
    core = lax.axis_index("act")
    start = lax.axis_index("states") * row_blocks + core * blocks - blocks
    for n in range(actions):
        action = (core if n < half else 1 - core) * half + n % half
        for b in range(blocks):
            for t in range(2):
                slot = columns_ref[action, t, core * blocks + b] - start
                slot = jnp.where(slot < 0, slot + total, slot)
                out_ref[(n * blocks + b) * 2 + t] = jnp.where(slot >= total, slot - total, slot)


def sweep_kernel(slot_ref, right_ref, own_ref, ici_ref, sib_ref, target_ref, out_ref, parts_ref):
    blocks, width, lanes = own_ref.shape
    core = lax.axis_index("act")
    for place, ref in ((1, own_ref), (2 - 2 * core, sib_ref), (2 * core, ici_ref)):
        for b in range(blocks):
            high, low = split(ref[b])
            parts_ref[place * blocks + b, :width] = high
            parts_ref[place * blocks + b, width:] = low
    for b in range(blocks):
        largest = None
        for a in range(right_ref.shape[1]):
            at = (a * blocks + b) * 2
            left = jnp.concatenate([parts_ref[slot_ref[at]], parts_ref[slot_ref[at + 1]]], axis=1)
            both = jnp.dot(left, right_ref[b, a], preferred_element_type=jnp.float32)
            q = (both[:width, :lanes] + both[:width, lanes:]) + (both[width:, :lanes] + both[width:, lanes:])
            largest = q if largest is None else jnp.maximum(largest, q)
        out_ref[b] = jnp.where(target_ref[b] == 1.0, 1.0, largest)


def finish_kernel(*refs):
    own_refs, sib_refs, (out_ref, held_ref, sems) = refs[:CHUNKS], refs[CHUNKS : 2 * CHUNKS], refs[2 * CHUNKS :]
    blocks, width, lanes = own_refs[0].shape
    core = lax.axis_index("act")
    one = unit(lanes, 3)
    copies = []
    for n, (part, group) in enumerate(((core, own_refs), (1 - core, sib_refs))):
        for b in range(blocks):
            panel = jnp.concatenate([ref[b] for ref in group], axis=0)
            high = panel.astype(jnp.bfloat16)
            middle, low = split(panel - high.astype(jnp.float32))
            held_ref[n, b * lanes : (b + 1) * lanes] = times_turned(one, jnp.concatenate([high, middle, low], axis=1))
        copies.append(pltpu.make_async_copy(held_ref.at[n], half_of(out_ref, part), sems.at[n]))
        copies[-1].start()
    for copy in copies:
        copy.wait()


def per_device(transitions, columns, targets):
    acts_here, row_blocks, _, lanes, _ = transitions.shape
    sets = targets.shape[1]
    width = sets // CHUNKS
    blocks = row_blocks // 2
    devices = 2 * lax.axis_size("states")

    to_sib = [(i, i ^ 1) for i in range(devices)]
    to_ici = [(i, (i + 1) % devices if i % 2 else (i - 1) % devices) for i in range(devices)]
    chunk = jax.ShapeDtypeStruct((blocks, width, lanes), jnp.float32)

    taken = lax.ppermute(transitions, AXES, to_sib)

    panel = pltpu.VMEM((blocks * lanes, sets), jnp.int32)
    targets = pltpu.with_memory_space_constraint(targets, HBM)
    zero = pl.pallas_call(
        own_kernel,
        out_shape=[chunk] * CHUNKS,
        in_specs=[ANYWHERE],
        out_specs=[WHOLE] * CHUNKS,
        scratch_shapes=[panel, pltpu.SemaphoreType.DMA],
        name="own_targets",
        compiler_params=pltpu.CompilerParams(vmem_limit_bytes=4 << 20),
    )(targets)
    ici = [lax.ppermute(v, AXES, to_ici) for v in zero]

    slots, right, *sib = pl.pallas_call(
        rest_kernel,
        out_shape=[
            SMEM((2 * acts_here * blocks * 2,), jnp.int32),
            jax.ShapeDtypeStruct((blocks, 2 * acts_here, 2 * lanes, 2 * lanes), jnp.bfloat16),
        ]
        + [chunk] * CHUNKS,
        in_specs=[SCALARS, ANYWHERE, ANYWHERE, WHOLE],
        out_specs=[SCALARS] + [WHOLE] * (1 + CHUNKS),
        scratch_shapes=[panel, pltpu.VMEM((acts_here, blocks, 2, lanes, lanes), jnp.float32), pltpu.SemaphoreType.DMA((2,))],
        name="rest",
        compiler_params=pltpu.CompilerParams(vmem_limit_bytes=16 << 20),
    )(columns.transpose(0, 2, 1), targets, pltpu.with_memory_space_constraint(transitions, HBM), taken)
    slots = pltpu.with_memory_space_constraint(slots, SMEM)

    def sweep(own, sib, ici, zero):
        return pl.pallas_call(
            sweep_kernel,
            out_shape=chunk,
            in_specs=[SCALARS] + [WHOLE] * 5,
            out_specs=WHOLE,
            scratch_shapes=[pltpu.VMEM((3 * blocks, 2 * width, lanes), jnp.bfloat16)],
            name="sweep",
            compiler_params=pltpu.CompilerParams(vmem_limit_bytes=16 << 20),
            cost_estimate=pl.CostEstimate(
                flops=2 * 2 * acts_here * blocks * (2 * width) * (2 * lanes) ** 2,
                bytes_accessed=4 * 5 * blocks * width * lanes + 8 * acts_here * blocks * (2 * lanes) ** 2,
                transcendentals=0,
            ),
        )(slots, right, own, ici, sib, zero)

    zero, own = list(zero), list(zero)
    for step in range(SWEEPS):
        for c in range(CHUNKS):
            own[c] = sweep(own[c], sib[c], ici[c], zero[c])
            if step < SWEEPS - 1:
                ici[c] = lax.ppermute(own[c], AXES, to_ici)
            sib[c] = lax.ppermute(own[c], AXES, to_sib)

    return pl.pallas_call(
        finish_kernel,
        out_shape=jax.ShapeDtypeStruct((2 * blocks * lanes, sets), jnp.float32),
        in_specs=[WHOLE] * (2 * CHUNKS),
        out_specs=ANYWHERE,
        scratch_shapes=[pltpu.VMEM((2, blocks * lanes, sets), jnp.float32), pltpu.SemaphoreType.DMA((2,))],
        name="finish",
        compiler_params=pltpu.CompilerParams(vmem_limit_bytes=8 << 20),
    )(*own, *sib)


def solution(mesh):
    return jax.shard_map(
        per_device,
        mesh=mesh,
        in_specs=(P("act", "states", None, None, None), P(None, "states", None), P("states", None)),
        out_specs=P("states", None),
        check_vma=False,
    )
```

time: 163 us -> 148 us (0.908)
  Pallas kernels: 50.3 us -> 28.4 us
  starting transfers between devices: 97.7 us -> 112 us
  local copies, waits for them, and re-layouts: 5.78 us -> 0.69 us
  waiting for transfers between devices: 8.75 us -> 6.05 us
    pallas_call x28 -> x27, Pallas kernels: 50.3 us -> 28.4 us  [the longest x24 21.4 us: sweep(): pl.pallas_call(sweep_kernel, out_shape=chunk, in_specs=[SCALARS] + [WHOLE...]
    ppermute x22, starting transfers between devices: 85.3 us -> 104 us  [per_device(): ici[c] = lax.ppermute(own[c], AXES, to_ici)]
    ppermute x24, starting transfers between devices: 5.23 us -> 0.99 us  [per_device(): sib[c] = lax.ppermute(own[c], AXES, to_sib)]
    dynamic_slice x2 -> x0, local copies, waits for them, and re-layouts: 3.25 us -> none  [the longest x1 3.18 us: per_device(): lax.dynamic_slice_in_dim(transitions, (1 - core) * blocks, blocks, 1)]
    ppermute x22, waiting for transfers between devices: 7.34 us -> 4.47 us  [per_device(): ici[c] = lax.ppermute(own[c], AXES, to_ici)]
  transfers between devices with their start and end apart: 49 -> 49, of which waited for: 12 -> 3; matrix products, arithmetic and copies ran while one was open for 0% -> 0% of each run, Pallas kernels for 29% -> 18%
where the time goes in v2:
time: 148 us; the launch traced here: 147 us
  starting transfers between devices  112 us (76%)
  Pallas kernels  28.4 us (19%)
  waiting for transfers between devices  6.05 us (4%)
    ppermute x22, starting transfers between devices, per_device(): ici[c] = lax.ppermute(own[c], AXES, to_ici)  104 us
    pallas_call x24, Pallas kernels, sweep(): pl.pallas_call(sweep_kernel, out_shape=chunk, in_specs=[SCALARS] + [WHOLE...  21.4 us
    ppermute x2, starting transfers between devices, per_device(): ici = [lax.ppermute(v, AXES, to_ici) for v in zero]  6.74 us
    ppermute x22, waiting for transfers between devices, per_device(): ici[c] = lax.ppermute(own[c], AXES, to_ici)  4.47 us
    pallas_call x1, Pallas kernels, per_device(): pl.pallas_call(rest_kernel, out_shape=[SMEM((2 * acts_here * blocks * 2,)...  4.03 us
  transfers between devices with their start and end apart: 49, of which 3 were waited for; matrix products, arithmetic and copies ran while one was open for 0% of the time, Pallas kernels for 18%

profile of v2, /device:TPU:0, one launch (start us, length us, event | category | flops | bytes accessed | tf_op | source)
XLA Modules:
  0.0 147.5 jit_solution(11224133391444265835)
XLA Ops:
  0.0 0.5 collective-permute-start
  0.5 1.4 own_targets.1
  1.8 6.7 %collective-permute-start.24 = (f32[8,64,128]{2,1,0:T(8,128)S(1)}, f32[8,64,128]{2,1,0:T(8,128)S(1)}, u32[]{:S(2)}, u32[]{:S(2)}) collective-permute-start(f32[8,64,128]{2,1,0:T(8,128)S(1)} %get-tuple-element.15.own_ref.target_ref), channel_id=1, source_target_pairs={{0,31},{1,2},{2,1},{3,4},{4,3},{5,6},{6,5},{7,8},{8,7},{9,10},{10,... | collective-permute-start | bytes 786440 | tf_op jit(solution)/shard_map/ppermute | solution.py:166
  8.5 0.1 collective-permute-start.1
  8.6 0.7 copy-done
  9.3 4.0 %rest.1 = (s32[64]{0:T(128)S(4)}, bf16[8,4,256,256]{3,2,1,0:T(8,128)(2,1)S(1)}, f32[8,64,128]{2,1,0:T(8,128)S(1)}, f32[8,64,128]{2,1,0:T(8,128)S(1)}) custom-call(s32[4,2,16]{2,1,0:T(2,128)S(1)} %bitcast.1, s32[2048,128]{1,0:T(8,128)} %targets_ref.3, f32[2,16,2,128,128]{4,3,2,1,0:T(8,128)} %tiles_ref.1, ...), custom_call_target="tpu_custom_call" | custom-call | tf_op jit(solution)/shard_map/rest/pallas_call | solution.py:168
  13.3 0.0 collective-permute-done.24.ici_ref
  13.3 0.9 sweep.36.own_ref
  14.2 5.5 %collective-permute-start.25 = (f32[8,64,128]{2,1,0:T(8,128)S(1)}, f32[8,64,128]{2,1,0:T(8,128)S(1)}, u32[]{:S(2)}, u32[]{:S(2)}) collective-permute-start(f32[8,64,128]{2,1,0:T(8,128)S(1)} %sweep.36.own_ref), channel_id=1, source_target_pairs={{0,31},{1,2},{2,1},{3,4},{4,3},{5,6},{6,5},{7,8},{8,7},{9,10},{10,... | collective-permute-start | bytes 786440 | tf_op jit(solution)/shard_map/ppermute | solution.py:204
  19.7 0.0 collective-permute-start.26
  19.7 0.0 collective-permute-done.1.ici_ref
  19.7 0.9 sweep.24.own_ref
  20.6 2.1 %collective-permute-start.2 = (f32[8,64,128]{2,1,0:T(8,128)S(1)}, f32[8,64,128]{2,1,0:T(8,128)S(1)}, u32[]{:S(2)}, u32[]{:S(2)}) collective-permute-start(f32[8,64,128]{2,1,0:T(8,128)S(1)} %sweep.24.own_ref), channel_id=1, source_target_pairs={{0,31},{1,2},{2,1},{3,4},{4,3},{5,6},{6,5},{7,8},{8,7},{9,10},{10,... | collective-permute-start | bytes 786440 | tf_op jit(solution)/shard_map/ppermute | solution.py:204
  22.8 1.1 collective-permute-done.25.ici_ref
  23.9 0.9 sweep.37.own_ref
  24.8 5.4 %collective-permute-start.27 = (f32[8,64,128]{2,1,0:T(8,128)S(1)}, f32[8,64,128]{2,1,0:T(8,128)S(1)}, u32[]{:S(2)}, u32[]{:S(2)}) collective-permute-start(f32[8,64,128]{2,1,0:T(8,128)S(1)} %sweep.37.own_ref), channel_id=1, source_target_pairs={{0,31},{1,2},{2,1},{3,4},{4,3},{5,6},{6,5},{7,8},{8,7},{9,10},{10,... | collective-permute-start | bytes 786440 | tf_op jit(solution)/shard_map/ppermute | solution.py:204
  30.2 0.0 collective-permute-start.28
  30.2 0.0 collective-permute-done.2.ici_ref
  30.2 0.9 sweep.25.own_ref
  31.1 3.4 %collective-permute-start.4 = (f32[8,64,128]{2,1,0:T(8,128)S(1)}, f32[8,64,128]{2,1,0:T(8,128)S(1)}, u32[]{:S(2)}, u32[]{:S(2)}) collective-permute-start(f32[8,64,128]{2,1,0:T(8,128)S(1)} %sweep.25.own_ref), channel_id=1, source_target_pairs={{0,31},{1,2},{2,1},{3,4},{4,3},{5,6},{6,5},{7,8},{8,7},{9,10},{10,... | collective-permute-start | bytes 786440 | tf_op jit(solution)/shard_map/ppermute | solution.py:204
  34.5 0.3 collective-permute-start.5
  34.8 0.9 sweep.38.own_ref
  35.7 7.2 %collective-permute-start.29 = (f32[8,64,128]{2,1,0:T(8,128)S(1)}, f32[8,64,128]{2,1,0:T(8,128)S(1)}, u32[]{:S(2)}, u32[]{:S(2)}) collective-permute-start(f32[8,64,128]{2,1,0:T(8,128)S(1)} %sweep.38.own_ref), channel_id=1, source_target_pairs={{0,31},{1,2},{2,1},{3,4},{4,3},{5,6},{6,5},{7,8},{8,7},{9,10},{10,... | collective-permute-start | bytes 786440 | tf_op jit(solution)/shard_map/ppermute | solution.py:204
  43.0 0.9 sweep.26.own_ref
  43.9 4.7 %collective-permute-start.6 = (f32[8,64,128]{2,1,0:T(8,128)S(1)}, f32[8,64,128]{2,1,0:T(8,128)S(1)}, u32[]{:S(2)}, u32[]{:S(2)}) collective-permute-start(f32[8,64,128]{2,1,0:T(8,128)S(1)} %sweep.26.own_ref), channel_id=1, source_target_pairs={{0,31},{1,2},{2,1},{3,4},{4,3},{5,6},{6,5},{7,8},{8,7},{9,10},{10,... | collective-permute-start | bytes 786440 | tf_op jit(solution)/shard_map/ppermute | solution.py:204
  48.6 0.9 sweep.39.own_ref
  49.5 4.7 %collective-permute-start.31 = (f32[8,64,128]{2,1,0:T(8,128)S(1)}, f32[8,64,128]{2,1,0:T(8,128)S(1)}, u32[]{:S(2)}, u32[]{:S(2)}) collective-permute-start(f32[8,64,128]{2,1,0:T(8,128)S(1)} %sweep.39.own_ref), channel_id=1, source_target_pairs={{0,31},{1,2},{2,1},{3,4},{4,3},{5,6},{6,5},{7,8},{8,7},{9,10},{10,... | collective-permute-start | bytes 786440 | tf_op jit(solution)/shard_map/ppermute | solution.py:204
  54.2 0.9 sweep.27.own_ref
  55.1 4.7 %collective-permute-start.8 = (f32[8,64,128]{2,1,0:T(8,128)S(1)}, f32[8,64,128]{2,1,0:T(8,128)S(1)}, u32[]{:S(2)}, u32[]{:S(2)}) collective-permute-start(f32[8,64,128]{2,1,0:T(8,128)S(1)} %sweep.27.own_ref), channel_id=1, source_target_pairs={{0,31},{1,2},{2,1},{3,4},{4,3},{5,6},{6,5},{7,8},{8,7},{9,10},{10,... | collective-permute-start | bytes 786440 | tf_op jit(solution)/shard_map/ppermute | solution.py:204
  59.8 0.9 sweep.40.own_ref
  60.7 4.7 %collective-permute-start.33 = (f32[8,64,128]{2,1,0:T(8,128)S(1)}, f32[8,64,128]{2,1,0:T(8,128)S(1)}, u32[]{:S(2)}, u32[]{:S(2)}) collective-permute-start(f32[8,64,128]{2,1,0:T(8,128)S(1)} %sweep.40.own_ref), channel_id=1, source_target_pairs={{0,31},{1,2},{2,1},{3,4},{4,3},{5,6},{6,5},{7,8},{8,7},{9,10},{10,... | collective-permute-start | bytes 786440 | tf_op jit(solution)/shard_map/ppermute | solution.py:204
  65.5 0.9 sweep.28.own_ref
  66.3 4.7 %collective-permute-start.10 = (f32[8,64,128]{2,1,0:T(8,128)S(1)}, f32[8,64,128]{2,1,0:T(8,128)S(1)}, u32[]{:S(2)}, u32[]{:S(2)}) collective-permute-start(f32[8,64,128]{2,1,0:T(8,128)S(1)} %sweep.28.own_ref), channel_id=1, source_target_pairs={{0,31},{1,2},{2,1},{3,4},{4,3},{5,6},{6,5},{7,8},{8,7},{9,10},{10,... | collective-permute-start | bytes 786440 | tf_op jit(solution)/shard_map/ppermute | solution.py:204
  71.1 1.1 sweep.41.own_ref
  72.1 4.7 %collective-permute-start.35 = (f32[8,64,128]{2,1,0:T(8,128)S(1)}, f32[8,64,128]{2,1,0:T(8,128)S(1)}, u32[]{:S(2)}, u32[]{:S(2)}) collective-permute-start(f32[8,64,128]{2,1,0:T(8,128)S(1)} %sweep.41.own_ref), channel_id=1, source_target_pairs={{0,31},{1,2},{2,1},{3,4},{4,3},{5,6},{6,5},{7,8},{8,7},{9,10},{10,... | collective-permute-start | bytes 786440 | tf_op jit(solution)/shard_map/ppermute | solution.py:204
  76.9 0.9 sweep.29.own_ref
  77.8 4.7 %collective-permute-start.12 = (f32[8,64,128]{2,1,0:T(8,128)S(1)}, f32[8,64,128]{2,1,0:T(8,128)S(1)}, u32[]{:S(2)}, u32[]{:S(2)}) collective-permute-start(f32[8,64,128]{2,1,0:T(8,128)S(1)} %sweep.29.own_ref), channel_id=1, source_target_pairs={{0,31},{1,2},{2,1},{3,4},{4,3},{5,6},{6,5},{7,8},{8,7},{9,10},{10,... | collective-permute-start | bytes 786440 | tf_op jit(solution)/shard_map/ppermute | solution.py:204
  82.5 0.9 sweep.42.own_ref
  83.4 4.5 %collective-permute-start.37 = (f32[8,64,128]{2,1,0:T(8,128)S(1)}, f32[8,64,128]{2,1,0:T(8,128)S(1)}, u32[]{:S(2)}, u32[]{:S(2)}) collective-permute-start(f32[8,64,128]{2,1,0:T(8,128)S(1)} %sweep.42.own_ref), channel_id=1, source_target_pairs={{0,31},{1,2},{2,1},{3,4},{4,3},{5,6},{6,5},{7,8},{8,7},{9,10},{10,... | collective-permute-start | bytes 786440 | tf_op jit(solution)/shard_map/ppermute | solution.py:204
  87.9 0.9 sweep.30.own_ref
  88.8 4.7 %collective-permute-start.14 = (f32[8,64,128]{2,1,0:T(8,128)S(1)}, f32[8,64,128]{2,1,0:T(8,128)S(1)}, u32[]{:S(2)}, u32[]{:S(2)}) collective-permute-start(f32[8,64,128]{2,1,0:T(8,128)S(1)} %sweep.30.own_ref), channel_id=1, source_target_pairs={{0,31},{1,2},{2,1},{3,4},{4,3},{5,6},{6,5},{7,8},{8,7},{9,10},{10,... | collective-permute-start | bytes 786440 | tf_op jit(solution)/shard_map/ppermute | solution.py:204
  93.5 0.9 sweep.43.own_ref
  94.4 4.7 %collective-permute-start.39 = (f32[8,64,128]{2,1,0:T(8,128)S(1)}, f32[8,64,128]{2,1,0:T(8,128)S(1)}, u32[]{:S(2)}, u32[]{:S(2)}) collective-permute-start(f32[8,64,128]{2,1,0:T(8,128)S(1)} %sweep.43.own_ref), channel_id=1, source_target_pairs={{0,31},{1,2},{2,1},{3,4},{4,3},{5,6},{6,5},{7,8},{8,7},{9,10},{10,... | collective-permute-start | bytes 786440 | tf_op jit(solution)/shard_map/ppermute | solution.py:204
  99.2 0.9 sweep.31.own_ref
  100.1 4.7 %collective-permute-start.16 = (f32[8,64,128]{2,1,0:T(8,128)S(1)}, f32[8,64,128]{2,1,0:T(8,128)S(1)}, u32[]{:S(2)}, u32[]{:S(2)}) collective-permute-start(f32[8,64,128]{2,1,0:T(8,128)S(1)} %sweep.31.own_ref), channel_id=1, source_target_pairs={{0,31},{1,2},{2,1},{3,4},{4,3},{5,6},{6,5},{7,8},{8,7},{9,10},{10,... | collective-permute-start | bytes 786440 | tf_op jit(solution)/shard_map/ppermute | solution.py:204
  104.8 0.9 sweep.44.own_ref
  105.7 4.7 %collective-permute-start.41 = (f32[8,64,128]{2,1,0:T(8,128)S(1)}, f32[8,64,128]{2,1,0:T(8,128)S(1)}, u32[]{:S(2)}, u32[]{:S(2)}) collective-permute-start(f32[8,64,128]{2,1,0:T(8,128)S(1)} %sweep.44.own_ref), channel_id=1, source_target_pairs={{0,31},{1,2},{2,1},{3,4},{4,3},{5,6},{6,5},{7,8},{8,7},{9,10},{10,... | collective-permute-start | bytes 786440 | tf_op jit(solution)/shard_map/ppermute | solution.py:204
  110.4 0.9 sweep.32.own_ref
  111.3 4.7 %collective-permute-start.18 = (f32[8,64,128]{2,1,0:T(8,128)S(1)}, f32[8,64,128]{2,1,0:T(8,128)S(1)}, u32[]{:S(2)}, u32[]{:S(2)}) collective-permute-start(f32[8,64,128]{2,1,0:T(8,128)S(1)} %sweep.32.own_ref), channel_id=1, source_target_pairs={{0,31},{1,2},{2,1},{3,4},{4,3},{5,6},{6,5},{7,8},{8,7},{9,10},{10,... | collective-permute-start | bytes 786440 | tf_op jit(solution)/shard_map/ppermute | solution.py:204
  116.0 0.9 sweep.45.own_ref
  116.9 4.7 %collective-permute-start.43 = (f32[8,64,128]{2,1,0:T(8,128)S(1)}, f32[8,64,128]{2,1,0:T(8,128)S(1)}, u32[]{:S(2)}, u32[]{:S(2)}) collective-permute-start(f32[8,64,128]{2,1,0:T(8,128)S(1)} %sweep.45.own_ref), channel_id=1, source_target_pairs={{0,31},{1,2},{2,1},{3,4},{4,3},{5,6},{6,5},{7,8},{8,7},{9,10},{10,... | collective-permute-start | bytes 786440 | tf_op jit(solution)/shard_map/ppermute | solution.py:204
  121.6 0.9 sweep.33.own_ref
  122.5 4.7 %collective-permute-start.20 = (f32[8,64,128]{2,1,0:T(8,128)S(1)}, f32[8,64,128]{2,1,0:T(8,128)S(1)}, u32[]{:S(2)}, u32[]{:S(2)}) collective-permute-start(f32[8,64,128]{2,1,0:T(8,128)S(1)} %sweep.33.own_ref), channel_id=1, source_target_pairs={{0,31},{1,2},{2,1},{3,4},{4,3},{5,6},{6,5},{7,8},{8,7},{9,10},{10,... | collective-permute-start | bytes 786440 | tf_op jit(solution)/shard_map/ppermute | solution.py:204
  127.2 0.9 sweep.46.own_ref
  128.1 4.7 %collective-permute-start.45 = (f32[8,64,128]{2,1,0:T(8,128)S(1)}, f32[8,64,128]{2,1,0:T(8,128)S(1)}, u32[]{:S(2)}, u32[]{:S(2)}) collective-permute-start(f32[8,64,128]{2,1,0:T(8,128)S(1)} %sweep.46.own_ref), channel_id=1, source_target_pairs={{0,31},{1,2},{2,1},{3,4},{4,3},{5,6},{6,5},{7,8},{8,7},{9,10},{10,... | collective-permute-start | bytes 786440 | tf_op jit(solution)/shard_map/ppermute | solution.py:204
  132.9 0.9 sweep.34.own_ref
  133.8 4.7 %collective-permute-start.22 = (f32[8,64,128]{2,1,0:T(8,128)S(1)}, f32[8,64,128]{2,1,0:T(8,128)S(1)}, u32[]{:S(2)}, u32[]{:S(2)}) collective-permute-start(f32[8,64,128]{2,1,0:T(8,128)S(1)} %sweep.34.own_ref), channel_id=1, source_target_pairs={{0,31},{1,2},{2,1},{3,4},{4,3},{5,6},{6,5},{7,8},{8,7},{9,10},{10,... | collective-permute-start | bytes 786440 | tf_op jit(solution)/shard_map/ppermute | solution.py:204
  138.5 0.9 sweep.47.refs_1_
  139.4 0.6 collective-permute-start.48
  139.9 3.3 %collective-permute-done.22.ici_ref = f32[8,64,128]{2,1,0:T(8,128)S(1)} collective-permute-done((f32[8,64,128]{2,1,0:T(8,128)S(1)}, f32[8,64,128]{2,1,0:T(8,128)S(1)}, u32[]{:S(2)}, u32[]{:S(2)}) %collective-permute-start.22) | collective-permute-done | bytes 262176 | tf_op jit(solution)/shard_map/ppermute | solution.py:204
  143.2 0.9 sweep.35.refs_0_
  144.1 0.1 collective-permute-start.47
  144.2 1.5 %collective-permute-done.47.refs_2_ = f32[8,64,128]{2,1,0:T(8,128)S(1)} collective-permute-done((f32[8,64,128]{2,1,0:T(8,128)S(1)}, f32[8,64,128]{2,1,0:T(8,128)S(1)}, u32[]{:S(2)}, u32[]{:S(2)}) %collective-permute-start.47) | collective-permute-done | bytes 262176 | tf_op jit(solution)/shard_map/ppermute | solution.py:205
  145.7 1.6 %finish.1 = f32[2048,128]{1,0:T(8,128)} custom-call(f32[8,64,128]{2,1,0:T(8,128)S(1)} %sweep.35.refs_0_, f32[8,64,128]{2,1,0:T(8,128)S(1)} %sweep.47.refs_1_, f32[8,64,128]{2,1,0:T(8,128)S(1)} %collective-permute-done.47.refs_2_, f32[8,64,128]{2,1,0:T(8,128)S(1)} %collective-permute-done.48.refs_3_), custom_call_target="tpu_custom_call" | custom-call | tf_op jit(solution)/shard_map/finish/pallas_call | solution.py:207
  (63 shorter events, 0.2 us)
Async XLA Ops:
  0.0 8.6 %collective-permute-start = (f32[2,16,2,128,128]{4,3,2,1,0:T(8,128)}, f32[2,16,2,128,128]{4,3,2,1,0:T(8,128)S(1)}, u32[]{:S(2)}, u32[]{:S(2)}) collective-permute-start(f32[2,16,2,128,128]{4,3,2,1,0:T(8,128)} %tiles_ref.1), channel_id=1, source_target_pairs={{0,1},{1,0},{2,3},{3,2},{4,5},{5,4},{6,7},{7,6},{8,9},{9,8},{10,11... | collective-permute-start | bytes 12582920 | tf_op jit(solution)/shard_map/ppermute | solution.py:153
  1.8 11.5 %collective-permute-start.24 = (f32[8,64,128]{2,1,0:T(8,128)S(1)}, f32[8,64,128]{2,1,0:T(8,128)S(1)}, u32[]{:S(2)}, u32[]{:S(2)}) collective-permute-start(f32[8,64,128]{2,1,0:T(8,128)S(1)} %get-tuple-element.15.own_ref.target_ref), channel_id=1, source_target_pairs={{0,31},{1,2},{2,1},{3,4},{4,3},{5,6},{6,5},{7,8},{8,7},{9,10},{10,... | collective-permute-start | bytes 786440 | tf_op jit(solution)/shard_map/ppermute | solution.py:166
  8.5 11.3 %collective-permute-start.1 = (f32[8,64,128]{2,1,0:T(8,128)S(1)}, f32[8,64,128]{2,1,0:T(8,128)S(1)}, u32[]{:S(2)}, u32[]{:S(2)}) collective-permute-start(f32[8,64,128]{2,1,0:T(8,128)S(1)} %get-tuple-element.13.own_ref.target_ref), channel_id=1, source_target_pairs={{0,31},{1,2},{2,1},{3,4},{4,3},{5,6},{6,5},{7,8},{8,7},{9,10},{10,... | collective-permute-start | bytes 786440 | tf_op jit(solution)/shard_map/ppermute | solution.py:166
  8.6 0.7 copy-start
  14.2 9.7 %collective-permute-start.25 = (f32[8,64,128]{2,1,0:T(8,128)S(1)}, f32[8,64,128]{2,1,0:T(8,128)S(1)}, u32[]{:S(2)}, u32[]{:S(2)}) collective-permute-start(f32[8,64,128]{2,1,0:T(8,128)S(1)} %sweep.36.own_ref), channel_id=1, source_target_pairs={{0,31},{1,2},{2,1},{3,4},{4,3},{5,6},{6,5},{7,8},{8,7},{9,10},{10,... | collective-permute-start | bytes 786440 | tf_op jit(solution)/shard_map/ppermute | solution.py:204
  19.7 4.2 %collective-permute-start.26 = (f32[8,64,128]{2,1,0:T(8,128)S(1)}, f32[8,64,128]{2,1,0:T(8,128)S(1)}, u32[]{:S(2)}, u32[]{:S(2)}) collective-permute-start(f32[8,64,128]{2,1,0:T(8,128)S(1)} %sweep.36.own_ref), channel_id=1, source_target_pairs={{0,1},{1,0},{2,3},{3,2},{4,5},{5,4},{6,7},{7,6},{8,9},{9,8},{10,11... | collective-permute-start | bytes 786440 | tf_op jit(solution)/shard_map/ppermute | solution.py:205
  20.6 9.6 %collective-permute-start.2 = (f32[8,64,128]{2,1,0:T(8,128)S(1)}, f32[8,64,128]{2,1,0:T(8,128)S(1)}, u32[]{:S(2)}, u32[]{:S(2)}) collective-permute-start(f32[8,64,128]{2,1,0:T(8,128)S(1)} %sweep.24.own_ref), channel_id=1, source_target_pairs={{0,31},{1,2},{2,1},{3,4},{4,3},{5,6},{6,5},{7,8},{8,7},{9,10},{10,... | collective-permute-start | bytes 786440 | tf_op jit(solution)/shard_map/ppermute | solution.py:204
  22.7 7.5 %collective-permute-start.3 = (f32[8,64,128]{2,1,0:T(8,128)S(1)}, f32[8,64,128]{2,1,0:T(8,128)S(1)}, u32[]{:S(2)}, u32[]{:S(2)}) collective-permute-start(f32[8,64,128]{2,1,0:T(8,128)S(1)} %sweep.24.own_ref), channel_id=1, source_target_pairs={{0,1},{1,0},{2,3},{3,2},{4,5},{5,4},{6,7},{7,6},{8,9},{9,8},{10,11... | collective-permute-start | bytes 786440 | tf_op jit(solution)/shard_map/ppermute | solution.py:205
  24.8 10.1 %collective-permute-start.27 = (f32[8,64,128]{2,1,0:T(8,128)S(1)}, f32[8,64,128]{2,1,0:T(8,128)S(1)}, u32[]{:S(2)}, u32[]{:S(2)}) collective-permute-start(f32[8,64,128]{2,1,0:T(8,128)S(1)} %sweep.37.own_ref), channel_id=1, source_target_pairs={{0,31},{1,2},{2,1},{3,4},{4,3},{5,6},{6,5},{7,8},{8,7},{9,10},{10,... | collective-permute-start | bytes 786440 | tf_op jit(solution)/shard_map/ppermute | solution.py:204
  30.2 4.7 %collective-permute-start.28 = (f32[8,64,128]{2,1,0:T(8,128)S(1)}, f32[8,64,128]{2,1,0:T(8,128)S(1)}, u32[]{:S(2)}, u32[]{:S(2)}) collective-permute-start(f32[8,64,128]{2,1,0:T(8,128)S(1)} %sweep.37.own_ref), channel_id=1, source_target_pairs={{0,1},{1,0},{2,3},{3,2},{4,5},{5,4},{6,7},{7,6},{8,9},{9,8},{10,11... | collective-permute-start | bytes 786440 | tf_op jit(solution)/shard_map/ppermute | solution.py:205
  31.1 11.9 %collective-permute-start.4 = (f32[8,64,128]{2,1,0:T(8,128)S(1)}, f32[8,64,128]{2,1,0:T(8,128)S(1)}, u32[]{:S(2)}, u32[]{:S(2)}) collective-permute-start(f32[8,64,128]{2,1,0:T(8,128)S(1)} %sweep.25.own_ref), channel_id=1, source_target_pairs={{0,31},{1,2},{2,1},{3,4},{4,3},{5,6},{6,5},{7,8},{8,7},{9,10},{10,... | collective-permute-start | bytes 786440 | tf_op jit(solution)/shard_map/ppermute | solution.py:204
  34.5 8.4 %collective-permute-start.5 = (f32[8,64,128]{2,1,0:T(8,128)S(1)}, f32[8,64,128]{2,1,0:T(8,128)S(1)}, u32[]{:S(2)}, u32[]{:S(2)}) collective-permute-start(f32[8,64,128]{2,1,0:T(8,128)S(1)} %sweep.25.own_ref), channel_id=1, source_target_pairs={{0,1},{1,0},{2,3},{3,2},{4,5},{5,4},{6,7},{7,6},{8,9},{9,8},{10,11... | collective-permute-start | bytes 786440 | tf_op jit(solution)/shard_map/ppermute | solution.py:205
  35.7 12.9 %collective-permute-start.29 = (f32[8,64,128]{2,1,0:T(8,128)S(1)}, f32[8,64,128]{2,1,0:T(8,128)S(1)}, u32[]{:S(2)}, u32[]{:S(2)}) collective-permute-start(f32[8,64,128]{2,1,0:T(8,128)S(1)} %sweep.38.own_ref), channel_id=1, source_target_pairs={{0,31},{1,2},{2,1},{3,4},{4,3},{5,6},{6,5},{7,8},{8,7},{9,10},{10,... | collective-permute-start | bytes 786440 | tf_op jit(solution)/shard_map/ppermute | solution.py:204
  43.0 5.6 %collective-permute-start.30 = (f32[8,64,128]{2,1,0:T(8,128)S(1)}, f32[8,64,128]{2,1,0:T(8,128)S(1)}, u32[]{:S(2)}, u32[]{:S(2)}) collective-permute-start(f32[8,64,128]{2,1,0:T(8,128)S(1)} %sweep.38.own_ref), channel_id=1, source_target_pairs={{0,1},{1,0},{2,3},{3,2},{4,5},{5,4},{6,7},{7,6},{8,9},{9,8},{10,11... | collective-permute-start | bytes 786440 | tf_op jit(solution)/shard_map/ppermute | solution.py:205
  43.9 10.3 %collective-permute-start.6 = (f32[8,64,128]{2,1,0:T(8,128)S(1)}, f32[8,64,128]{2,1,0:T(8,128)S(1)}, u32[]{:S(2)}, u32[]{:S(2)}) collective-permute-start(f32[8,64,128]{2,1,0:T(8,128)S(1)} %sweep.26.own_ref), channel_id=1, source_target_pairs={{0,31},{1,2},{2,1},{3,4},{4,3},{5,6},{6,5},{7,8},{8,7},{9,10},{10,... | collective-permute-start | bytes 786440 | tf_op jit(solution)/shard_map/ppermute | solution.py:204
  48.6 5.6 %collective-permute-start.7 = (f32[8,64,128]{2,1,0:T(8,128)S(1)}, f32[8,64,128]{2,1,0:T(8,128)S(1)}, u32[]{:S(2)}, u32[]{:S(2)}) collective-permute-start(f32[8,64,128]{2,1,0:T(8,128)S(1)} %sweep.26.own_ref), channel_id=1, source_target_pairs={{0,1},{1,0},{2,3},{3,2},{4,5},{5,4},{6,7},{7,6},{8,9},{9,8},{10,11... | collective-permute-start | bytes 786440 | tf_op jit(solution)/shard_map/ppermute | solution.py:205
  49.5 10.3 %collective-permute-start.31 = (f32[8,64,128]{2,1,0:T(8,128)S(1)}, f32[8,64,128]{2,1,0:T(8,128)S(1)}, u32[]{:S(2)}, u32[]{:S(2)}) collective-permute-start(f32[8,64,128]{2,1,0:T(8,128)S(1)} %sweep.39.own_ref), channel_id=1, source_target_pairs={{0,31},{1,2},{2,1},{3,4},{4,3},{5,6},{6,5},{7,8},{8,7},{9,10},{10,... | collective-permute-start | bytes 786440 | tf_op jit(solution)/shard_map/ppermute | solution.py:204
  54.2 5.6 %collective-permute-start.32 = (f32[8,64,128]{2,1,0:T(8,128)S(1)}, f32[8,64,128]{2,1,0:T(8,128)S(1)}, u32[]{:S(2)}, u32[]{:S(2)}) collective-permute-start(f32[8,64,128]{2,1,0:T(8,128)S(1)} %sweep.39.own_ref), channel_id=1, source_target_pairs={{0,1},{1,0},{2,3},{3,2},{4,5},{5,4},{6,7},{7,6},{8,9},{9,8},{10,11... | collective-permute-start | bytes 786440 | tf_op jit(solution)/shard_map/ppermute | solution.py:205
  55.1 10.3 %collective-permute-start.8 = (f32[8,64,128]{2,1,0:T(8,128)S(1)}, f32[8,64,128]{2,1,0:T(8,128)S(1)}, u32[]{:S(2)}, u32[]{:S(2)}) collective-permute-start(f32[8,64,128]{2,1,0:T(8,128)S(1)} %sweep.27.own_ref), channel_id=1, source_target_pairs={{0,31},{1,2},{2,1},{3,4},{4,3},{5,6},{6,5},{7,8},{8,7},{9,10},{10,... | collective-permute-start | bytes 786440 | tf_op jit(solution)/shard_map/ppermute | solution.py:204
  59.8 5.6 %collective-permute-start.9 = (f32[8,64,128]{2,1,0:T(8,128)S(1)}, f32[8,64,128]{2,1,0:T(8,128)S(1)}, u32[]{:S(2)}, u32[]{:S(2)}) collective-permute-start(f32[8,64,128]{2,1,0:T(8,128)S(1)} %sweep.27.own_ref), channel_id=1, source_target_pairs={{0,1},{1,0},{2,3},{3,2},{4,5},{5,4},{6,7},{7,6},{8,9},{9,8},{10,11... | collective-permute-start | bytes 786440 | tf_op jit(solution)/shard_map/ppermute | solution.py:205
  60.7 10.3 %collective-permute-start.33 = (f32[8,64,128]{2,1,0:T(8,128)S(1)}, f32[8,64,128]{2,1,0:T(8,128)S(1)}, u32[]{:S(2)}, u32[]{:S(2)}) collective-permute-start(f32[8,64,128]{2,1,0:T(8,128)S(1)} %sweep.40.own_ref), channel_id=1, source_target_pairs={{0,31},{1,2},{2,1},{3,4},{4,3},{5,6},{6,5},{7,8},{8,7},{9,10},{10,... | collective-permute-start | bytes 786440 | tf_op jit(solution)/shard_map/ppermute | solution.py:204
  65.4 5.6 %collective-permute-start.34 = (f32[8,64,128]{2,1,0:T(8,128)S(1)}, f32[8,64,128]{2,1,0:T(8,128)S(1)}, u32[]{:S(2)}, u32[]{:S(2)}) collective-permute-start(f32[8,64,128]{2,1,0:T(8,128)S(1)} %sweep.40.own_ref), channel_id=1, source_target_pairs={{0,1},{1,0},{2,3},{3,2},{4,5},{5,4},{6,7},{7,6},{8,9},{9,8},{10,11... | collective-permute-start | bytes 786440 | tf_op jit(solution)/shard_map/ppermute | solution.py:205
  66.3 10.5 %collective-permute-start.10 = (f32[8,64,128]{2,1,0:T(8,128)S(1)}, f32[8,64,128]{2,1,0:T(8,128)S(1)}, u32[]{:S(2)}, u32[]{:S(2)}) collective-permute-start(f32[8,64,128]{2,1,0:T(8,128)S(1)} %sweep.28.own_ref), channel_id=1, source_target_pairs={{0,31},{1,2},{2,1},{3,4},{4,3},{5,6},{6,5},{7,8},{8,7},{9,10},{10,... | collective-permute-start | bytes 786440 | tf_op jit(solution)/shard_map/ppermute | solution.py:204
  71.1 5.8 %collective-permute-start.11 = (f32[8,64,128]{2,1,0:T(8,128)S(1)}, f32[8,64,128]{2,1,0:T(8,128)S(1)}, u32[]{:S(2)}, u32[]{:S(2)}) collective-permute-start(f32[8,64,128]{2,1,0:T(8,128)S(1)} %sweep.28.own_ref), channel_id=1, source_target_pairs={{0,1},{1,0},{2,3},{3,2},{4,5},{5,4},{6,7},{7,6},{8,9},{9,8},{10,11... | collective-permute-start | bytes 786440 | tf_op jit(solution)/shard_map/ppermute | solution.py:205
  72.1 10.3 %collective-permute-start.35 = (f32[8,64,128]{2,1,0:T(8,128)S(1)}, f32[8,64,128]{2,1,0:T(8,128)S(1)}, u32[]{:S(2)}, u32[]{:S(2)}) collective-permute-start(f32[8,64,128]{2,1,0:T(8,128)S(1)} %sweep.41.own_ref), channel_id=1, source_target_pairs={{0,31},{1,2},{2,1},{3,4},{4,3},{5,6},{6,5},{7,8},{8,7},{9,10},{10,... | collective-permute-start | bytes 786440 | tf_op jit(solution)/shard_map/ppermute | solution.py:204
  76.9 5.6 %collective-permute-start.36 = (f32[8,64,128]{2,1,0:T(8,128)S(1)}, f32[8,64,128]{2,1,0:T(8,128)S(1)}, u32[]{:S(2)}, u32[]{:S(2)}) collective-permute-start(f32[8,64,128]{2,1,0:T(8,128)S(1)} %sweep.41.own_ref), channel_id=1, source_target_pairs={{0,1},{1,0},{2,3},{3,2},{4,5},{5,4},{6,7},{7,6},{8,9},{9,8},{10,11... | collective-permute-start | bytes 786440 | tf_op jit(solution)/shard_map/ppermute | solution.py:205
  77.8 10.2 %collective-permute-start.12 = (f32[8,64,128]{2,1,0:T(8,128)S(1)}, f32[8,64,128]{2,1,0:T(8,128)S(1)}, u32[]{:S(2)}, u32[]{:S(2)}) collective-permute-start(f32[8,64,128]{2,1,0:T(8,128)S(1)} %sweep.29.own_ref), channel_id=1, source_target_pairs={{0,31},{1,2},{2,1},{3,4},{4,3},{5,6},{6,5},{7,8},{8,7},{9,10},{10,... | collective-permute-start | bytes 786440 | tf_op jit(solution)/shard_map/ppermute | solution.py:204
  82.5 5.4 %collective-permute-start.13 = (f32[8,64,128]{2,1,0:T(8,128)S(1)}, f32[8,64,128]{2,1,0:T(8,128)S(1)}, u32[]{:S(2)}, u32[]{:S(2)}) collective-permute-start(f32[8,64,128]{2,1,0:T(8,128)S(1)} %sweep.29.own_ref), channel_id=1, source_target_pairs={{0,1},{1,0},{2,3},{3,2},{4,5},{5,4},{6,7},{7,6},{8,9},{9,8},{10,11... | collective-permute-start | bytes 786440 | tf_op jit(solution)/shard_map/ppermute | solution.py:205
  83.4 10.2 %collective-permute-start.37 = (f32[8,64,128]{2,1,0:T(8,128)S(1)}, f32[8,64,128]{2,1,0:T(8,128)S(1)}, u32[]{:S(2)}, u32[]{:S(2)}) collective-permute-start(f32[8,64,128]{2,1,0:T(8,128)S(1)} %sweep.42.own_ref), channel_id=1, source_target_pairs={{0,31},{1,2},{2,1},{3,4},{4,3},{5,6},{6,5},{7,8},{8,7},{9,10},{10,... | collective-permute-start | bytes 786440 | tf_op jit(solution)/shard_map/ppermute | solution.py:204
  87.9 5.6 %collective-permute-start.38 = (f32[8,64,128]{2,1,0:T(8,128)S(1)}, f32[8,64,128]{2,1,0:T(8,128)S(1)}, u32[]{:S(2)}, u32[]{:S(2)}) collective-permute-start(f32[8,64,128]{2,1,0:T(8,128)S(1)} %sweep.42.own_ref), channel_id=1, source_target_pairs={{0,1},{1,0},{2,3},{3,2},{4,5},{5,4},{6,7},{7,6},{8,9},{9,8},{10,11... | collective-permute-start | bytes 786440 | tf_op jit(solution)/shard_map/ppermute | solution.py:205
  88.8 10.3 %collective-permute-start.14 = (f32[8,64,128]{2,1,0:T(8,128)S(1)}, f32[8,64,128]{2,1,0:T(8,128)S(1)}, u32[]{:S(2)}, u32[]{:S(2)}) collective-permute-start(f32[8,64,128]{2,1,0:T(8,128)S(1)} %sweep.30.own_ref), channel_id=1, source_target_pairs={{0,31},{1,2},{2,1},{3,4},{4,3},{5,6},{6,5},{7,8},{8,7},{9,10},{10,... | collective-permute-start | bytes 786440 | tf_op jit(solution)/shard_map/ppermute | solution.py:204
  93.5 5.6 %collective-permute-start.15 = (f32[8,64,128]{2,1,0:T(8,128)S(1)}, f32[8,64,128]{2,1,0:T(8,128)S(1)}, u32[]{:S(2)}, u32[]{:S(2)}) collective-permute-start(f32[8,64,128]{2,1,0:T(8,128)S(1)} %sweep.30.own_ref), channel_id=1, source_target_pairs={{0,1},{1,0},{2,3},{3,2},{4,5},{5,4},{6,7},{7,6},{8,9},{9,8},{10,11... | collective-permute-start | bytes 786440 | tf_op jit(solution)/shard_map/ppermute | solution.py:205
  94.4 10.3 %collective-permute-start.39 = (f32[8,64,128]{2,1,0:T(8,128)S(1)}, f32[8,64,128]{2,1,0:T(8,128)S(1)}, u32[]{:S(2)}, u32[]{:S(2)}) collective-permute-start(f32[8,64,128]{2,1,0:T(8,128)S(1)} %sweep.43.own_ref), channel_id=1, source_target_pairs={{0,31},{1,2},{2,1},{3,4},{4,3},{5,6},{6,5},{7,8},{8,7},{9,10},{10,... | collective-permute-start | bytes 786440 | tf_op jit(solution)/shard_map/ppermute | solution.py:204
  99.1 5.6 %collective-permute-start.40 = (f32[8,64,128]{2,1,0:T(8,128)S(1)}, f32[8,64,128]{2,1,0:T(8,128)S(1)}, u32[]{:S(2)}, u32[]{:S(2)}) collective-permute-start(f32[8,64,128]{2,1,0:T(8,128)S(1)} %sweep.43.own_ref), channel_id=1, source_target_pairs={{0,1},{1,0},{2,3},{3,2},{4,5},{5,4},{6,7},{7,6},{8,9},{9,8},{10,11... | collective-permute-start | bytes 786440 | tf_op jit(solution)/shard_map/ppermute | solution.py:205
  100.1 10.3 %collective-permute-start.16 = (f32[8,64,128]{2,1,0:T(8,128)S(1)}, f32[8,64,128]{2,1,0:T(8,128)S(1)}, u32[]{:S(2)}, u32[]{:S(2)}) collective-permute-start(f32[8,64,128]{2,1,0:T(8,128)S(1)} %sweep.31.own_ref), channel_id=1, source_target_pairs={{0,31},{1,2},{2,1},{3,4},{4,3},{5,6},{6,5},{7,8},{8,7},{9,10},{10,... | collective-permute-start | bytes 786440 | tf_op jit(solution)/shard_map/ppermute | solution.py:204
  104.8 5.6 %collective-permute-start.17 = (f32[8,64,128]{2,1,0:T(8,128)S(1)}, f32[8,64,128]{2,1,0:T(8,128)S(1)}, u32[]{:S(2)}, u32[]{:S(2)}) collective-permute-start(f32[8,64,128]{2,1,0:T(8,128)S(1)} %sweep.31.own_ref), channel_id=1, source_target_pairs={{0,1},{1,0},{2,3},{3,2},{4,5},{5,4},{6,7},{7,6},{8,9},{9,8},{10,11... | collective-permute-start | bytes 786440 | tf_op jit(solution)/shard_map/ppermute | solution.py:205
  105.7 10.3 %collective-permute-start.41 = (f32[8,64,128]{2,1,0:T(8,128)S(1)}, f32[8,64,128]{2,1,0:T(8,128)S(1)}, u32[]{:S(2)}, u32[]{:S(2)}) collective-permute-start(f32[8,64,128]{2,1,0:T(8,128)S(1)} %sweep.44.own_ref), channel_id=1, source_target_pairs={{0,31},{1,2},{2,1},{3,4},{4,3},{5,6},{6,5},{7,8},{8,7},{9,10},{10,... | collective-permute-start | bytes 786440 | tf_op jit(solution)/shard_map/ppermute | solution.py:204
  110.4 5.6 %collective-permute-start.42 = (f32[8,64,128]{2,1,0:T(8,128)S(1)}, f32[8,64,128]{2,1,0:T(8,128)S(1)}, u32[]{:S(2)}, u32[]{:S(2)}) collective-permute-start(f32[8,64,128]{2,1,0:T(8,128)S(1)} %sweep.44.own_ref), channel_id=1, source_target_pairs={{0,1},{1,0},{2,3},{3,2},{4,5},{5,4},{6,7},{7,6},{8,9},{9,8},{10,11... | collective-permute-start | bytes 786440 | tf_op jit(solution)/shard_map/ppermute | solution.py:205
  111.3 10.3 %collective-permute-start.18 = (f32[8,64,128]{2,1,0:T(8,128)S(1)}, f32[8,64,128]{2,1,0:T(8,128)S(1)}, u32[]{:S(2)}, u32[]{:S(2)}) collective-permute-start(f32[8,64,128]{2,1,0:T(8,128)S(1)} %sweep.32.own_ref), channel_id=1, source_target_pairs={{0,31},{1,2},{2,1},{3,4},{4,3},{5,6},{6,5},{7,8},{8,7},{9,10},{10,... | collective-permute-start | bytes 786440 | tf_op jit(solution)/shard_map/ppermute | solution.py:204
  116.0 5.6 %collective-permute-start.19 = (f32[8,64,128]{2,1,0:T(8,128)S(1)}, f32[8,64,128]{2,1,0:T(8,128)S(1)}, u32[]{:S(2)}, u32[]{:S(2)}) collective-permute-start(f32[8,64,128]{2,1,0:T(8,128)S(1)} %sweep.32.own_ref), channel_id=1, source_target_pairs={{0,1},{1,0},{2,3},{3,2},{4,5},{5,4},{6,7},{7,6},{8,9},{9,8},{10,11... | collective-permute-start | bytes 786440 | tf_op jit(solution)/shard_map/ppermute | solution.py:205
  116.9 10.3 %collective-permute-start.43 = (f32[8,64,128]{2,1,0:T(8,128)S(1)}, f32[8,64,128]{2,1,0:T(8,128)S(1)}, u32[]{:S(2)}, u32[]{:S(2)}) collective-permute-start(f32[8,64,128]{2,1,0:T(8,128)S(1)} %sweep.45.own_ref), channel_id=1, source_target_pairs={{0,31},{1,2},{2,1},{3,4},{4,3},{5,6},{6,5},{7,8},{8,7},{9,10},{10,... | collective-permute-start | bytes 786440 | tf_op jit(solution)/shard_map/ppermute | solution.py:204
  121.6 5.6 %collective-permute-start.44 = (f32[8,64,128]{2,1,0:T(8,128)S(1)}, f32[8,64,128]{2,1,0:T(8,128)S(1)}, u32[]{:S(2)}, u32[]{:S(2)}) collective-permute-start(f32[8,64,128]{2,1,0:T(8,128)S(1)} %sweep.45.own_ref), channel_id=1, source_target_pairs={{0,1},{1,0},{2,3},{3,2},{4,5},{5,4},{6,7},{7,6},{8,9},{9,8},{10,11... | collective-permute-start | bytes 786440 | tf_op jit(solution)/shard_map/ppermute | solution.py:205
  122.5 10.3 %collective-permute-start.20 = (f32[8,64,128]{2,1,0:T(8,128)S(1)}, f32[8,64,128]{2,1,0:T(8,128)S(1)}, u32[]{:S(2)}, u32[]{:S(2)}) collective-permute-start(f32[8,64,128]{2,1,0:T(8,128)S(1)} %sweep.33.own_ref), channel_id=1, source_target_pairs={{0,31},{1,2},{2,1},{3,4},{4,3},{5,6},{6,5},{7,8},{8,7},{9,10},{10,... | collective-permute-start | bytes 786440 | tf_op jit(solution)/shard_map/ppermute | solution.py:204
  127.2 5.6 %collective-permute-start.21 = (f32[8,64,128]{2,1,0:T(8,128)S(1)}, f32[8,64,128]{2,1,0:T(8,128)S(1)}, u32[]{:S(2)}, u32[]{:S(2)}) collective-permute-start(f32[8,64,128]{2,1,0:T(8,128)S(1)} %sweep.33.own_ref), channel_id=1, source_target_pairs={{0,1},{1,0},{2,3},{3,2},{4,5},{5,4},{6,7},{7,6},{8,9},{9,8},{10,11... | collective-permute-start | bytes 786440 | tf_op jit(solution)/shard_map/ppermute | solution.py:205
  128.1 10.3 %collective-permute-start.45 = (f32[8,64,128]{2,1,0:T(8,128)S(1)}, f32[8,64,128]{2,1,0:T(8,128)S(1)}, u32[]{:S(2)}, u32[]{:S(2)}) collective-permute-start(f32[8,64,128]{2,1,0:T(8,128)S(1)} %sweep.46.own_ref), channel_id=1, source_target_pairs={{0,31},{1,2},{2,1},{3,4},{4,3},{5,6},{6,5},{7,8},{8,7},{9,10},{10,... | collective-permute-start | bytes 786440 | tf_op jit(solution)/shard_map/ppermute | solution.py:204
  132.9 5.6 %collective-permute-start.46 = (f32[8,64,128]{2,1,0:T(8,128)S(1)}, f32[8,64,128]{2,1,0:T(8,128)S(1)}, u32[]{:S(2)}, u32[]{:S(2)}) collective-permute-start(f32[8,64,128]{2,1,0:T(8,128)S(1)} %sweep.46.own_ref), channel_id=1, source_target_pairs={{0,1},{1,0},{2,3},{3,2},{4,5},{5,4},{6,7},{7,6},{8,9},{9,8},{10,11... | collective-permute-start | bytes 786440 | tf_op jit(solution)/shard_map/ppermute | solution.py:205
  133.8 9.5 %collective-permute-start.22 = (f32[8,64,128]{2,1,0:T(8,128)S(1)}, f32[8,64,128]{2,1,0:T(8,128)S(1)}, u32[]{:S(2)}, u32[]{:S(2)}) collective-permute-start(f32[8,64,128]{2,1,0:T(8,128)S(1)} %sweep.34.own_ref), channel_id=1, source_target_pairs={{0,31},{1,2},{2,1},{3,4},{4,3},{5,6},{6,5},{7,8},{8,7},{9,10},{10,... | collective-permute-start | bytes 786440 | tf_op jit(solution)/shard_map/ppermute | solution.py:204
  138.5 4.7 %collective-permute-start.23 = (f32[8,64,128]{2,1,0:T(8,128)S(1)}, f32[8,64,128]{2,1,0:T(8,128)S(1)}, u32[]{:S(2)}, u32[]{:S(2)}) collective-permute-start(f32[8,64,128]{2,1,0:T(8,128)S(1)} %sweep.34.own_ref), channel_id=1, source_target_pairs={{0,1},{1,0},{2,3},{3,2},{4,5},{5,4},{6,7},{7,6},{8,9},{9,8},{10,11... | collective-permute-start | bytes 786440 | tf_op jit(solution)/shard_map/ppermute | solution.py:205
  139.4 4.8 %collective-permute-start.48 = (f32[8,64,128]{2,1,0:T(8,128)S(1)}, f32[8,64,128]{2,1,0:T(8,128)S(1)}, u32[]{:S(2)}, u32[]{:S(2)}) collective-permute-start(f32[8,64,128]{2,1,0:T(8,128)S(1)} %sweep.47.refs_1_), channel_id=1, source_target_pairs={{0,1},{1,0},{2,3},{3,2},{4,5},{5,4},{6,7},{7,6},{8,9},{9,8},{10,11... | collective-permute-start | bytes 786440 | tf_op jit(solution)/shard_map/ppermute | solution.py:205
  144.1 1.6 %collective-permute-start.47 = (f32[8,64,128]{2,1,0:T(8,128)S(1)}, f32[8,64,128]{2,1,0:T(8,128)S(1)}, u32[]{:S(2)}, u32[]{:S(2)}) collective-permute-start(f32[8,64,128]{2,1,0:T(8,128)S(1)} %sweep.35.refs_0_), channel_id=1, source_target_pairs={{0,1},{1,0},{2,3},{3,2},{4,5},{5,4},{6,7},{7,6},{8,9},{9,8},{10,11... | collective-permute-start | bytes 786440 | tf_op jit(solution)/shard_map/ppermute | solution.py:205

commit v3 on v2

--- a/solution.py
+++ b/solution.py
@@ -1,5 +1,3 @@
-import functools
-
 import jax
 import jax.numpy as jnp
 from jax import lax
@@ -9,6 +7,7 @@
 
 SWEEPS = 12
 CHUNKS = 2
+UNIT = 16
 AXES = ("states", "act")
 VMEM = pltpu.VMEM
 SMEM = pltpu.SMEM
@@ -35,13 +34,15 @@
 
 
 def turn_targets(held_ref, out_refs):
-    blocks, width, lanes = out_refs[0].shape
+    blocks, _, lanes = out_refs[0].shape
     one = unit(held_ref.shape[1])
     for b in range(blocks):
         hit = held_ref[b * lanes : (b + 1) * lanes, :].astype(jnp.float32).astype(jnp.bfloat16)
         turned = times_turned(one, hit)
-        for c, out_ref in enumerate(out_refs):
-            out_ref[b] = turned[c * width : (c + 1) * width, :]
+        at = 0
+        for out_ref in out_refs:
+            out_ref[b] = turned[at : at + out_ref.shape[1]]
+            at += out_ref.shape[1]
 
 
 def half_of(ref, part):
@@ -49,11 +50,16 @@
     return ref.at[pl.ds(pl.multiple_of(part * rows, rows), rows)]
 
 
-def own_kernel(targets_ref, *refs):
-    out_refs, (held_ref, sem) = refs[:CHUNKS], refs[CHUNKS:]
-    copy = pltpu.make_async_copy(half_of(targets_ref, lax.axis_index("act")), held_ref, sem)
-    copy.start()
-    copy.wait()
+def own_kernel(targets_ref, columns_ref, columns_out_ref, *refs):
+    out_refs, (held_ref, sems) = refs[:CHUNKS], refs[CHUNKS:]
+    copies = [
+        pltpu.make_async_copy(half_of(targets_ref, lax.axis_index("act")), held_ref, sems.at[0]),
+        pltpu.make_async_copy(columns_ref, columns_out_ref, sems.at[1]),
+    ]
+    for copy in copies:
+        copy.start()
+    for copy in copies:
+        copy.wait()
     turn_targets(held_ref, out_refs)
 
 
@@ -123,7 +129,7 @@
 
 def finish_kernel(*refs):
     own_refs, sib_refs, (out_ref, held_ref, sems) = refs[:CHUNKS], refs[CHUNKS : 2 * CHUNKS], refs[2 * CHUNKS :]
-    blocks, width, lanes = own_refs[0].shape
+    blocks, _, lanes = own_refs[0].shape
     core = lax.axis_index("act")
     one = unit(lanes, 3)
     copies = []
@@ -142,27 +148,28 @@
 def per_device(transitions, columns, targets):
     acts_here, row_blocks, _, lanes, _ = transitions.shape
     sets = targets.shape[1]
-    width = sets // CHUNKS
+    widths = [min(UNIT * -(-sets // (UNIT * CHUNKS)), sets - c * UNIT * -(-sets // (UNIT * CHUNKS))) for c in range(CHUNKS)]
     blocks = row_blocks // 2
     devices = 2 * lax.axis_size("states")
 
     to_sib = [(i, i ^ 1) for i in range(devices)]
     to_ici = [(i, (i + 1) % devices if i % 2 else (i - 1) % devices) for i in range(devices)]
-    chunk = jax.ShapeDtypeStruct((blocks, width, lanes), jnp.float32)
+    chunks = [jax.ShapeDtypeStruct((blocks, width, lanes), jnp.float32) for width in widths]
 
     taken = lax.ppermute(transitions, AXES, to_sib)
 
     panel = pltpu.VMEM((blocks * lanes, sets), jnp.int32)
     targets = pltpu.with_memory_space_constraint(targets, HBM)
-    zero = pl.pallas_call(
+    columns = columns.transpose(0, 2, 1)
+    columns, *zero = pl.pallas_call(
         own_kernel,
-        out_shape=[chunk] * CHUNKS,
-        in_specs=[ANYWHERE],
-        out_specs=[WHOLE] * CHUNKS,
-        scratch_shapes=[panel, pltpu.SemaphoreType.DMA],
+        out_shape=[SMEM(columns.shape, jnp.int32)] + chunks,
+        in_specs=[ANYWHERE] * 2,
+        out_specs=[SCALARS] + [WHOLE] * CHUNKS,
+        scratch_shapes=[panel, pltpu.SemaphoreType.DMA((2,))],
         name="own_targets",
         compiler_params=pltpu.CompilerParams(vmem_limit_bytes=4 << 20),
-    )(targets)
+    )(targets, pltpu.with_memory_space_constraint(columns, HBM))
     ici = [lax.ppermute(v, AXES, to_ici) for v in zero]
 
     slots, right, *sib = pl.pallas_call(
@@ -171,19 +178,20 @@
             SMEM((2 * acts_here * blocks * 2,), jnp.int32),
             jax.ShapeDtypeStruct((blocks, 2 * acts_here, 2 * lanes, 2 * lanes), jnp.bfloat16),
         ]
-        + [chunk] * CHUNKS,
+        + chunks,
         in_specs=[SCALARS, ANYWHERE, ANYWHERE, WHOLE],
         out_specs=[SCALARS] + [WHOLE] * (1 + CHUNKS),
         scratch_shapes=[panel, pltpu.VMEM((acts_here, blocks, 2, lanes, lanes), jnp.float32), pltpu.SemaphoreType.DMA((2,))],
         name="rest",
         compiler_params=pltpu.CompilerParams(vmem_limit_bytes=16 << 20),
-    )(columns.transpose(0, 2, 1), targets, pltpu.with_memory_space_constraint(transitions, HBM), taken)
+    )(pltpu.with_memory_space_constraint(columns, SMEM), targets, pltpu.with_memory_space_constraint(transitions, HBM), taken)
     slots = pltpu.with_memory_space_constraint(slots, SMEM)
 
     def sweep(own, sib, ici, zero):
+        width = own.shape[1]
         return pl.pallas_call(
             sweep_kernel,
-            out_shape=chunk,
+            out_shape=jax.ShapeDtypeStruct(own.shape, jnp.float32),
             in_specs=[SCALARS] + [WHOLE] * 5,
             out_specs=WHOLE,
             scratch_shapes=[pltpu.VMEM((3 * blocks, 2 * width, lanes), jnp.bfloat16)],
@@ -203,6 +211,9 @@
             if step < SWEEPS - 1:
                 ici[c] = lax.ppermute(own[c], AXES, to_ici)
             sib[c] = lax.ppermute(own[c], AXES, to_sib)
+            if step < SWEEPS - 1 or c < CHUNKS - 1:
+                n = (c + 1) % CHUNKS
+                ici[n], sib[c] = lax.optimization_barrier((ici[n], sib[c]))
 
     return pl.pallas_call(
         finish_kernel,

time: 148 us -> 147 us (level)
  starting transfers between devices: 112 us -> 114 us
  Pallas kernels: 28.4 us -> 26.5 us
    ppermute x24, starting transfers between devices: 0.99 us -> 14.9 us  [per_device(): sib[c] = lax.ppermute(own[c], AXES, to_sib)]
    ppermute x22, starting transfers between devices: 104 us -> 92 us  [per_device(): ici[c] = lax.ppermute(own[c], AXES, to_ici)]
  transfers between devices with their start and end apart: 49 -> 49, of which waited for: 3 -> 3; matrix products, arithmetic and copies ran while one was open for 0% -> 0% of each run, Pallas kernels for 18% -> 16%
where the time goes in v3:
time: 147 us
  starting transfers between devices  114 us (78%)
  Pallas kernels  26.5 us (18%)
  waiting for transfers between devices  6.16 us (4%)
    ppermute x22, starting transfers between devices, per_device(): ici[c] = lax.ppermute(own[c], AXES, to_ici)  92 us
    pallas_call x24, Pallas kernels, sweep(): pl.pallas_call(sweep_kernel, out_shape=jax.ShapeDtypeStruct(own.shape, jn...  20.1 us
    ppermute x24, starting transfers between devices, per_device(): sib[c] = lax.ppermute(own[c], AXES, to_sib)  14.9 us
    ppermute x2, starting transfers between devices, per_device(): ici = [lax.ppermute(v, AXES, to_ici) for v in zero]  6.73 us
    ppermute x22, waiting for transfers between devices, per_device(): ici[c] = lax.ppermute(own[c], AXES, to_ici)  3.94 us
    pallas_call x1, Pallas kernels, per_device(): pl.pallas_call(rest_kernel, out_shape=[SMEM((2 * acts_here * blocks * 2,)...  3.44 us
  transfers between devices with their start and end apart: 49, of which 3 were waited for; matrix products, arithmetic and copies ran while one was open for 0% of the time, Pallas kernels for 16%

profile of v3, /device:TPU:0, one launch (start us, length us, event | category | flops | bytes accessed | tf_op | source)
XLA Modules:
  0.0 147.2 jit_solution(2485770954530402347)
XLA Ops:
  0.5 1.4 own_targets.1
  1.8 6.7 %collective-permute-start.1 = (f32[8,64,128]{2,1,0:T(8,128)S(1)}, f32[8,64,128]{2,1,0:T(8,128)S(1)}, u32[]{:S(2)}, u32[]{:S(2)}) collective-permute-start(f32[8,64,128]{2,1,0:T(8,128)S(1)} %get-tuple-element.61.own_ref.target_ref), channel_id=1, source_target_pairs={{0,31},{1,2},{2,1},{3,4},{4,3},{5,6},{6,5},{7,8},{8,7},{9,10},{10,... | collective-permute-start | bytes 786440 | tf_op jit(solution)/shard_map/ppermute | solution.py:173
  8.6 3.4 %rest.1 = (s32[64]{0:T(128)S(4)}, bf16[8,4,256,256]{3,2,1,0:T(8,128)(2,1)S(1)}, f32[8,64,128]{2,1,0:T(8,128)S(1)}, f32[8,64,128]{2,1,0:T(8,128)S(1)}) custom-call(s32[4,2,16]{2,1,0:T(2,128)S(4)} %get-tuple-element.58.columns_ref, s32[2048,128]{1,0:T(8,128)} %targets_ref.3, f32[2,16,2,128,128]{4,3,2,1,0:T(8,128)} %tiles_ref.1, ...), custom_call_target="tpu_custom_call" | custom-call | tf_op jit(solution)/shard_map/rest/pallas_call | solution.py:175
  12.7 0.8 sweep.24.own_ref
  13.6 6.0 %collective-permute-start.2 = (f32[8,64,128]{2,1,0:T(8,128)S(1)}, f32[8,64,128]{2,1,0:T(8,128)S(1)}, u32[]{:S(2)}, u32[]{:S(2)}) collective-permute-start(f32[8,64,128]{2,1,0:T(8,128)S(1)} %sweep.24.own_ref), channel_id=1, source_target_pairs={{0,31},{1,2},{2,1},{3,4},{4,3},{5,6},{6,5},{7,8},{8,7},{9,10},{10,... | collective-permute-start | bytes 786440 | tf_op jit(solution)/shard_map/ppermute | solution.py:212
  19.6 0.8 sweep.25.own_ref
  20.5 4.7 %collective-permute-start.7 = (f32[8,64,128]{2,1,0:T(8,128)S(1)}, f32[8,64,128]{2,1,0:T(8,128)S(1)}, u32[]{:S(2)}, u32[]{:S(2)}) collective-permute-start(f32[8,64,128]{2,1,0:T(8,128)S(1)} %sweep.25.own_ref), channel_id=1, source_target_pairs={{0,31},{1,2},{2,1},{3,4},{4,3},{5,6},{6,5},{7,8},{8,7},{9,10},{10,... | collective-permute-start | bytes 786440 | tf_op jit(solution)/shard_map/ppermute | solution.py:212
  25.2 0.8 sweep.26.own_ref
  26.7 4.1 %collective-permute-start.6 = (f32[8,64,128]{2,1,0:T(8,128)S(1)}, f32[8,64,128]{2,1,0:T(8,128)S(1)}, u32[]{:S(2)}, u32[]{:S(2)}) collective-permute-start(f32[8,64,128]{2,1,0:T(8,128)S(1)} %sweep.26.own_ref), channel_id=1, source_target_pairs={{0,31},{1,2},{2,1},{3,4},{4,3},{5,6},{6,5},{7,8},{8,7},{9,10},{10,... | collective-permute-start | bytes 786440 | tf_op jit(solution)/shard_map/ppermute | solution.py:212
  30.8 0.8 sweep.27.own_ref
  31.6 0.7 collective-permute-start.9
  32.4 4.1 %collective-permute-start.11 = (f32[8,64,128]{2,1,0:T(8,128)S(1)}, f32[8,64,128]{2,1,0:T(8,128)S(1)}, u32[]{:S(2)}, u32[]{:S(2)}) collective-permute-start(f32[8,64,128]{2,1,0:T(8,128)S(1)} %sweep.27.own_ref), channel_id=1, source_target_pairs={{0,31},{1,2},{2,1},{3,4},{4,3},{5,6},{6,5},{7,8},{8,7},{9,10},{10,... | collective-permute-start | bytes 786440 | tf_op jit(solution)/shard_map/ppermute | solution.py:212
  36.4 0.8 sweep.28.own_ref
  37.3 0.7 collective-permute-start.12
  38.0 4.1 %collective-permute-start.10 = (f32[8,64,128]{2,1,0:T(8,128)S(1)}, f32[8,64,128]{2,1,0:T(8,128)S(1)}, u32[]{:S(2)}, u32[]{:S(2)}) collective-permute-start(f32[8,64,128]{2,1,0:T(8,128)S(1)} %sweep.28.own_ref), channel_id=1, source_target_pairs={{0,31},{1,2},{2,1},{3,4},{4,3},{5,6},{6,5},{7,8},{8,7},{9,10},{10,... | collective-permute-start | bytes 786440 | tf_op jit(solution)/shard_map/ppermute | solution.py:212
  42.0 0.8 sweep.29.own_ref
  42.9 0.7 collective-permute-start.13
  43.6 4.1 %collective-permute-start.15 = (f32[8,64,128]{2,1,0:T(8,128)S(1)}, f32[8,64,128]{2,1,0:T(8,128)S(1)}, u32[]{:S(2)}, u32[]{:S(2)}) collective-permute-start(f32[8,64,128]{2,1,0:T(8,128)S(1)} %sweep.29.own_ref), channel_id=1, source_target_pairs={{0,31},{1,2},{2,1},{3,4},{4,3},{5,6},{6,5},{7,8},{8,7},{9,10},{10,... | collective-permute-start | bytes 786440 | tf_op jit(solution)/shard_map/ppermute | solution.py:212
  47.7 0.8 sweep.30.own_ref
  48.5 0.7 collective-permute-start.16
  49.2 4.1 %collective-permute-start.14 = (f32[8,64,128]{2,1,0:T(8,128)S(1)}, f32[8,64,128]{2,1,0:T(8,128)S(1)}, u32[]{:S(2)}, u32[]{:S(2)}) collective-permute-start(f32[8,64,128]{2,1,0:T(8,128)S(1)} %sweep.30.own_ref), channel_id=1, source_target_pairs={{0,31},{1,2},{2,1},{3,4},{4,3},{5,6},{6,5},{7,8},{8,7},{9,10},{10,... | collective-permute-start | bytes 786440 | tf_op jit(solution)/shard_map/ppermute | solution.py:212
  53.3 0.8 sweep.31.own_ref
  54.8 4.1 %collective-permute-start.19 = (f32[8,64,128]{2,1,0:T(8,128)S(1)}, f32[8,64,128]{2,1,0:T(8,128)S(1)}, u32[]{:S(2)}, u32[]{:S(2)}) collective-permute-start(f32[8,64,128]{2,1,0:T(8,128)S(1)} %sweep.31.own_ref), channel_id=1, source_target_pairs={{0,31},{1,2},{2,1},{3,4},{4,3},{5,6},{6,5},{7,8},{8,7},{9,10},{10,... | collective-permute-start | bytes 786440 | tf_op jit(solution)/shard_map/ppermute | solution.py:212
  58.9 0.8 sweep.32.own_ref
  59.7 0.7 collective-permute-start.20
  60.4 4.1 %collective-permute-start.18 = (f32[8,64,128]{2,1,0:T(8,128)S(1)}, f32[8,64,128]{2,1,0:T(8,128)S(1)}, u32[]{:S(2)}, u32[]{:S(2)}) collective-permute-start(f32[8,64,128]{2,1,0:T(8,128)S(1)} %sweep.32.own_ref), channel_id=1, source_target_pairs={{0,31},{1,2},{2,1},{3,4},{4,3},{5,6},{6,5},{7,8},{8,7},{9,10},{10,... | collective-permute-start | bytes 786440 | tf_op jit(solution)/shard_map/ppermute | solution.py:212
  64.5 0.8 sweep.33.own_ref
  66.1 4.1 %collective-permute-start.23 = (f32[8,64,128]{2,1,0:T(8,128)S(1)}, f32[8,64,128]{2,1,0:T(8,128)S(1)}, u32[]{:S(2)}, u32[]{:S(2)}) collective-permute-start(f32[8,64,128]{2,1,0:T(8,128)S(1)} %sweep.33.own_ref), channel_id=1, source_target_pairs={{0,31},{1,2},{2,1},{3,4},{4,3},{5,6},{6,5},{7,8},{8,7},{9,10},{10,... | collective-permute-start | bytes 786440 | tf_op jit(solution)/shard_map/ppermute | solution.py:212
  70.1 1.0 sweep.34.own_ref
  71.9 4.1 %collective-permute-start.22 = (f32[8,64,128]{2,1,0:T(8,128)S(1)}, f32[8,64,128]{2,1,0:T(8,128)S(1)}, u32[]{:S(2)}, u32[]{:S(2)}) collective-permute-start(f32[8,64,128]{2,1,0:T(8,128)S(1)} %sweep.34.own_ref), channel_id=1, source_target_pairs={{0,31},{1,2},{2,1},{3,4},{4,3},{5,6},{6,5},{7,8},{8,7},{9,10},{10,... | collective-permute-start | bytes 786440 | tf_op jit(solution)/shard_map/ppermute | solution.py:212
  75.9 0.8 sweep.35.own_ref
  77.3 4.1 %collective-permute-start.27 = (f32[8,64,128]{2,1,0:T(8,128)S(1)}, f32[8,64,128]{2,1,0:T(8,128)S(1)}, u32[]{:S(2)}, u32[]{:S(2)}) collective-permute-start(f32[8,64,128]{2,1,0:T(8,128)S(1)} %sweep.35.own_ref), channel_id=1, source_target_pairs={{0,31},{1,2},{2,1},{3,4},{4,3},{5,6},{6,5},{7,8},{8,7},{9,10},{10,... | collective-permute-start | bytes 786440 | tf_op jit(solution)/shard_map/ppermute | solution.py:212
  81.4 0.8 sweep.36.own_ref
  82.2 0.7 collective-permute-start.28
  82.9 4.1 %collective-permute-start.26 = (f32[8,64,128]{2,1,0:T(8,128)S(1)}, f32[8,64,128]{2,1,0:T(8,128)S(1)}, u32[]{:S(2)}, u32[]{:S(2)}) collective-permute-start(f32[8,64,128]{2,1,0:T(8,128)S(1)} %sweep.36.own_ref), channel_id=1, source_target_pairs={{0,31},{1,2},{2,1},{3,4},{4,3},{5,6},{6,5},{7,8},{8,7},{9,10},{10,... | collective-permute-start | bytes 786440 | tf_op jit(solution)/shard_map/ppermute | solution.py:212
  87.0 0.8 sweep.37.own_ref
  87.8 0.7 collective-permute-start.29
  88.5 4.1 %collective-permute-start.31 = (f32[8,64,128]{2,1,0:T(8,128)S(1)}, f32[8,64,128]{2,1,0:T(8,128)S(1)}, u32[]{:S(2)}, u32[]{:S(2)}) collective-permute-start(f32[8,64,128]{2,1,0:T(8,128)S(1)} %sweep.37.own_ref), channel_id=1, source_target_pairs={{0,31},{1,2},{2,1},{3,4},{4,3},{5,6},{6,5},{7,8},{8,7},{9,10},{10,... | collective-permute-start | bytes 786440 | tf_op jit(solution)/shard_map/ppermute | solution.py:212
  92.6 0.8 sweep.38.own_ref
  93.4 0.7 collective-permute-start.32
  94.1 4.1 %collective-permute-start.30 = (f32[8,64,128]{2,1,0:T(8,128)S(1)}, f32[8,64,128]{2,1,0:T(8,128)S(1)}, u32[]{:S(2)}, u32[]{:S(2)}) collective-permute-start(f32[8,64,128]{2,1,0:T(8,128)S(1)} %sweep.38.own_ref), channel_id=1, source_target_pairs={{0,31},{1,2},{2,1},{3,4},{4,3},{5,6},{6,5},{7,8},{8,7},{9,10},{10,... | collective-permute-start | bytes 786440 | tf_op jit(solution)/shard_map/ppermute | solution.py:212
  98.2 0.8 sweep.39.own_ref
  99.0 0.7 collective-permute-start.33
  99.8 4.1 %collective-permute-start.35 = (f32[8,64,128]{2,1,0:T(8,128)S(1)}, f32[8,64,128]{2,1,0:T(8,128)S(1)}, u32[]{:S(2)}, u32[]{:S(2)}) collective-permute-start(f32[8,64,128]{2,1,0:T(8,128)S(1)} %sweep.39.own_ref), channel_id=1, source_target_pairs={{0,31},{1,2},{2,1},{3,4},{4,3},{5,6},{6,5},{7,8},{8,7},{9,10},{10,... | collective-permute-start | bytes 786440 | tf_op jit(solution)/shard_map/ppermute | solution.py:212
  103.8 0.8 sweep.40.own_ref
  104.7 0.7 collective-permute-start.36
  105.4 4.1 %collective-permute-start.34 = (f32[8,64,128]{2,1,0:T(8,128)S(1)}, f32[8,64,128]{2,1,0:T(8,128)S(1)}, u32[]{:S(2)}, u32[]{:S(2)}) collective-permute-start(f32[8,64,128]{2,1,0:T(8,128)S(1)} %sweep.40.own_ref), channel_id=1, source_target_pairs={{0,31},{1,2},{2,1},{3,4},{4,3},{5,6},{6,5},{7,8},{8,7},{9,10},{10,... | collective-permute-start | bytes 786440 | tf_op jit(solution)/shard_map/ppermute | solution.py:212
  109.5 0.8 sweep.41.own_ref
  111.0 4.1 %collective-permute-start.39 = (f32[8,64,128]{2,1,0:T(8,128)S(1)}, f32[8,64,128]{2,1,0:T(8,128)S(1)}, u32[]{:S(2)}, u32[]{:S(2)}) collective-permute-start(f32[8,64,128]{2,1,0:T(8,128)S(1)} %sweep.41.own_ref), channel_id=1, source_target_pairs={{0,31},{1,2},{2,1},{3,4},{4,3},{5,6},{6,5},{7,8},{8,7},{9,10},{10,... | collective-permute-start | bytes 786440 | tf_op jit(solution)/shard_map/ppermute | solution.py:212
  115.1 0.8 sweep.42.own_ref
  115.9 0.7 collective-permute-start.40
  116.6 4.1 %collective-permute-start.38 = (f32[8,64,128]{2,1,0:T(8,128)S(1)}, f32[8,64,128]{2,1,0:T(8,128)S(1)}, u32[]{:S(2)}, u32[]{:S(2)}) collective-permute-start(f32[8,64,128]{2,1,0:T(8,128)S(1)} %sweep.42.own_ref), channel_id=1, source_target_pairs={{0,31},{1,2},{2,1},{3,4},{4,3},{5,6},{6,5},{7,8},{8,7},{9,10},{10,... | collective-permute-start | bytes 786440 | tf_op jit(solution)/shard_map/ppermute | solution.py:212
  120.7 0.8 sweep.43.own_ref
  122.2 4.1 %collective-permute-start.43 = (f32[8,64,128]{2,1,0:T(8,128)S(1)}, f32[8,64,128]{2,1,0:T(8,128)S(1)}, u32[]{:S(2)}, u32[]{:S(2)}) collective-permute-start(f32[8,64,128]{2,1,0:T(8,128)S(1)} %sweep.43.own_ref), channel_id=1, source_target_pairs={{0,31},{1,2},{2,1},{3,4},{4,3},{5,6},{6,5},{7,8},{8,7},{9,10},{10,... | collective-permute-start | bytes 786440 | tf_op jit(solution)/shard_map/ppermute | solution.py:212
  126.3 0.8 sweep.44.own_ref
  127.9 4.1 %collective-permute-start.42 = (f32[8,64,128]{2,1,0:T(8,128)S(1)}, f32[8,64,128]{2,1,0:T(8,128)S(1)}, u32[]{:S(2)}, u32[]{:S(2)}) collective-permute-start(f32[8,64,128]{2,1,0:T(8,128)S(1)} %sweep.44.own_ref), channel_id=1, source_target_pairs={{0,31},{1,2},{2,1},{3,4},{4,3},{5,6},{6,5},{7,8},{8,7},{9,10},{10,... | collective-permute-start | bytes 786440 | tf_op jit(solution)/shard_map/ppermute | solution.py:212
  131.9 0.8 sweep.45.own_ref
  132.8 0.7 collective-permute-start.45
  133.5 4.1 %collective-permute-start.46 = (f32[8,64,128]{2,1,0:T(8,128)S(1)}, f32[8,64,128]{2,1,0:T(8,128)S(1)}, u32[]{:S(2)}, u32[]{:S(2)}) collective-permute-start(f32[8,64,128]{2,1,0:T(8,128)S(1)} %sweep.45.own_ref), channel_id=1, source_target_pairs={{0,31},{1,2},{2,1},{3,4},{4,3},{5,6},{6,5},{7,8},{8,7},{9,10},{10,... | collective-permute-start | bytes 786440 | tf_op jit(solution)/shard_map/ppermute | solution.py:212
  137.5 0.8 sweep.46.refs_0_
  139.1 3.9 %collective-permute-done.46.ici_ref = f32[8,64,128]{2,1,0:T(8,128)S(1)} collective-permute-done((f32[8,64,128]{2,1,0:T(8,128)S(1)}, f32[8,64,128]{2,1,0:T(8,128)S(1)}, u32[]{:S(2)}, u32[]{:S(2)}) %collective-permute-start.46) | collective-permute-done | bytes 262176 | tf_op jit(solution)/shard_map/ppermute | solution.py:212
  143.0 0.8 sweep.47.refs_1_
  143.9 1.5 %collective-permute-done.48.refs_3_ = f32[8,64,128]{2,1,0:T(8,128)S(1)} collective-permute-done((f32[8,64,128]{2,1,0:T(8,128)S(1)}, f32[8,64,128]{2,1,0:T(8,128)S(1)}, u32[]{:S(2)}, u32[]{:S(2)}) %collective-permute-start.48) | collective-permute-done | bytes 262176 | tf_op jit(solution)/shard_map/ppermute | solution.py:213
  145.4 1.6 %finish.1 = f32[2048,128]{1,0:T(8,128)} custom-call(f32[8,64,128]{2,1,0:T(8,128)S(1)} %sweep.46.refs_0_, f32[8,64,128]{2,1,0:T(8,128)S(1)} %sweep.47.refs_1_, f32[8,64,128]{2,1,0:T(8,128)S(1)} %collective-permute-done.47.refs_2_, f32[8,64,128]{2,1,0:T(8,128)S(1)} %collective-permute-done.48.refs_3_), custom_call_target="tpu_custom_call" | custom-call | tf_op jit(solution)/shard_map/finish/pallas_call | solution.py:218
  (61 shorter events, 7.7 us)
Async XLA Ops:
  0.0 8.6 %collective-permute-start = (f32[2,16,2,128,128]{4,3,2,1,0:T(8,128)}, f32[2,16,2,128,128]{4,3,2,1,0:T(8,128)S(1)}, u32[]{:S(2)}, u32[]{:S(2)}) collective-permute-start(f32[2,16,2,128,128]{4,3,2,1,0:T(8,128)} %tiles_ref.1), channel_id=1, source_target_pairs={{0,1},{1,0},{2,3},{3,2},{4,5},{5,4},{6,7},{7,6},{8,9},{9,8},{10,11... | collective-permute-start | bytes 12582920 | tf_op jit(solution)/shard_map/ppermute | solution.py:159
  1.8 10.8 %collective-permute-start.1 = (f32[8,64,128]{2,1,0:T(8,128)S(1)}, f32[8,64,128]{2,1,0:T(8,128)S(1)}, u32[]{:S(2)}, u32[]{:S(2)}) collective-permute-start(f32[8,64,128]{2,1,0:T(8,128)S(1)} %get-tuple-element.61.own_ref.target_ref), channel_id=1, source_target_pairs={{0,31},{1,2},{2,1},{3,4},{4,3},{5,6},{6,5},{7,8},{8,7},{9,10},{10,... | collective-permute-start | bytes 786440 | tf_op jit(solution)/shard_map/ppermute | solution.py:173
  8.5 11.1 %collective-permute-start.3 = (f32[8,64,128]{2,1,0:T(8,128)S(1)}, f32[8,64,128]{2,1,0:T(8,128)S(1)}, u32[]{:S(2)}, u32[]{:S(2)}) collective-permute-start(f32[8,64,128]{2,1,0:T(8,128)S(1)} %get-tuple-element.63.own_ref.target_ref), channel_id=1, source_target_pairs={{0,31},{1,2},{2,1},{3,4},{4,3},{5,6},{6,5},{7,8},{8,7},{9,10},{10,... | collective-permute-start | bytes 786440 | tf_op jit(solution)/shard_map/ppermute | solution.py:173
  13.5 6.1 %collective-permute-start.4 = (f32[8,64,128]{2,1,0:T(8,128)S(1)}, f32[8,64,128]{2,1,0:T(8,128)S(1)}, u32[]{:S(2)}, u32[]{:S(2)}) collective-permute-start(f32[8,64,128]{2,1,0:T(8,128)S(1)} %sweep.24.own_ref), channel_id=1, source_target_pairs={{0,1},{1,0},{2,3},{3,2},{4,5},{5,4},{6,7},{7,6},{8,9},{9,8},{10,11... | collective-permute-start | bytes 786440 | tf_op jit(solution)/shard_map/ppermute | solution.py:213
  13.6 11.6 %collective-permute-start.2 = (f32[8,64,128]{2,1,0:T(8,128)S(1)}, f32[8,64,128]{2,1,0:T(8,128)S(1)}, u32[]{:S(2)}, u32[]{:S(2)}) collective-permute-start(f32[8,64,128]{2,1,0:T(8,128)S(1)} %sweep.24.own_ref), channel_id=1, source_target_pairs={{0,31},{1,2},{2,1},{3,4},{4,3},{5,6},{6,5},{7,8},{8,7},{9,10},{10,... | collective-permute-start | bytes 786440 | tf_op jit(solution)/shard_map/ppermute | solution.py:212
  20.4 4.8 %collective-permute-start.5 = (f32[8,64,128]{2,1,0:T(8,128)S(1)}, f32[8,64,128]{2,1,0:T(8,128)S(1)}, u32[]{:S(2)}, u32[]{:S(2)}) collective-permute-start(f32[8,64,128]{2,1,0:T(8,128)S(1)} %sweep.25.own_ref), channel_id=1, source_target_pairs={{0,1},{1,0},{2,3},{3,2},{4,5},{5,4},{6,7},{7,6},{8,9},{9,8},{10,11... | collective-permute-start | bytes 786440 | tf_op jit(solution)/shard_map/ppermute | solution.py:213
  20.5 10.3 %collective-permute-start.7 = (f32[8,64,128]{2,1,0:T(8,128)S(1)}, f32[8,64,128]{2,1,0:T(8,128)S(1)}, u32[]{:S(2)}, u32[]{:S(2)}) collective-permute-start(f32[8,64,128]{2,1,0:T(8,128)S(1)} %sweep.25.own_ref), channel_id=1, source_target_pairs={{0,31},{1,2},{2,1},{3,4},{4,3},{5,6},{6,5},{7,8},{8,7},{9,10},{10,... | collective-permute-start | bytes 786440 | tf_op jit(solution)/shard_map/ppermute | solution.py:212
  26.1 4.7 %collective-permute-start.8 = (f32[8,64,128]{2,1,0:T(8,128)S(1)}, f32[8,64,128]{2,1,0:T(8,128)S(1)}, u32[]{:S(2)}, u32[]{:S(2)}) collective-permute-start(f32[8,64,128]{2,1,0:T(8,128)S(1)} %sweep.26.own_ref), channel_id=1, source_target_pairs={{0,1},{1,0},{2,3},{3,2},{4,5},{5,4},{6,7},{7,6},{8,9},{9,8},{10,11... | collective-permute-start | bytes 786440 | tf_op jit(solution)/shard_map/ppermute | solution.py:213
  26.7 9.7 %collective-permute-start.6 = (f32[8,64,128]{2,1,0:T(8,128)S(1)}, f32[8,64,128]{2,1,0:T(8,128)S(1)}, u32[]{:S(2)}, u32[]{:S(2)}) collective-permute-start(f32[8,64,128]{2,1,0:T(8,128)S(1)} %sweep.26.own_ref), channel_id=1, source_target_pairs={{0,31},{1,2},{2,1},{3,4},{4,3},{5,6},{6,5},{7,8},{8,7},{9,10},{10,... | collective-permute-start | bytes 786440 | tf_op jit(solution)/shard_map/ppermute | solution.py:212
  31.6 4.8 %collective-permute-start.9 = (f32[8,64,128]{2,1,0:T(8,128)S(1)}, f32[8,64,128]{2,1,0:T(8,128)S(1)}, u32[]{:S(2)}, u32[]{:S(2)}) collective-permute-start(f32[8,64,128]{2,1,0:T(8,128)S(1)} %sweep.27.own_ref), channel_id=1, source_target_pairs={{0,1},{1,0},{2,3},{3,2},{4,5},{5,4},{6,7},{7,6},{8,9},{9,8},{10,11... | collective-permute-start | bytes 786440 | tf_op jit(solution)/shard_map/ppermute | solution.py:213
  32.4 9.7 %collective-permute-start.11 = (f32[8,64,128]{2,1,0:T(8,128)S(1)}, f32[8,64,128]{2,1,0:T(8,128)S(1)}, u32[]{:S(2)}, u32[]{:S(2)}) collective-permute-start(f32[8,64,128]{2,1,0:T(8,128)S(1)} %sweep.27.own_ref), channel_id=1, source_target_pairs={{0,31},{1,2},{2,1},{3,4},{4,3},{5,6},{6,5},{7,8},{8,7},{9,10},{10,... | collective-permute-start | bytes 786440 | tf_op jit(solution)/shard_map/ppermute | solution.py:212
  37.3 4.8 %collective-permute-start.12 = (f32[8,64,128]{2,1,0:T(8,128)S(1)}, f32[8,64,128]{2,1,0:T(8,128)S(1)}, u32[]{:S(2)}, u32[]{:S(2)}) collective-permute-start(f32[8,64,128]{2,1,0:T(8,128)S(1)} %sweep.28.own_ref), channel_id=1, source_target_pairs={{0,1},{1,0},{2,3},{3,2},{4,5},{5,4},{6,7},{7,6},{8,9},{9,8},{10,11... | collective-permute-start | bytes 786440 | tf_op jit(solution)/shard_map/ppermute | solution.py:213
  38.0 9.7 %collective-permute-start.10 = (f32[8,64,128]{2,1,0:T(8,128)S(1)}, f32[8,64,128]{2,1,0:T(8,128)S(1)}, u32[]{:S(2)}, u32[]{:S(2)}) collective-permute-start(f32[8,64,128]{2,1,0:T(8,128)S(1)} %sweep.28.own_ref), channel_id=1, source_target_pairs={{0,31},{1,2},{2,1},{3,4},{4,3},{5,6},{6,5},{7,8},{8,7},{9,10},{10,... | collective-permute-start | bytes 786440 | tf_op jit(solution)/shard_map/ppermute | solution.py:212
  42.9 4.8 %collective-permute-start.13 = (f32[8,64,128]{2,1,0:T(8,128)S(1)}, f32[8,64,128]{2,1,0:T(8,128)S(1)}, u32[]{:S(2)}, u32[]{:S(2)}) collective-permute-start(f32[8,64,128]{2,1,0:T(8,128)S(1)} %sweep.29.own_ref), channel_id=1, source_target_pairs={{0,1},{1,0},{2,3},{3,2},{4,5},{5,4},{6,7},{7,6},{8,9},{9,8},{10,11... | collective-permute-start | bytes 786440 | tf_op jit(solution)/shard_map/ppermute | solution.py:213
  43.6 9.7 %collective-permute-start.15 = (f32[8,64,128]{2,1,0:T(8,128)S(1)}, f32[8,64,128]{2,1,0:T(8,128)S(1)}, u32[]{:S(2)}, u32[]{:S(2)}) collective-permute-start(f32[8,64,128]{2,1,0:T(8,128)S(1)} %sweep.29.own_ref), channel_id=1, source_target_pairs={{0,31},{1,2},{2,1},{3,4},{4,3},{5,6},{6,5},{7,8},{8,7},{9,10},{10,... | collective-permute-start | bytes 786440 | tf_op jit(solution)/shard_map/ppermute | solution.py:212
  48.5 4.8 %collective-permute-start.16 = (f32[8,64,128]{2,1,0:T(8,128)S(1)}, f32[8,64,128]{2,1,0:T(8,128)S(1)}, u32[]{:S(2)}, u32[]{:S(2)}) collective-permute-start(f32[8,64,128]{2,1,0:T(8,128)S(1)} %sweep.30.own_ref), channel_id=1, source_target_pairs={{0,1},{1,0},{2,3},{3,2},{4,5},{5,4},{6,7},{7,6},{8,9},{9,8},{10,11... | collective-permute-start | bytes 786440 | tf_op jit(solution)/shard_map/ppermute | solution.py:213
  49.2 9.7 %collective-permute-start.14 = (f32[8,64,128]{2,1,0:T(8,128)S(1)}, f32[8,64,128]{2,1,0:T(8,128)S(1)}, u32[]{:S(2)}, u32[]{:S(2)}) collective-permute-start(f32[8,64,128]{2,1,0:T(8,128)S(1)} %sweep.30.own_ref), channel_id=1, source_target_pairs={{0,31},{1,2},{2,1},{3,4},{4,3},{5,6},{6,5},{7,8},{8,7},{9,10},{10,... | collective-permute-start | bytes 786440 | tf_op jit(solution)/shard_map/ppermute | solution.py:212
  54.1 4.8 %collective-permute-start.17 = (f32[8,64,128]{2,1,0:T(8,128)S(1)}, f32[8,64,128]{2,1,0:T(8,128)S(1)}, u32[]{:S(2)}, u32[]{:S(2)}) collective-permute-start(f32[8,64,128]{2,1,0:T(8,128)S(1)} %sweep.31.own_ref), channel_id=1, source_target_pairs={{0,1},{1,0},{2,3},{3,2},{4,5},{5,4},{6,7},{7,6},{8,9},{9,8},{10,11... | collective-permute-start | bytes 786440 | tf_op jit(solution)/shard_map/ppermute | solution.py:213
  54.8 9.7 %collective-permute-start.19 = (f32[8,64,128]{2,1,0:T(8,128)S(1)}, f32[8,64,128]{2,1,0:T(8,128)S(1)}, u32[]{:S(2)}, u32[]{:S(2)}) collective-permute-start(f32[8,64,128]{2,1,0:T(8,128)S(1)} %sweep.31.own_ref), channel_id=1, source_target_pairs={{0,31},{1,2},{2,1},{3,4},{4,3},{5,6},{6,5},{7,8},{8,7},{9,10},{10,... | collective-permute-start | bytes 786440 | tf_op jit(solution)/shard_map/ppermute | solution.py:212
  59.7 4.8 %collective-permute-start.20 = (f32[8,64,128]{2,1,0:T(8,128)S(1)}, f32[8,64,128]{2,1,0:T(8,128)S(1)}, u32[]{:S(2)}, u32[]{:S(2)}) collective-permute-start(f32[8,64,128]{2,1,0:T(8,128)S(1)} %sweep.32.own_ref), channel_id=1, source_target_pairs={{0,1},{1,0},{2,3},{3,2},{4,5},{5,4},{6,7},{7,6},{8,9},{9,8},{10,11... | collective-permute-start | bytes 786440 | tf_op jit(solution)/shard_map/ppermute | solution.py:213
  60.4 9.7 %collective-permute-start.18 = (f32[8,64,128]{2,1,0:T(8,128)S(1)}, f32[8,64,128]{2,1,0:T(8,128)S(1)}, u32[]{:S(2)}, u32[]{:S(2)}) collective-permute-start(f32[8,64,128]{2,1,0:T(8,128)S(1)} %sweep.32.own_ref), channel_id=1, source_target_pairs={{0,31},{1,2},{2,1},{3,4},{4,3},{5,6},{6,5},{7,8},{8,7},{9,10},{10,... | collective-permute-start | bytes 786440 | tf_op jit(solution)/shard_map/ppermute | solution.py:212
  65.3 4.8 %collective-permute-start.21 = (f32[8,64,128]{2,1,0:T(8,128)S(1)}, f32[8,64,128]{2,1,0:T(8,128)S(1)}, u32[]{:S(2)}, u32[]{:S(2)}) collective-permute-start(f32[8,64,128]{2,1,0:T(8,128)S(1)} %sweep.33.own_ref), channel_id=1, source_target_pairs={{0,1},{1,0},{2,3},{3,2},{4,5},{5,4},{6,7},{7,6},{8,9},{9,8},{10,11... | collective-permute-start | bytes 786440 | tf_op jit(solution)/shard_map/ppermute | solution.py:213
  66.1 9.9 %collective-permute-start.23 = (f32[8,64,128]{2,1,0:T(8,128)S(1)}, f32[8,64,128]{2,1,0:T(8,128)S(1)}, u32[]{:S(2)}, u32[]{:S(2)}) collective-permute-start(f32[8,64,128]{2,1,0:T(8,128)S(1)} %sweep.33.own_ref), channel_id=1, source_target_pairs={{0,31},{1,2},{2,1},{3,4},{4,3},{5,6},{6,5},{7,8},{8,7},{9,10},{10,... | collective-permute-start | bytes 786440 | tf_op jit(solution)/shard_map/ppermute | solution.py:212
  71.1 4.8 %collective-permute-start.24 = (f32[8,64,128]{2,1,0:T(8,128)S(1)}, f32[8,64,128]{2,1,0:T(8,128)S(1)}, u32[]{:S(2)}, u32[]{:S(2)}) collective-permute-start(f32[8,64,128]{2,1,0:T(8,128)S(1)} %sweep.34.own_ref), channel_id=1, source_target_pairs={{0,1},{1,0},{2,3},{3,2},{4,5},{5,4},{6,7},{7,6},{8,9},{9,8},{10,11... | collective-permute-start | bytes 786440 | tf_op jit(solution)/shard_map/ppermute | solution.py:213
  71.9 9.5 %collective-permute-start.22 = (f32[8,64,128]{2,1,0:T(8,128)S(1)}, f32[8,64,128]{2,1,0:T(8,128)S(1)}, u32[]{:S(2)}, u32[]{:S(2)}) collective-permute-start(f32[8,64,128]{2,1,0:T(8,128)S(1)} %sweep.34.own_ref), channel_id=1, source_target_pairs={{0,31},{1,2},{2,1},{3,4},{4,3},{5,6},{6,5},{7,8},{8,7},{9,10},{10,... | collective-permute-start | bytes 786440 | tf_op jit(solution)/shard_map/ppermute | solution.py:212
  76.8 4.6 %collective-permute-start.25 = (f32[8,64,128]{2,1,0:T(8,128)S(1)}, f32[8,64,128]{2,1,0:T(8,128)S(1)}, u32[]{:S(2)}, u32[]{:S(2)}) collective-permute-start(f32[8,64,128]{2,1,0:T(8,128)S(1)} %sweep.35.own_ref), channel_id=1, source_target_pairs={{0,1},{1,0},{2,3},{3,2},{4,5},{5,4},{6,7},{7,6},{8,9},{9,8},{10,11... | collective-permute-start | bytes 786440 | tf_op jit(solution)/shard_map/ppermute | solution.py:213
  77.3 9.7 %collective-permute-start.27 = (f32[8,64,128]{2,1,0:T(8,128)S(1)}, f32[8,64,128]{2,1,0:T(8,128)S(1)}, u32[]{:S(2)}, u32[]{:S(2)}) collective-permute-start(f32[8,64,128]{2,1,0:T(8,128)S(1)} %sweep.35.own_ref), channel_id=1, source_target_pairs={{0,31},{1,2},{2,1},{3,4},{4,3},{5,6},{6,5},{7,8},{8,7},{9,10},{10,... | collective-permute-start | bytes 786440 | tf_op jit(solution)/shard_map/ppermute | solution.py:212
  82.2 4.8 %collective-permute-start.28 = (f32[8,64,128]{2,1,0:T(8,128)S(1)}, f32[8,64,128]{2,1,0:T(8,128)S(1)}, u32[]{:S(2)}, u32[]{:S(2)}) collective-permute-start(f32[8,64,128]{2,1,0:T(8,128)S(1)} %sweep.36.own_ref), channel_id=1, source_target_pairs={{0,1},{1,0},{2,3},{3,2},{4,5},{5,4},{6,7},{7,6},{8,9},{9,8},{10,11... | collective-permute-start | bytes 786440 | tf_op jit(solution)/shard_map/ppermute | solution.py:213
  82.9 9.7 %collective-permute-start.26 = (f32[8,64,128]{2,1,0:T(8,128)S(1)}, f32[8,64,128]{2,1,0:T(8,128)S(1)}, u32[]{:S(2)}, u32[]{:S(2)}) collective-permute-start(f32[8,64,128]{2,1,0:T(8,128)S(1)} %sweep.36.own_ref), channel_id=1, source_target_pairs={{0,31},{1,2},{2,1},{3,4},{4,3},{5,6},{6,5},{7,8},{8,7},{9,10},{10,... | collective-permute-start | bytes 786440 | tf_op jit(solution)/shard_map/ppermute | solution.py:212
  87.8 4.8 %collective-permute-start.29 = (f32[8,64,128]{2,1,0:T(8,128)S(1)}, f32[8,64,128]{2,1,0:T(8,128)S(1)}, u32[]{:S(2)}, u32[]{:S(2)}) collective-permute-start(f32[8,64,128]{2,1,0:T(8,128)S(1)} %sweep.37.own_ref), channel_id=1, source_target_pairs={{0,1},{1,0},{2,3},{3,2},{4,5},{5,4},{6,7},{7,6},{8,9},{9,8},{10,11... | collective-permute-start | bytes 786440 | tf_op jit(solution)/shard_map/ppermute | solution.py:213
  88.5 9.7 %collective-permute-start.31 = (f32[8,64,128]{2,1,0:T(8,128)S(1)}, f32[8,64,128]{2,1,0:T(8,128)S(1)}, u32[]{:S(2)}, u32[]{:S(2)}) collective-permute-start(f32[8,64,128]{2,1,0:T(8,128)S(1)} %sweep.37.own_ref), channel_id=1, source_target_pairs={{0,31},{1,2},{2,1},{3,4},{4,3},{5,6},{6,5},{7,8},{8,7},{9,10},{10,... | collective-permute-start | bytes 786440 | tf_op jit(solution)/shard_map/ppermute | solution.py:212
  93.4 4.8 %collective-permute-start.32 = (f32[8,64,128]{2,1,0:T(8,128)S(1)}, f32[8,64,128]{2,1,0:T(8,128)S(1)}, u32[]{:S(2)}, u32[]{:S(2)}) collective-permute-start(f32[8,64,128]{2,1,0:T(8,128)S(1)} %sweep.38.own_ref), channel_id=1, source_target_pairs={{0,1},{1,0},{2,3},{3,2},{4,5},{5,4},{6,7},{7,6},{8,9},{9,8},{10,11... | collective-permute-start | bytes 786440 | tf_op jit(solution)/shard_map/ppermute | solution.py:213
  94.1 9.7 %collective-permute-start.30 = (f32[8,64,128]{2,1,0:T(8,128)S(1)}, f32[8,64,128]{2,1,0:T(8,128)S(1)}, u32[]{:S(2)}, u32[]{:S(2)}) collective-permute-start(f32[8,64,128]{2,1,0:T(8,128)S(1)} %sweep.38.own_ref), channel_id=1, source_target_pairs={{0,31},{1,2},{2,1},{3,4},{4,3},{5,6},{6,5},{7,8},{8,7},{9,10},{10,... | collective-permute-start | bytes 786440 | tf_op jit(solution)/shard_map/ppermute | solution.py:212
  99.0 4.8 %collective-permute-start.33 = (f32[8,64,128]{2,1,0:T(8,128)S(1)}, f32[8,64,128]{2,1,0:T(8,128)S(1)}, u32[]{:S(2)}, u32[]{:S(2)}) collective-permute-start(f32[8,64,128]{2,1,0:T(8,128)S(1)} %sweep.39.own_ref), channel_id=1, source_target_pairs={{0,1},{1,0},{2,3},{3,2},{4,5},{5,4},{6,7},{7,6},{8,9},{9,8},{10,11... | collective-permute-start | bytes 786440 | tf_op jit(solution)/shard_map/ppermute | solution.py:213
  99.8 9.7 %collective-permute-start.35 = (f32[8,64,128]{2,1,0:T(8,128)S(1)}, f32[8,64,128]{2,1,0:T(8,128)S(1)}, u32[]{:S(2)}, u32[]{:S(2)}) collective-permute-start(f32[8,64,128]{2,1,0:T(8,128)S(1)} %sweep.39.own_ref), channel_id=1, source_target_pairs={{0,31},{1,2},{2,1},{3,4},{4,3},{5,6},{6,5},{7,8},{8,7},{9,10},{10,... | collective-permute-start | bytes 786440 | tf_op jit(solution)/shard_map/ppermute | solution.py:212
  104.7 4.8 %collective-permute-start.36 = (f32[8,64,128]{2,1,0:T(8,128)S(1)}, f32[8,64,128]{2,1,0:T(8,128)S(1)}, u32[]{:S(2)}, u32[]{:S(2)}) collective-permute-start(f32[8,64,128]{2,1,0:T(8,128)S(1)} %sweep.40.own_ref), channel_id=1, source_target_pairs={{0,1},{1,0},{2,3},{3,2},{4,5},{5,4},{6,7},{7,6},{8,9},{9,8},{10,11... | collective-permute-start | bytes 786440 | tf_op jit(solution)/shard_map/ppermute | solution.py:213
  105.4 9.7 %collective-permute-start.34 = (f32[8,64,128]{2,1,0:T(8,128)S(1)}, f32[8,64,128]{2,1,0:T(8,128)S(1)}, u32[]{:S(2)}, u32[]{:S(2)}) collective-permute-start(f32[8,64,128]{2,1,0:T(8,128)S(1)} %sweep.40.own_ref), channel_id=1, source_target_pairs={{0,31},{1,2},{2,1},{3,4},{4,3},{5,6},{6,5},{7,8},{8,7},{9,10},{10,... | collective-permute-start | bytes 786440 | tf_op jit(solution)/shard_map/ppermute | solution.py:212
  110.3 4.8 %collective-permute-start.37 = (f32[8,64,128]{2,1,0:T(8,128)S(1)}, f32[8,64,128]{2,1,0:T(8,128)S(1)}, u32[]{:S(2)}, u32[]{:S(2)}) collective-permute-start(f32[8,64,128]{2,1,0:T(8,128)S(1)} %sweep.41.own_ref), channel_id=1, source_target_pairs={{0,1},{1,0},{2,3},{3,2},{4,5},{5,4},{6,7},{7,6},{8,9},{9,8},{10,11... | collective-permute-start | bytes 786440 | tf_op jit(solution)/shard_map/ppermute | solution.py:213
  111.0 9.7 %collective-permute-start.39 = (f32[8,64,128]{2,1,0:T(8,128)S(1)}, f32[8,64,128]{2,1,0:T(8,128)S(1)}, u32[]{:S(2)}, u32[]{:S(2)}) collective-permute-start(f32[8,64,128]{2,1,0:T(8,128)S(1)} %sweep.41.own_ref), channel_id=1, source_target_pairs={{0,31},{1,2},{2,1},{3,4},{4,3},{5,6},{6,5},{7,8},{8,7},{9,10},{10,... | collective-permute-start | bytes 786440 | tf_op jit(solution)/shard_map/ppermute | solution.py:212
  115.9 4.8 %collective-permute-start.40 = (f32[8,64,128]{2,1,0:T(8,128)S(1)}, f32[8,64,128]{2,1,0:T(8,128)S(1)}, u32[]{:S(2)}, u32[]{:S(2)}) collective-permute-start(f32[8,64,128]{2,1,0:T(8,128)S(1)} %sweep.42.own_ref), channel_id=1, source_target_pairs={{0,1},{1,0},{2,3},{3,2},{4,5},{5,4},{6,7},{7,6},{8,9},{9,8},{10,11... | collective-permute-start | bytes 786440 | tf_op jit(solution)/shard_map/ppermute | solution.py:213
  116.6 9.7 %collective-permute-start.38 = (f32[8,64,128]{2,1,0:T(8,128)S(1)}, f32[8,64,128]{2,1,0:T(8,128)S(1)}, u32[]{:S(2)}, u32[]{:S(2)}) collective-permute-start(f32[8,64,128]{2,1,0:T(8,128)S(1)} %sweep.42.own_ref), channel_id=1, source_target_pairs={{0,31},{1,2},{2,1},{3,4},{4,3},{5,6},{6,5},{7,8},{8,7},{9,10},{10,... | collective-permute-start | bytes 786440 | tf_op jit(solution)/shard_map/ppermute | solution.py:212
  121.5 4.8 %collective-permute-start.41 = (f32[8,64,128]{2,1,0:T(8,128)S(1)}, f32[8,64,128]{2,1,0:T(8,128)S(1)}, u32[]{:S(2)}, u32[]{:S(2)}) collective-permute-start(f32[8,64,128]{2,1,0:T(8,128)S(1)} %sweep.43.own_ref), channel_id=1, source_target_pairs={{0,1},{1,0},{2,3},{3,2},{4,5},{5,4},{6,7},{7,6},{8,9},{9,8},{10,11... | collective-permute-start | bytes 786440 | tf_op jit(solution)/shard_map/ppermute | solution.py:213
  122.2 9.7 %collective-permute-start.43 = (f32[8,64,128]{2,1,0:T(8,128)S(1)}, f32[8,64,128]{2,1,0:T(8,128)S(1)}, u32[]{:S(2)}, u32[]{:S(2)}) collective-permute-start(f32[8,64,128]{2,1,0:T(8,128)S(1)} %sweep.43.own_ref), channel_id=1, source_target_pairs={{0,31},{1,2},{2,1},{3,4},{4,3},{5,6},{6,5},{7,8},{8,7},{9,10},{10,... | collective-permute-start | bytes 786440 | tf_op jit(solution)/shard_map/ppermute | solution.py:212
  127.1 4.8 %collective-permute-start.44 = (f32[8,64,128]{2,1,0:T(8,128)S(1)}, f32[8,64,128]{2,1,0:T(8,128)S(1)}, u32[]{:S(2)}, u32[]{:S(2)}) collective-permute-start(f32[8,64,128]{2,1,0:T(8,128)S(1)} %sweep.44.own_ref), channel_id=1, source_target_pairs={{0,1},{1,0},{2,3},{3,2},{4,5},{5,4},{6,7},{7,6},{8,9},{9,8},{10,11... | collective-permute-start | bytes 786440 | tf_op jit(solution)/shard_map/ppermute | solution.py:213
  127.9 9.7 %collective-permute-start.42 = (f32[8,64,128]{2,1,0:T(8,128)S(1)}, f32[8,64,128]{2,1,0:T(8,128)S(1)}, u32[]{:S(2)}, u32[]{:S(2)}) collective-permute-start(f32[8,64,128]{2,1,0:T(8,128)S(1)} %sweep.44.own_ref), channel_id=1, source_target_pairs={{0,31},{1,2},{2,1},{3,4},{4,3},{5,6},{6,5},{7,8},{8,7},{9,10},{10,... | collective-permute-start | bytes 786440 | tf_op jit(solution)/shard_map/ppermute | solution.py:212
  132.8 4.8 %collective-permute-start.45 = (f32[8,64,128]{2,1,0:T(8,128)S(1)}, f32[8,64,128]{2,1,0:T(8,128)S(1)}, u32[]{:S(2)}, u32[]{:S(2)}) collective-permute-start(f32[8,64,128]{2,1,0:T(8,128)S(1)} %sweep.45.own_ref), channel_id=1, source_target_pairs={{0,1},{1,0},{2,3},{3,2},{4,5},{5,4},{6,7},{7,6},{8,9},{9,8},{10,11... | collective-permute-start | bytes 786440 | tf_op jit(solution)/shard_map/ppermute | solution.py:213
  133.5 9.5 %collective-permute-start.46 = (f32[8,64,128]{2,1,0:T(8,128)S(1)}, f32[8,64,128]{2,1,0:T(8,128)S(1)}, u32[]{:S(2)}, u32[]{:S(2)}) collective-permute-start(f32[8,64,128]{2,1,0:T(8,128)S(1)} %sweep.45.own_ref), channel_id=1, source_target_pairs={{0,31},{1,2},{2,1},{3,4},{4,3},{5,6},{6,5},{7,8},{8,7},{9,10},{10,... | collective-permute-start | bytes 786440 | tf_op jit(solution)/shard_map/ppermute | solution.py:212
  138.4 4.6 %collective-permute-start.47 = (f32[8,64,128]{2,1,0:T(8,128)S(1)}, f32[8,64,128]{2,1,0:T(8,128)S(1)}, u32[]{:S(2)}, u32[]{:S(2)}) collective-permute-start(f32[8,64,128]{2,1,0:T(8,128)S(1)} %sweep.46.refs_0_), channel_id=1, source_target_pairs={{0,1},{1,0},{2,3},{3,2},{4,5},{5,4},{6,7},{7,6},{8,9},{9,8},{10,11... | collective-permute-start | bytes 786440 | tf_op jit(solution)/shard_map/ppermute | solution.py:213
  143.8 1.6 %collective-permute-start.48 = (f32[8,64,128]{2,1,0:T(8,128)S(1)}, f32[8,64,128]{2,1,0:T(8,128)S(1)}, u32[]{:S(2)}, u32[]{:S(2)}) collective-permute-start(f32[8,64,128]{2,1,0:T(8,128)S(1)} %sweep.47.refs_1_), channel_id=1, source_target_pairs={{0,1},{1,0},{2,3},{3,2},{4,5},{5,4},{6,7},{7,6},{8,9},{9,8},{10,11... | collective-permute-start | bytes 786440 | tf_op jit(solution)/shard_map/ppermute | solution.py:213

commit v4 on v3

--- a/solution.py
+++ b/solution.py
@@ -1,3 +1,5 @@
+import functools
+
 import jax
 import jax.numpy as jnp
 from jax import lax
@@ -127,22 +129,19 @@
         out_ref[b] = jnp.where(target_ref[b] == 1.0, 1.0, largest)
 
 
-def finish_kernel(*refs):
-    own_refs, sib_refs, (out_ref, held_ref, sems) = refs[:CHUNKS], refs[CHUNKS : 2 * CHUNKS], refs[2 * CHUNKS :]
-    blocks, _, lanes = own_refs[0].shape
+def finish_kernel(other, *refs):
+    chunk_refs, (out_ref, held_ref, sem) = refs[:CHUNKS], refs[-3:]
+    blocks, _, lanes = chunk_refs[0].shape
     core = lax.axis_index("act")
     one = unit(lanes, 3)
-    copies = []
-    for n, (part, group) in enumerate(((core, own_refs), (1 - core, sib_refs))):
-        for b in range(blocks):
-            panel = jnp.concatenate([ref[b] for ref in group], axis=0)
-            high = panel.astype(jnp.bfloat16)
-            middle, low = split(panel - high.astype(jnp.float32))
-            held_ref[n, b * lanes : (b + 1) * lanes] = times_turned(one, jnp.concatenate([high, middle, low], axis=1))
-        copies.append(pltpu.make_async_copy(held_ref.at[n], half_of(out_ref, part), sems.at[n]))
-        copies[-1].start()
-    for copy in copies:
-        copy.wait()
+    for b in range(blocks):
+        panel = jnp.concatenate([ref[b] for ref in chunk_refs], axis=0)
+        high = panel.astype(jnp.bfloat16)
+        middle, low = split(panel - high.astype(jnp.float32))
+        held_ref[b * lanes : (b + 1) * lanes] = times_turned(one, jnp.concatenate([high, middle, low], axis=1))
+    copy = pltpu.make_async_copy(held_ref, half_of(out_ref, 1 - core if other else core), sem)
+    copy.start()
+    copy.wait()
 
 
 def per_device(transitions, columns, targets):
@@ -215,15 +214,19 @@
                 n = (c + 1) % CHUNKS
                 ici[n], sib[c] = lax.optimization_barrier((ici[n], sib[c]))
 
-    return pl.pallas_call(
-        finish_kernel,
-        out_shape=jax.ShapeDtypeStruct((2 * blocks * lanes, sets), jnp.float32),
-        in_specs=[WHOLE] * (2 * CHUNKS),
-        out_specs=ANYWHERE,
-        scratch_shapes=[pltpu.VMEM((2, blocks * lanes, sets), jnp.float32), pltpu.SemaphoreType.DMA((2,))],
-        name="finish",
-        compiler_params=pltpu.CompilerParams(vmem_limit_bytes=8 << 20),
-    )(*own, *sib)
+    def finish(other, chunks, *half):
+        return pl.pallas_call(
+            functools.partial(finish_kernel, other),
+            out_shape=jax.ShapeDtypeStruct((2 * blocks * lanes, sets), jnp.float32),
+            in_specs=[WHOLE] * CHUNKS + [ANYWHERE] * len(half),
+            out_specs=ANYWHERE,
+            scratch_shapes=[pltpu.VMEM((blocks * lanes, sets), jnp.float32), pltpu.SemaphoreType.DMA],
+            input_output_aliases={CHUNKS: 0} if half else {},
+            name="finish",
+            compiler_params=pltpu.CompilerParams(vmem_limit_bytes=8 << 20),
+        )(*chunks, *half)
+
+    return finish(True, sib, finish(False, own))
 
 
 def solution(mesh):

time: 147 us -> 147 us (level)
  transfers between devices with their start and end apart: 49 -> 49, of which waited for: 3 -> 3; matrix products, arithmetic and copies ran while one was open for 0% -> 0% of each run, Pallas kernels for 16% -> 17%
where the time goes in v4:
time: 147 us
  starting transfers between devices  114 us (78%)
  Pallas kernels  27.5 us (19%)
  waiting for transfers between devices  4.87 us (3%)
    ppermute x22, starting transfers between devices, per_device(): ici[c] = lax.ppermute(own[c], AXES, to_ici)  92 us
    pallas_call x24, Pallas kernels, sweep(): pl.pallas_call(sweep_kernel, out_shape=jax.ShapeDtypeStruct(own.shape, jn...  20.1 us
    ppermute x24, starting transfers between devices, per_device(): sib[c] = lax.ppermute(own[c], AXES, to_sib)  14.9 us
    ppermute x2, starting transfers between devices, per_device(): ici = [lax.ppermute(v, AXES, to_ici) for v in zero]  6.73 us
    ppermute x22, waiting for transfers between devices, per_device(): ici[c] = lax.ppermute(own[c], AXES, to_ici)  3.94 us
    pallas_call x1, Pallas kernels, per_device(): pl.pallas_call(rest_kernel, out_shape=[SMEM((2 * acts_here * blocks * 2,)...  3.44 us
  transfers between devices with their start and end apart: 49, of which 3 were waited for; matrix products, arithmetic and copies ran while one was open for 0% of the time, Pallas kernels for 17%

profile of v4, /device:TPU:0, one launch (start us, length us, event | category | flops | bytes accessed | tf_op | source)
XLA Modules:
  0.0 146.8 jit_solution(15911683537735145824)
XLA Ops:
  0.5 1.4 own_targets.1
  1.8 6.7 %collective-permute-start.2 = (f32[8,64,128]{2,1,0:T(8,128)S(1)}, f32[8,64,128]{2,1,0:T(8,128)S(1)}, u32[]{:S(2)}, u32[]{:S(2)}) collective-permute-start(f32[8,64,128]{2,1,0:T(8,128)S(1)} %get-tuple-element.62.own_ref.target_ref), channel_id=1, source_target_pairs={{0,31},{1,2},{2,1},{3,4},{4,3},{5,6},{6,5},{7,8},{8,7},{9,10},{10,... | collective-permute-start | bytes 786440 | tf_op jit(solution)/shard_map/ppermute | solution.py:172
  8.6 3.4 %rest.1 = (s32[64]{0:T(128)S(4)}, bf16[8,4,256,256]{3,2,1,0:T(8,128)(2,1)S(1)}, f32[8,64,128]{2,1,0:T(8,128)S(1)}, f32[8,64,128]{2,1,0:T(8,128)S(1)}) custom-call(s32[4,2,16]{2,1,0:T(2,128)S(4)} %get-tuple-element.58.columns_ref, s32[2048,128]{1,0:T(8,128)} %targets_ref.3, f32[2,16,2,128,128]{4,3,2,1,0:T(8,128)} %tiles_ref.1, ...), custom_call_target="tpu_custom_call" | custom-call | tf_op jit(solution)/shard_map/rest/pallas_call | solution.py:174
  12.7 0.8 sweep.24.own_ref
  13.6 6.0 %collective-permute-start.5 = (f32[8,64,128]{2,1,0:T(8,128)S(1)}, f32[8,64,128]{2,1,0:T(8,128)S(1)}, u32[]{:S(2)}, u32[]{:S(2)}) collective-permute-start(f32[8,64,128]{2,1,0:T(8,128)S(1)} %sweep.24.own_ref), channel_id=1, source_target_pairs={{0,31},{1,2},{2,1},{3,4},{4,3},{5,6},{6,5},{7,8},{8,7},{9,10},{10,... | collective-permute-start | bytes 786440 | tf_op jit(solution)/shard_map/ppermute | solution.py:211
  19.6 0.8 sweep.25.own_ref
  20.5 4.7 %collective-permute-start.4 = (f32[8,64,128]{2,1,0:T(8,128)S(1)}, f32[8,64,128]{2,1,0:T(8,128)S(1)}, u32[]{:S(2)}, u32[]{:S(2)}) collective-permute-start(f32[8,64,128]{2,1,0:T(8,128)S(1)} %sweep.25.own_ref), channel_id=1, source_target_pairs={{0,31},{1,2},{2,1},{3,4},{4,3},{5,6},{6,5},{7,8},{8,7},{9,10},{10,... | collective-permute-start | bytes 786440 | tf_op jit(solution)/shard_map/ppermute | solution.py:211
  25.2 0.8 sweep.26.own_ref
  26.7 4.1 %collective-permute-start.9 = (f32[8,64,128]{2,1,0:T(8,128)S(1)}, f32[8,64,128]{2,1,0:T(8,128)S(1)}, u32[]{:S(2)}, u32[]{:S(2)}) collective-permute-start(f32[8,64,128]{2,1,0:T(8,128)S(1)} %sweep.26.own_ref), channel_id=1, source_target_pairs={{0,31},{1,2},{2,1},{3,4},{4,3},{5,6},{6,5},{7,8},{8,7},{9,10},{10,... | collective-permute-start | bytes 786440 | tf_op jit(solution)/shard_map/ppermute | solution.py:211
  30.8 0.8 sweep.27.own_ref
  31.6 0.7 collective-permute-start.10
  32.4 4.1 %collective-permute-start.8 = (f32[8,64,128]{2,1,0:T(8,128)S(1)}, f32[8,64,128]{2,1,0:T(8,128)S(1)}, u32[]{:S(2)}, u32[]{:S(2)}) collective-permute-start(f32[8,64,128]{2,1,0:T(8,128)S(1)} %sweep.27.own_ref), channel_id=1, source_target_pairs={{0,31},{1,2},{2,1},{3,4},{4,3},{5,6},{6,5},{7,8},{8,7},{9,10},{10,... | collective-permute-start | bytes 786440 | tf_op jit(solution)/shard_map/ppermute | solution.py:211
  36.4 0.8 sweep.28.own_ref
  37.3 0.7 collective-permute-start.11
  38.0 4.1 %collective-permute-start.13 = (f32[8,64,128]{2,1,0:T(8,128)S(1)}, f32[8,64,128]{2,1,0:T(8,128)S(1)}, u32[]{:S(2)}, u32[]{:S(2)}) collective-permute-start(f32[8,64,128]{2,1,0:T(8,128)S(1)} %sweep.28.own_ref), channel_id=1, source_target_pairs={{0,31},{1,2},{2,1},{3,4},{4,3},{5,6},{6,5},{7,8},{8,7},{9,10},{10,... | collective-permute-start | bytes 786440 | tf_op jit(solution)/shard_map/ppermute | solution.py:211
  42.0 0.8 sweep.29.own_ref
  42.9 0.7 collective-permute-start.14
  43.6 4.1 %collective-permute-start.12 = (f32[8,64,128]{2,1,0:T(8,128)S(1)}, f32[8,64,128]{2,1,0:T(8,128)S(1)}, u32[]{:S(2)}, u32[]{:S(2)}) collective-permute-start(f32[8,64,128]{2,1,0:T(8,128)S(1)} %sweep.29.own_ref), channel_id=1, source_target_pairs={{0,31},{1,2},{2,1},{3,4},{4,3},{5,6},{6,5},{7,8},{8,7},{9,10},{10,... | collective-permute-start | bytes 786440 | tf_op jit(solution)/shard_map/ppermute | solution.py:211
  47.7 0.8 sweep.30.own_ref
  48.5 0.7 collective-permute-start.15
  49.2 4.1 %collective-permute-start.17 = (f32[8,64,128]{2,1,0:T(8,128)S(1)}, f32[8,64,128]{2,1,0:T(8,128)S(1)}, u32[]{:S(2)}, u32[]{:S(2)}) collective-permute-start(f32[8,64,128]{2,1,0:T(8,128)S(1)} %sweep.30.own_ref), channel_id=1, source_target_pairs={{0,31},{1,2},{2,1},{3,4},{4,3},{5,6},{6,5},{7,8},{8,7},{9,10},{10,... | collective-permute-start | bytes 786440 | tf_op jit(solution)/shard_map/ppermute | solution.py:211
  53.3 0.8 sweep.31.own_ref
  54.8 4.1 %collective-permute-start.16 = (f32[8,64,128]{2,1,0:T(8,128)S(1)}, f32[8,64,128]{2,1,0:T(8,128)S(1)}, u32[]{:S(2)}, u32[]{:S(2)}) collective-permute-start(f32[8,64,128]{2,1,0:T(8,128)S(1)} %sweep.31.own_ref), channel_id=1, source_target_pairs={{0,31},{1,2},{2,1},{3,4},{4,3},{5,6},{6,5},{7,8},{8,7},{9,10},{10,... | collective-permute-start | bytes 786440 | tf_op jit(solution)/shard_map/ppermute | solution.py:211
  58.9 0.8 sweep.32.own_ref
  59.7 0.7 collective-permute-start.19
  60.4 4.1 %collective-permute-start.21 = (f32[8,64,128]{2,1,0:T(8,128)S(1)}, f32[8,64,128]{2,1,0:T(8,128)S(1)}, u32[]{:S(2)}, u32[]{:S(2)}) collective-permute-start(f32[8,64,128]{2,1,0:T(8,128)S(1)} %sweep.32.own_ref), channel_id=1, source_target_pairs={{0,31},{1,2},{2,1},{3,4},{4,3},{5,6},{6,5},{7,8},{8,7},{9,10},{10,... | collective-permute-start | bytes 786440 | tf_op jit(solution)/shard_map/ppermute | solution.py:211
  64.5 0.8 sweep.33.own_ref
  66.1 4.1 %collective-permute-start.20 = (f32[8,64,128]{2,1,0:T(8,128)S(1)}, f32[8,64,128]{2,1,0:T(8,128)S(1)}, u32[]{:S(2)}, u32[]{:S(2)}) collective-permute-start(f32[8,64,128]{2,1,0:T(8,128)S(1)} %sweep.33.own_ref), channel_id=1, source_target_pairs={{0,31},{1,2},{2,1},{3,4},{4,3},{5,6},{6,5},{7,8},{8,7},{9,10},{10,... | collective-permute-start | bytes 786440 | tf_op jit(solution)/shard_map/ppermute | solution.py:211
  70.1 1.0 sweep.34.own_ref
  71.9 4.1 %collective-permute-start.25 = (f32[8,64,128]{2,1,0:T(8,128)S(1)}, f32[8,64,128]{2,1,0:T(8,128)S(1)}, u32[]{:S(2)}, u32[]{:S(2)}) collective-permute-start(f32[8,64,128]{2,1,0:T(8,128)S(1)} %sweep.34.own_ref), channel_id=1, source_target_pairs={{0,31},{1,2},{2,1},{3,4},{4,3},{5,6},{6,5},{7,8},{8,7},{9,10},{10,... | collective-permute-start | bytes 786440 | tf_op jit(solution)/shard_map/ppermute | solution.py:211
  75.9 0.8 sweep.35.own_ref
  77.3 4.1 %collective-permute-start.24 = (f32[8,64,128]{2,1,0:T(8,128)S(1)}, f32[8,64,128]{2,1,0:T(8,128)S(1)}, u32[]{:S(2)}, u32[]{:S(2)}) collective-permute-start(f32[8,64,128]{2,1,0:T(8,128)S(1)} %sweep.35.own_ref), channel_id=1, source_target_pairs={{0,31},{1,2},{2,1},{3,4},{4,3},{5,6},{6,5},{7,8},{8,7},{9,10},{10,... | collective-permute-start | bytes 786440 | tf_op jit(solution)/shard_map/ppermute | solution.py:211
  81.4 0.8 sweep.36.own_ref
  82.2 0.7 collective-permute-start.27
  82.9 4.1 %collective-permute-start.29 = (f32[8,64,128]{2,1,0:T(8,128)S(1)}, f32[8,64,128]{2,1,0:T(8,128)S(1)}, u32[]{:S(2)}, u32[]{:S(2)}) collective-permute-start(f32[8,64,128]{2,1,0:T(8,128)S(1)} %sweep.36.own_ref), channel_id=1, source_target_pairs={{0,31},{1,2},{2,1},{3,4},{4,3},{5,6},{6,5},{7,8},{8,7},{9,10},{10,... | collective-permute-start | bytes 786440 | tf_op jit(solution)/shard_map/ppermute | solution.py:211
  87.0 0.8 sweep.37.own_ref
  87.8 0.7 collective-permute-start.30
  88.5 4.1 %collective-permute-start.28 = (f32[8,64,128]{2,1,0:T(8,128)S(1)}, f32[8,64,128]{2,1,0:T(8,128)S(1)}, u32[]{:S(2)}, u32[]{:S(2)}) collective-permute-start(f32[8,64,128]{2,1,0:T(8,128)S(1)} %sweep.37.own_ref), channel_id=1, source_target_pairs={{0,31},{1,2},{2,1},{3,4},{4,3},{5,6},{6,5},{7,8},{8,7},{9,10},{10,... | collective-permute-start | bytes 786440 | tf_op jit(solution)/shard_map/ppermute | solution.py:211
  92.6 0.8 sweep.38.own_ref
  93.4 0.7 collective-permute-start.31
  94.1 4.1 %collective-permute-start.33 = (f32[8,64,128]{2,1,0:T(8,128)S(1)}, f32[8,64,128]{2,1,0:T(8,128)S(1)}, u32[]{:S(2)}, u32[]{:S(2)}) collective-permute-start(f32[8,64,128]{2,1,0:T(8,128)S(1)} %sweep.38.own_ref), channel_id=1, source_target_pairs={{0,31},{1,2},{2,1},{3,4},{4,3},{5,6},{6,5},{7,8},{8,7},{9,10},{10,... | collective-permute-start | bytes 786440 | tf_op jit(solution)/shard_map/ppermute | solution.py:211
  98.2 0.8 sweep.39.own_ref
  99.0 0.7 collective-permute-start.34
  99.8 4.1 %collective-permute-start.32 = (f32[8,64,128]{2,1,0:T(8,128)S(1)}, f32[8,64,128]{2,1,0:T(8,128)S(1)}, u32[]{:S(2)}, u32[]{:S(2)}) collective-permute-start(f32[8,64,128]{2,1,0:T(8,128)S(1)} %sweep.39.own_ref), channel_id=1, source_target_pairs={{0,31},{1,2},{2,1},{3,4},{4,3},{5,6},{6,5},{7,8},{8,7},{9,10},{10,... | collective-permute-start | bytes 786440 | tf_op jit(solution)/shard_map/ppermute | solution.py:211
  103.8 0.8 sweep.40.own_ref
  104.7 0.7 collective-permute-start.35
  105.4 4.1 %collective-permute-start.37 = (f32[8,64,128]{2,1,0:T(8,128)S(1)}, f32[8,64,128]{2,1,0:T(8,128)S(1)}, u32[]{:S(2)}, u32[]{:S(2)}) collective-permute-start(f32[8,64,128]{2,1,0:T(8,128)S(1)} %sweep.40.own_ref), channel_id=1, source_target_pairs={{0,31},{1,2},{2,1},{3,4},{4,3},{5,6},{6,5},{7,8},{8,7},{9,10},{10,... | collective-permute-start | bytes 786440 | tf_op jit(solution)/shard_map/ppermute | solution.py:211
  109.5 0.8 sweep.41.own_ref
  111.0 4.1 %collective-permute-start.36 = (f32[8,64,128]{2,1,0:T(8,128)S(1)}, f32[8,64,128]{2,1,0:T(8,128)S(1)}, u32[]{:S(2)}, u32[]{:S(2)}) collective-permute-start(f32[8,64,128]{2,1,0:T(8,128)S(1)} %sweep.41.own_ref), channel_id=1, source_target_pairs={{0,31},{1,2},{2,1},{3,4},{4,3},{5,6},{6,5},{7,8},{8,7},{9,10},{10,... | collective-permute-start | bytes 786440 | tf_op jit(solution)/shard_map/ppermute | solution.py:211
  115.1 0.8 sweep.42.own_ref
  115.9 0.7 collective-permute-start.39
  116.6 4.1 %collective-permute-start.41 = (f32[8,64,128]{2,1,0:T(8,128)S(1)}, f32[8,64,128]{2,1,0:T(8,128)S(1)}, u32[]{:S(2)}, u32[]{:S(2)}) collective-permute-start(f32[8,64,128]{2,1,0:T(8,128)S(1)} %sweep.42.own_ref), channel_id=1, source_target_pairs={{0,31},{1,2},{2,1},{3,4},{4,3},{5,6},{6,5},{7,8},{8,7},{9,10},{10,... | collective-permute-start | bytes 786440 | tf_op jit(solution)/shard_map/ppermute | solution.py:211
  120.7 0.8 sweep.43.own_ref
  122.2 4.1 %collective-permute-start.40 = (f32[8,64,128]{2,1,0:T(8,128)S(1)}, f32[8,64,128]{2,1,0:T(8,128)S(1)}, u32[]{:S(2)}, u32[]{:S(2)}) collective-permute-start(f32[8,64,128]{2,1,0:T(8,128)S(1)} %sweep.43.own_ref), channel_id=1, source_target_pairs={{0,31},{1,2},{2,1},{3,4},{4,3},{5,6},{6,5},{7,8},{8,7},{9,10},{10,... | collective-permute-start | bytes 786440 | tf_op jit(solution)/shard_map/ppermute | solution.py:211
  126.3 0.8 sweep.44.own_ref
  127.9 4.1 %collective-permute-start.45 = (f32[8,64,128]{2,1,0:T(8,128)S(1)}, f32[8,64,128]{2,1,0:T(8,128)S(1)}, u32[]{:S(2)}, u32[]{:S(2)}) collective-permute-start(f32[8,64,128]{2,1,0:T(8,128)S(1)} %sweep.44.own_ref), channel_id=1, source_target_pairs={{0,31},{1,2},{2,1},{3,4},{4,3},{5,6},{6,5},{7,8},{8,7},{9,10},{10,... | collective-permute-start | bytes 786440 | tf_op jit(solution)/shard_map/ppermute | solution.py:211
  131.9 0.8 sweep.45.own_ref
  132.8 0.7 collective-permute-start.46
  133.5 4.1 %collective-permute-start.44 = (f32[8,64,128]{2,1,0:T(8,128)S(1)}, f32[8,64,128]{2,1,0:T(8,128)S(1)}, u32[]{:S(2)}, u32[]{:S(2)}) collective-permute-start(f32[8,64,128]{2,1,0:T(8,128)S(1)} %sweep.45.own_ref), channel_id=1, source_target_pairs={{0,31},{1,2},{2,1},{3,4},{4,3},{5,6},{6,5},{7,8},{8,7},{9,10},{10,... | collective-permute-start | bytes 786440 | tf_op jit(solution)/shard_map/ppermute | solution.py:211
  137.5 0.8 sweep.46.refs_0_
  139.1 3.9 %collective-permute-done.44.ici_ref = f32[8,64,128]{2,1,0:T(8,128)S(1)} collective-permute-done((f32[8,64,128]{2,1,0:T(8,128)S(1)}, f32[8,64,128]{2,1,0:T(8,128)S(1)}, u32[]{:S(2)}, u32[]{:S(2)}) %collective-permute-start.44) | collective-permute-done | bytes 262176 | tf_op jit(solution)/shard_map/ppermute | solution.py:211
  143.0 0.8 sweep.47.refs_1_
  143.9 1.3 finish.2.refs_2_
  145.4 1.3 finish.3
  (62 shorter events, 7.9 us)
Async XLA Ops:
  0.0 8.6 %collective-permute-start = (f32[2,16,2,128,128]{4,3,2,1,0:T(8,128)}, f32[2,16,2,128,128]{4,3,2,1,0:T(8,128)S(1)}, u32[]{:S(2)}, u32[]{:S(2)}) collective-permute-start(f32[2,16,2,128,128]{4,3,2,1,0:T(8,128)} %tiles_ref.1), channel_id=1, source_target_pairs={{0,1},{1,0},{2,3},{3,2},{4,5},{5,4},{6,7},{7,6},{8,9},{9,8},{10,11... | collective-permute-start | bytes 12582920 | tf_op jit(solution)/shard_map/ppermute | solution.py:158
  1.8 10.8 %collective-permute-start.2 = (f32[8,64,128]{2,1,0:T(8,128)S(1)}, f32[8,64,128]{2,1,0:T(8,128)S(1)}, u32[]{:S(2)}, u32[]{:S(2)}) collective-permute-start(f32[8,64,128]{2,1,0:T(8,128)S(1)} %get-tuple-element.62.own_ref.target_ref), channel_id=1, source_target_pairs={{0,31},{1,2},{2,1},{3,4},{4,3},{5,6},{6,5},{7,8},{8,7},{9,10},{10,... | collective-permute-start | bytes 786440 | tf_op jit(solution)/shard_map/ppermute | solution.py:172
  8.5 11.1 %collective-permute-start.1 = (f32[8,64,128]{2,1,0:T(8,128)S(1)}, f32[8,64,128]{2,1,0:T(8,128)S(1)}, u32[]{:S(2)}, u32[]{:S(2)}) collective-permute-start(f32[8,64,128]{2,1,0:T(8,128)S(1)} %get-tuple-element.61.own_ref.target_ref), channel_id=1, source_target_pairs={{0,31},{1,2},{2,1},{3,4},{4,3},{5,6},{6,5},{7,8},{8,7},{9,10},{10,... | collective-permute-start | bytes 786440 | tf_op jit(solution)/shard_map/ppermute | solution.py:172
  13.5 6.1 %collective-permute-start.3 = (f32[8,64,128]{2,1,0:T(8,128)S(1)}, f32[8,64,128]{2,1,0:T(8,128)S(1)}, u32[]{:S(2)}, u32[]{:S(2)}) collective-permute-start(f32[8,64,128]{2,1,0:T(8,128)S(1)} %sweep.24.own_ref), channel_id=1, source_target_pairs={{0,1},{1,0},{2,3},{3,2},{4,5},{5,4},{6,7},{7,6},{8,9},{9,8},{10,11... | collective-permute-start | bytes 786440 | tf_op jit(solution)/shard_map/ppermute | solution.py:212
  13.6 11.6 %collective-permute-start.5 = (f32[8,64,128]{2,1,0:T(8,128)S(1)}, f32[8,64,128]{2,1,0:T(8,128)S(1)}, u32[]{:S(2)}, u32[]{:S(2)}) collective-permute-start(f32[8,64,128]{2,1,0:T(8,128)S(1)} %sweep.24.own_ref), channel_id=1, source_target_pairs={{0,31},{1,2},{2,1},{3,4},{4,3},{5,6},{6,5},{7,8},{8,7},{9,10},{10,... | collective-permute-start | bytes 786440 | tf_op jit(solution)/shard_map/ppermute | solution.py:211
  20.4 4.8 %collective-permute-start.6 = (f32[8,64,128]{2,1,0:T(8,128)S(1)}, f32[8,64,128]{2,1,0:T(8,128)S(1)}, u32[]{:S(2)}, u32[]{:S(2)}) collective-permute-start(f32[8,64,128]{2,1,0:T(8,128)S(1)} %sweep.25.own_ref), channel_id=1, source_target_pairs={{0,1},{1,0},{2,3},{3,2},{4,5},{5,4},{6,7},{7,6},{8,9},{9,8},{10,11... | collective-permute-start | bytes 786440 | tf_op jit(solution)/shard_map/ppermute | solution.py:212
  20.5 10.3 %collective-permute-start.4 = (f32[8,64,128]{2,1,0:T(8,128)S(1)}, f32[8,64,128]{2,1,0:T(8,128)S(1)}, u32[]{:S(2)}, u32[]{:S(2)}) collective-permute-start(f32[8,64,128]{2,1,0:T(8,128)S(1)} %sweep.25.own_ref), channel_id=1, source_target_pairs={{0,31},{1,2},{2,1},{3,4},{4,3},{5,6},{6,5},{7,8},{8,7},{9,10},{10,... | collective-permute-start | bytes 786440 | tf_op jit(solution)/shard_map/ppermute | solution.py:211
  26.1 4.7 %collective-permute-start.7 = (f32[8,64,128]{2,1,0:T(8,128)S(1)}, f32[8,64,128]{2,1,0:T(8,128)S(1)}, u32[]{:S(2)}, u32[]{:S(2)}) collective-permute-start(f32[8,64,128]{2,1,0:T(8,128)S(1)} %sweep.26.own_ref), channel_id=1, source_target_pairs={{0,1},{1,0},{2,3},{3,2},{4,5},{5,4},{6,7},{7,6},{8,9},{9,8},{10,11... | collective-permute-start | bytes 786440 | tf_op jit(solution)/shard_map/ppermute | solution.py:212
  26.7 9.7 %collective-permute-start.9 = (f32[8,64,128]{2,1,0:T(8,128)S(1)}, f32[8,64,128]{2,1,0:T(8,128)S(1)}, u32[]{:S(2)}, u32[]{:S(2)}) collective-permute-start(f32[8,64,128]{2,1,0:T(8,128)S(1)} %sweep.26.own_ref), channel_id=1, source_target_pairs={{0,31},{1,2},{2,1},{3,4},{4,3},{5,6},{6,5},{7,8},{8,7},{9,10},{10,... | collective-permute-start | bytes 786440 | tf_op jit(solution)/shard_map/ppermute | solution.py:211
  31.6 4.8 %collective-permute-start.10 = (f32[8,64,128]{2,1,0:T(8,128)S(1)}, f32[8,64,128]{2,1,0:T(8,128)S(1)}, u32[]{:S(2)}, u32[]{:S(2)}) collective-permute-start(f32[8,64,128]{2,1,0:T(8,128)S(1)} %sweep.27.own_ref), channel_id=1, source_target_pairs={{0,1},{1,0},{2,3},{3,2},{4,5},{5,4},{6,7},{7,6},{8,9},{9,8},{10,11... | collective-permute-start | bytes 786440 | tf_op jit(solution)/shard_map/ppermute | solution.py:212
  32.4 9.7 %collective-permute-start.8 = (f32[8,64,128]{2,1,0:T(8,128)S(1)}, f32[8,64,128]{2,1,0:T(8,128)S(1)}, u32[]{:S(2)}, u32[]{:S(2)}) collective-permute-start(f32[8,64,128]{2,1,0:T(8,128)S(1)} %sweep.27.own_ref), channel_id=1, source_target_pairs={{0,31},{1,2},{2,1},{3,4},{4,3},{5,6},{6,5},{7,8},{8,7},{9,10},{10,... | collective-permute-start | bytes 786440 | tf_op jit(solution)/shard_map/ppermute | solution.py:211
  37.3 4.8 %collective-permute-start.11 = (f32[8,64,128]{2,1,0:T(8,128)S(1)}, f32[8,64,128]{2,1,0:T(8,128)S(1)}, u32[]{:S(2)}, u32[]{:S(2)}) collective-permute-start(f32[8,64,128]{2,1,0:T(8,128)S(1)} %sweep.28.own_ref), channel_id=1, source_target_pairs={{0,1},{1,0},{2,3},{3,2},{4,5},{5,4},{6,7},{7,6},{8,9},{9,8},{10,11... | collective-permute-start | bytes 786440 | tf_op jit(solution)/shard_map/ppermute | solution.py:212
  38.0 9.7 %collective-permute-start.13 = (f32[8,64,128]{2,1,0:T(8,128)S(1)}, f32[8,64,128]{2,1,0:T(8,128)S(1)}, u32[]{:S(2)}, u32[]{:S(2)}) collective-permute-start(f32[8,64,128]{2,1,0:T(8,128)S(1)} %sweep.28.own_ref), channel_id=1, source_target_pairs={{0,31},{1,2},{2,1},{3,4},{4,3},{5,6},{6,5},{7,8},{8,7},{9,10},{10,... | collective-permute-start | bytes 786440 | tf_op jit(solution)/shard_map/ppermute | solution.py:211
  42.9 4.8 %collective-permute-start.14 = (f32[8,64,128]{2,1,0:T(8,128)S(1)}, f32[8,64,128]{2,1,0:T(8,128)S(1)}, u32[]{:S(2)}, u32[]{:S(2)}) collective-permute-start(f32[8,64,128]{2,1,0:T(8,128)S(1)} %sweep.29.own_ref), channel_id=1, source_target_pairs={{0,1},{1,0},{2,3},{3,2},{4,5},{5,4},{6,7},{7,6},{8,9},{9,8},{10,11... | collective-permute-start | bytes 786440 | tf_op jit(solution)/shard_map/ppermute | solution.py:212
  43.6 9.7 %collective-permute-start.12 = (f32[8,64,128]{2,1,0:T(8,128)S(1)}, f32[8,64,128]{2,1,0:T(8,128)S(1)}, u32[]{:S(2)}, u32[]{:S(2)}) collective-permute-start(f32[8,64,128]{2,1,0:T(8,128)S(1)} %sweep.29.own_ref), channel_id=1, source_target_pairs={{0,31},{1,2},{2,1},{3,4},{4,3},{5,6},{6,5},{7,8},{8,7},{9,10},{10,... | collective-permute-start | bytes 786440 | tf_op jit(solution)/shard_map/ppermute | solution.py:211
  48.5 4.8 %collective-permute-start.15 = (f32[8,64,128]{2,1,0:T(8,128)S(1)}, f32[8,64,128]{2,1,0:T(8,128)S(1)}, u32[]{:S(2)}, u32[]{:S(2)}) collective-permute-start(f32[8,64,128]{2,1,0:T(8,128)S(1)} %sweep.30.own_ref), channel_id=1, source_target_pairs={{0,1},{1,0},{2,3},{3,2},{4,5},{5,4},{6,7},{7,6},{8,9},{9,8},{10,11... | collective-permute-start | bytes 786440 | tf_op jit(solution)/shard_map/ppermute | solution.py:212
  49.2 9.7 %collective-permute-start.17 = (f32[8,64,128]{2,1,0:T(8,128)S(1)}, f32[8,64,128]{2,1,0:T(8,128)S(1)}, u32[]{:S(2)}, u32[]{:S(2)}) collective-permute-start(f32[8,64,128]{2,1,0:T(8,128)S(1)} %sweep.30.own_ref), channel_id=1, source_target_pairs={{0,31},{1,2},{2,1},{3,4},{4,3},{5,6},{6,5},{7,8},{8,7},{9,10},{10,... | collective-permute-start | bytes 786440 | tf_op jit(solution)/shard_map/ppermute | solution.py:211
  54.1 4.8 %collective-permute-start.18 = (f32[8,64,128]{2,1,0:T(8,128)S(1)}, f32[8,64,128]{2,1,0:T(8,128)S(1)}, u32[]{:S(2)}, u32[]{:S(2)}) collective-permute-start(f32[8,64,128]{2,1,0:T(8,128)S(1)} %sweep.31.own_ref), channel_id=1, source_target_pairs={{0,1},{1,0},{2,3},{3,2},{4,5},{5,4},{6,7},{7,6},{8,9},{9,8},{10,11... | collective-permute-start | bytes 786440 | tf_op jit(solution)/shard_map/ppermute | solution.py:212
  54.8 9.7 %collective-permute-start.16 = (f32[8,64,128]{2,1,0:T(8,128)S(1)}, f32[8,64,128]{2,1,0:T(8,128)S(1)}, u32[]{:S(2)}, u32[]{:S(2)}) collective-permute-start(f32[8,64,128]{2,1,0:T(8,128)S(1)} %sweep.31.own_ref), channel_id=1, source_target_pairs={{0,31},{1,2},{2,1},{3,4},{4,3},{5,6},{6,5},{7,8},{8,7},{9,10},{10,... | collective-permute-start | bytes 786440 | tf_op jit(solution)/shard_map/ppermute | solution.py:211
  59.7 4.8 %collective-permute-start.19 = (f32[8,64,128]{2,1,0:T(8,128)S(1)}, f32[8,64,128]{2,1,0:T(8,128)S(1)}, u32[]{:S(2)}, u32[]{:S(2)}) collective-permute-start(f32[8,64,128]{2,1,0:T(8,128)S(1)} %sweep.32.own_ref), channel_id=1, source_target_pairs={{0,1},{1,0},{2,3},{3,2},{4,5},{5,4},{6,7},{7,6},{8,9},{9,8},{10,11... | collective-permute-start | bytes 786440 | tf_op jit(solution)/shard_map/ppermute | solution.py:212
  60.4 9.7 %collective-permute-start.21 = (f32[8,64,128]{2,1,0:T(8,128)S(1)}, f32[8,64,128]{2,1,0:T(8,128)S(1)}, u32[]{:S(2)}, u32[]{:S(2)}) collective-permute-start(f32[8,64,128]{2,1,0:T(8,128)S(1)} %sweep.32.own_ref), channel_id=1, source_target_pairs={{0,31},{1,2},{2,1},{3,4},{4,3},{5,6},{6,5},{7,8},{8,7},{9,10},{10,... | collective-permute-start | bytes 786440 | tf_op jit(solution)/shard_map/ppermute | solution.py:211
  65.3 4.8 %collective-permute-start.22 = (f32[8,64,128]{2,1,0:T(8,128)S(1)}, f32[8,64,128]{2,1,0:T(8,128)S(1)}, u32[]{:S(2)}, u32[]{:S(2)}) collective-permute-start(f32[8,64,128]{2,1,0:T(8,128)S(1)} %sweep.33.own_ref), channel_id=1, source_target_pairs={{0,1},{1,0},{2,3},{3,2},{4,5},{5,4},{6,7},{7,6},{8,9},{9,8},{10,11... | collective-permute-start | bytes 786440 | tf_op jit(solution)/shard_map/ppermute | solution.py:212
  66.1 9.9 %collective-permute-start.20 = (f32[8,64,128]{2,1,0:T(8,128)S(1)}, f32[8,64,128]{2,1,0:T(8,128)S(1)}, u32[]{:S(2)}, u32[]{:S(2)}) collective-permute-start(f32[8,64,128]{2,1,0:T(8,128)S(1)} %sweep.33.own_ref), channel_id=1, source_target_pairs={{0,31},{1,2},{2,1},{3,4},{4,3},{5,6},{6,5},{7,8},{8,7},{9,10},{10,... | collective-permute-start | bytes 786440 | tf_op jit(solution)/shard_map/ppermute | solution.py:211
  71.1 4.8 %collective-permute-start.23 = (f32[8,64,128]{2,1,0:T(8,128)S(1)}, f32[8,64,128]{2,1,0:T(8,128)S(1)}, u32[]{:S(2)}, u32[]{:S(2)}) collective-permute-start(f32[8,64,128]{2,1,0:T(8,128)S(1)} %sweep.34.own_ref), channel_id=1, source_target_pairs={{0,1},{1,0},{2,3},{3,2},{4,5},{5,4},{6,7},{7,6},{8,9},{9,8},{10,11... | collective-permute-start | bytes 786440 | tf_op jit(solution)/shard_map/ppermute | solution.py:212
  71.9 9.5 %collective-permute-start.25 = (f32[8,64,128]{2,1,0:T(8,128)S(1)}, f32[8,64,128]{2,1,0:T(8,128)S(1)}, u32[]{:S(2)}, u32[]{:S(2)}) collective-permute-start(f32[8,64,128]{2,1,0:T(8,128)S(1)} %sweep.34.own_ref), channel_id=1, source_target_pairs={{0,31},{1,2},{2,1},{3,4},{4,3},{5,6},{6,5},{7,8},{8,7},{9,10},{10,... | collective-permute-start | bytes 786440 | tf_op jit(solution)/shard_map/ppermute | solution.py:211
  76.8 4.6 %collective-permute-start.26 = (f32[8,64,128]{2,1,0:T(8,128)S(1)}, f32[8,64,128]{2,1,0:T(8,128)S(1)}, u32[]{:S(2)}, u32[]{:S(2)}) collective-permute-start(f32[8,64,128]{2,1,0:T(8,128)S(1)} %sweep.35.own_ref), channel_id=1, source_target_pairs={{0,1},{1,0},{2,3},{3,2},{4,5},{5,4},{6,7},{7,6},{8,9},{9,8},{10,11... | collective-permute-start | bytes 786440 | tf_op jit(solution)/shard_map/ppermute | solution.py:212
  77.3 9.7 %collective-permute-start.24 = (f32[8,64,128]{2,1,0:T(8,128)S(1)}, f32[8,64,128]{2,1,0:T(8,128)S(1)}, u32[]{:S(2)}, u32[]{:S(2)}) collective-permute-start(f32[8,64,128]{2,1,0:T(8,128)S(1)} %sweep.35.own_ref), channel_id=1, source_target_pairs={{0,31},{1,2},{2,1},{3,4},{4,3},{5,6},{6,5},{7,8},{8,7},{9,10},{10,... | collective-permute-start | bytes 786440 | tf_op jit(solution)/shard_map/ppermute | solution.py:211
  82.2 4.8 %collective-permute-start.27 = (f32[8,64,128]{2,1,0:T(8,128)S(1)}, f32[8,64,128]{2,1,0:T(8,128)S(1)}, u32[]{:S(2)}, u32[]{:S(2)}) collective-permute-start(f32[8,64,128]{2,1,0:T(8,128)S(1)} %sweep.36.own_ref), channel_id=1, source_target_pairs={{0,1},{1,0},{2,3},{3,2},{4,5},{5,4},{6,7},{7,6},{8,9},{9,8},{10,11... | collective-permute-start | bytes 786440 | tf_op jit(solution)/shard_map/ppermute | solution.py:212
  82.9 9.7 %collective-permute-start.29 = (f32[8,64,128]{2,1,0:T(8,128)S(1)}, f32[8,64,128]{2,1,0:T(8,128)S(1)}, u32[]{:S(2)}, u32[]{:S(2)}) collective-permute-start(f32[8,64,128]{2,1,0:T(8,128)S(1)} %sweep.36.own_ref), channel_id=1, source_target_pairs={{0,31},{1,2},{2,1},{3,4},{4,3},{5,6},{6,5},{7,8},{8,7},{9,10},{10,... | collective-permute-start | bytes 786440 | tf_op jit(solution)/shard_map/ppermute | solution.py:211
  87.8 4.8 %collective-permute-start.30 = (f32[8,64,128]{2,1,0:T(8,128)S(1)}, f32[8,64,128]{2,1,0:T(8,128)S(1)}, u32[]{:S(2)}, u32[]{:S(2)}) collective-permute-start(f32[8,64,128]{2,1,0:T(8,128)S(1)} %sweep.37.own_ref), channel_id=1, source_target_pairs={{0,1},{1,0},{2,3},{3,2},{4,5},{5,4},{6,7},{7,6},{8,9},{9,8},{10,11... | collective-permute-start | bytes 786440 | tf_op jit(solution)/shard_map/ppermute | solution.py:212
  88.5 9.7 %collective-permute-start.28 = (f32[8,64,128]{2,1,0:T(8,128)S(1)}, f32[8,64,128]{2,1,0:T(8,128)S(1)}, u32[]{:S(2)}, u32[]{:S(2)}) collective-permute-start(f32[8,64,128]{2,1,0:T(8,128)S(1)} %sweep.37.own_ref), channel_id=1, source_target_pairs={{0,31},{1,2},{2,1},{3,4},{4,3},{5,6},{6,5},{7,8},{8,7},{9,10},{10,... | collective-permute-start | bytes 786440 | tf_op jit(solution)/shard_map/ppermute | solution.py:211
  93.4 4.8 %collective-permute-start.31 = (f32[8,64,128]{2,1,0:T(8,128)S(1)}, f32[8,64,128]{2,1,0:T(8,128)S(1)}, u32[]{:S(2)}, u32[]{:S(2)}) collective-permute-start(f32[8,64,128]{2,1,0:T(8,128)S(1)} %sweep.38.own_ref), channel_id=1, source_target_pairs={{0,1},{1,0},{2,3},{3,2},{4,5},{5,4},{6,7},{7,6},{8,9},{9,8},{10,11... | collective-permute-start | bytes 786440 | tf_op jit(solution)/shard_map/ppermute | solution.py:212
  94.1 9.7 %collective-permute-start.33 = (f32[8,64,128]{2,1,0:T(8,128)S(1)}, f32[8,64,128]{2,1,0:T(8,128)S(1)}, u32[]{:S(2)}, u32[]{:S(2)}) collective-permute-start(f32[8,64,128]{2,1,0:T(8,128)S(1)} %sweep.38.own_ref), channel_id=1, source_target_pairs={{0,31},{1,2},{2,1},{3,4},{4,3},{5,6},{6,5},{7,8},{8,7},{9,10},{10,... | collective-permute-start | bytes 786440 | tf_op jit(solution)/shard_map/ppermute | solution.py:211
  99.0 4.8 %collective-permute-start.34 = (f32[8,64,128]{2,1,0:T(8,128)S(1)}, f32[8,64,128]{2,1,0:T(8,128)S(1)}, u32[]{:S(2)}, u32[]{:S(2)}) collective-permute-start(f32[8,64,128]{2,1,0:T(8,128)S(1)} %sweep.39.own_ref), channel_id=1, source_target_pairs={{0,1},{1,0},{2,3},{3,2},{4,5},{5,4},{6,7},{7,6},{8,9},{9,8},{10,11... | collective-permute-start | bytes 786440 | tf_op jit(solution)/shard_map/ppermute | solution.py:212
  99.8 9.7 %collective-permute-start.32 = (f32[8,64,128]{2,1,0:T(8,128)S(1)}, f32[8,64,128]{2,1,0:T(8,128)S(1)}, u32[]{:S(2)}, u32[]{:S(2)}) collective-permute-start(f32[8,64,128]{2,1,0:T(8,128)S(1)} %sweep.39.own_ref), channel_id=1, source_target_pairs={{0,31},{1,2},{2,1},{3,4},{4,3},{5,6},{6,5},{7,8},{8,7},{9,10},{10,... | collective-permute-start | bytes 786440 | tf_op jit(solution)/shard_map/ppermute | solution.py:211
  104.7 4.8 %collective-permute-start.35 = (f32[8,64,128]{2,1,0:T(8,128)S(1)}, f32[8,64,128]{2,1,0:T(8,128)S(1)}, u32[]{:S(2)}, u32[]{:S(2)}) collective-permute-start(f32[8,64,128]{2,1,0:T(8,128)S(1)} %sweep.40.own_ref), channel_id=1, source_target_pairs={{0,1},{1,0},{2,3},{3,2},{4,5},{5,4},{6,7},{7,6},{8,9},{9,8},{10,11... | collective-permute-start | bytes 786440 | tf_op jit(solution)/shard_map/ppermute | solution.py:212
  105.4 9.7 %collective-permute-start.37 = (f32[8,64,128]{2,1,0:T(8,128)S(1)}, f32[8,64,128]{2,1,0:T(8,128)S(1)}, u32[]{:S(2)}, u32[]{:S(2)}) collective-permute-start(f32[8,64,128]{2,1,0:T(8,128)S(1)} %sweep.40.own_ref), channel_id=1, source_target_pairs={{0,31},{1,2},{2,1},{3,4},{4,3},{5,6},{6,5},{7,8},{8,7},{9,10},{10,... | collective-permute-start | bytes 786440 | tf_op jit(solution)/shard_map/ppermute | solution.py:211
  110.3 4.8 %collective-permute-start.38 = (f32[8,64,128]{2,1,0:T(8,128)S(1)}, f32[8,64,128]{2,1,0:T(8,128)S(1)}, u32[]{:S(2)}, u32[]{:S(2)}) collective-permute-start(f32[8,64,128]{2,1,0:T(8,128)S(1)} %sweep.41.own_ref), channel_id=1, source_target_pairs={{0,1},{1,0},{2,3},{3,2},{4,5},{5,4},{6,7},{7,6},{8,9},{9,8},{10,11... | collective-permute-start | bytes 786440 | tf_op jit(solution)/shard_map/ppermute | solution.py:212
  111.0 9.7 %collective-permute-start.36 = (f32[8,64,128]{2,1,0:T(8,128)S(1)}, f32[8,64,128]{2,1,0:T(8,128)S(1)}, u32[]{:S(2)}, u32[]{:S(2)}) collective-permute-start(f32[8,64,128]{2,1,0:T(8,128)S(1)} %sweep.41.own_ref), channel_id=1, source_target_pairs={{0,31},{1,2},{2,1},{3,4},{4,3},{5,6},{6,5},{7,8},{8,7},{9,10},{10,... | collective-permute-start | bytes 786440 | tf_op jit(solution)/shard_map/ppermute | solution.py:211
  115.9 4.8 %collective-permute-start.39 = (f32[8,64,128]{2,1,0:T(8,128)S(1)}, f32[8,64,128]{2,1,0:T(8,128)S(1)}, u32[]{:S(2)}, u32[]{:S(2)}) collective-permute-start(f32[8,64,128]{2,1,0:T(8,128)S(1)} %sweep.42.own_ref), channel_id=1, source_target_pairs={{0,1},{1,0},{2,3},{3,2},{4,5},{5,4},{6,7},{7,6},{8,9},{9,8},{10,11... | collective-permute-start | bytes 786440 | tf_op jit(solution)/shard_map/ppermute | solution.py:212
  116.6 9.7 %collective-permute-start.41 = (f32[8,64,128]{2,1,0:T(8,128)S(1)}, f32[8,64,128]{2,1,0:T(8,128)S(1)}, u32[]{:S(2)}, u32[]{:S(2)}) collective-permute-start(f32[8,64,128]{2,1,0:T(8,128)S(1)} %sweep.42.own_ref), channel_id=1, source_target_pairs={{0,31},{1,2},{2,1},{3,4},{4,3},{5,6},{6,5},{7,8},{8,7},{9,10},{10,... | collective-permute-start | bytes 786440 | tf_op jit(solution)/shard_map/ppermute | solution.py:211
  121.5 4.8 %collective-permute-start.42 = (f32[8,64,128]{2,1,0:T(8,128)S(1)}, f32[8,64,128]{2,1,0:T(8,128)S(1)}, u32[]{:S(2)}, u32[]{:S(2)}) collective-permute-start(f32[8,64,128]{2,1,0:T(8,128)S(1)} %sweep.43.own_ref), channel_id=1, source_target_pairs={{0,1},{1,0},{2,3},{3,2},{4,5},{5,4},{6,7},{7,6},{8,9},{9,8},{10,11... | collective-permute-start | bytes 786440 | tf_op jit(solution)/shard_map/ppermute | solution.py:212
  122.2 9.7 %collective-permute-start.40 = (f32[8,64,128]{2,1,0:T(8,128)S(1)}, f32[8,64,128]{2,1,0:T(8,128)S(1)}, u32[]{:S(2)}, u32[]{:S(2)}) collective-permute-start(f32[8,64,128]{2,1,0:T(8,128)S(1)} %sweep.43.own_ref), channel_id=1, source_target_pairs={{0,31},{1,2},{2,1},{3,4},{4,3},{5,6},{6,5},{7,8},{8,7},{9,10},{10,... | collective-permute-start | bytes 786440 | tf_op jit(solution)/shard_map/ppermute | solution.py:211
  127.1 4.8 %collective-permute-start.43 = (f32[8,64,128]{2,1,0:T(8,128)S(1)}, f32[8,64,128]{2,1,0:T(8,128)S(1)}, u32[]{:S(2)}, u32[]{:S(2)}) collective-permute-start(f32[8,64,128]{2,1,0:T(8,128)S(1)} %sweep.44.own_ref), channel_id=1, source_target_pairs={{0,1},{1,0},{2,3},{3,2},{4,5},{5,4},{6,7},{7,6},{8,9},{9,8},{10,11... | collective-permute-start | bytes 786440 | tf_op jit(solution)/shard_map/ppermute | solution.py:212
  127.9 9.7 %collective-permute-start.45 = (f32[8,64,128]{2,1,0:T(8,128)S(1)}, f32[8,64,128]{2,1,0:T(8,128)S(1)}, u32[]{:S(2)}, u32[]{:S(2)}) collective-permute-start(f32[8,64,128]{2,1,0:T(8,128)S(1)} %sweep.44.own_ref), channel_id=1, source_target_pairs={{0,31},{1,2},{2,1},{3,4},{4,3},{5,6},{6,5},{7,8},{8,7},{9,10},{10,... | collective-permute-start | bytes 786440 | tf_op jit(solution)/shard_map/ppermute | solution.py:211
  132.8 4.8 %collective-permute-start.46 = (f32[8,64,128]{2,1,0:T(8,128)S(1)}, f32[8,64,128]{2,1,0:T(8,128)S(1)}, u32[]{:S(2)}, u32[]{:S(2)}) collective-permute-start(f32[8,64,128]{2,1,0:T(8,128)S(1)} %sweep.45.own_ref), channel_id=1, source_target_pairs={{0,1},{1,0},{2,3},{3,2},{4,5},{5,4},{6,7},{7,6},{8,9},{9,8},{10,11... | collective-permute-start | bytes 786440 | tf_op jit(solution)/shard_map/ppermute | solution.py:212
  133.5 9.5 %collective-permute-start.44 = (f32[8,64,128]{2,1,0:T(8,128)S(1)}, f32[8,64,128]{2,1,0:T(8,128)S(1)}, u32[]{:S(2)}, u32[]{:S(2)}) collective-permute-start(f32[8,64,128]{2,1,0:T(8,128)S(1)} %sweep.45.own_ref), channel_id=1, source_target_pairs={{0,31},{1,2},{2,1},{3,4},{4,3},{5,6},{6,5},{7,8},{8,7},{9,10},{10,... | collective-permute-start | bytes 786440 | tf_op jit(solution)/shard_map/ppermute | solution.py:211
  138.4 4.6 %collective-permute-start.47 = (f32[8,64,128]{2,1,0:T(8,128)S(1)}, f32[8,64,128]{2,1,0:T(8,128)S(1)}, u32[]{:S(2)}, u32[]{:S(2)}) collective-permute-start(f32[8,64,128]{2,1,0:T(8,128)S(1)} %sweep.46.refs_0_), channel_id=1, source_target_pairs={{0,1},{1,0},{2,3},{3,2},{4,5},{5,4},{6,7},{7,6},{8,9},{9,8},{10,11... | collective-permute-start | bytes 786440 | tf_op jit(solution)/shard_map/ppermute | solution.py:212
  143.8 1.6 %collective-permute-start.48 = (f32[8,64,128]{2,1,0:T(8,128)S(1)}, f32[8,64,128]{2,1,0:T(8,128)S(1)}, u32[]{:S(2)}, u32[]{:S(2)}) collective-permute-start(f32[8,64,128]{2,1,0:T(8,128)S(1)} %sweep.47.refs_1_), channel_id=1, source_target_pairs={{0,1},{1,0},{2,3},{3,2},{4,5},{5,4},{6,7},{7,6},{8,9},{9,8},{10,11... | collective-permute-start | bytes 786440 | tf_op jit(solution)/shard_map/ppermute | solution.py:212

commit v5 on v4

--- a/solution.py
+++ b/solution.py
@@ -130,18 +130,25 @@
 
 
 def finish_kernel(other, *refs):
-    chunk_refs, (out_ref, held_ref, sem) = refs[:CHUNKS], refs[-3:]
+    chunk_refs, (out_ref, held_ref, sems) = refs[:CHUNKS], refs[-3:]
     blocks, _, lanes = chunk_refs[0].shape
     core = lax.axis_index("act")
     one = unit(lanes, 3)
+    half_ref = half_of(out_ref, 1 - core if other else core)
+    rows = blocks * lanes // 2
+    copies = []
     for b in range(blocks):
         panel = jnp.concatenate([ref[b] for ref in chunk_refs], axis=0)
         high = panel.astype(jnp.bfloat16)
         middle, low = split(panel - high.astype(jnp.float32))
         held_ref[b * lanes : (b + 1) * lanes] = times_turned(one, jnp.concatenate([high, middle, low], axis=1))
-    copy = pltpu.make_async_copy(held_ref, half_of(out_ref, 1 - core if other else core), sem)
-    copy.start()
-    copy.wait()
+        if (b + 1) % (blocks // 2) == 0:
+            n = len(copies)
+            part = pl.ds(n * rows, rows)
+            copies.append(pltpu.make_async_copy(held_ref.at[part], half_ref.at[part], sems.at[n]))
+            copies[-1].start()
+    for copy in copies:
+        copy.wait()
 
 
 def per_device(transitions, columns, targets):
@@ -220,7 +227,7 @@
             out_shape=jax.ShapeDtypeStruct((2 * blocks * lanes, sets), jnp.float32),
             in_specs=[WHOLE] * CHUNKS + [ANYWHERE] * len(half),
             out_specs=ANYWHERE,
-            scratch_shapes=[pltpu.VMEM((blocks * lanes, sets), jnp.float32), pltpu.SemaphoreType.DMA],
+            scratch_shapes=[pltpu.VMEM((blocks * lanes, sets), jnp.float32), pltpu.SemaphoreType.DMA((2,))],
             input_output_aliases={CHUNKS: 0} if half else {},
             name="finish",
             compiler_params=pltpu.CompilerParams(vmem_limit_bytes=8 << 20),

time: 147 us -> 147 us (level)
  no operation moved by 1% of the time
where the time goes in v5:
time: 147 us
  starting transfers between devices  114 us (78%)
  Pallas kernels  27.3 us (19%)
  waiting for transfers between devices  4.95 us (3%)
    ppermute x22, starting transfers between devices, per_device(): ici[c] = lax.ppermute(own[c], AXES, to_ici)  92 us
    pallas_call x24, Pallas kernels, sweep(): pl.pallas_call(sweep_kernel, out_shape=jax.ShapeDtypeStruct(own.shape, jn...  20.1 us
    ppermute x24, starting transfers between devices, per_device(): sib[c] = lax.ppermute(own[c], AXES, to_sib)  14.9 us
    ppermute x2, starting transfers between devices, per_device(): ici = [lax.ppermute(v, AXES, to_ici) for v in zero]  6.73 us
    ppermute x22, waiting for transfers between devices, per_device(): ici[c] = lax.ppermute(own[c], AXES, to_ici)  3.94 us
    pallas_call x1, Pallas kernels, per_device(): pl.pallas_call(rest_kernel, out_shape=[SMEM((2 * acts_here * blocks * 2,)...  3.44 us
  transfers between devices with their start and end apart: 49, of which 3 were waited for; matrix products, arithmetic and copies ran while one was open for 0% of the time, Pallas kernels for 17%

profile of v5, /device:TPU:0, one launch (start us, length us, event | category | flops | bytes accessed | tf_op | source)
XLA Modules:
  0.0 146.8 jit_solution(15710525911127534592)
XLA Ops:
  0.5 1.4 own_targets.1
  1.8 6.7 %collective-permute-start.2 = (f32[8,64,128]{2,1,0:T(8,128)S(1)}, f32[8,64,128]{2,1,0:T(8,128)S(1)}, u32[]{:S(2)}, u32[]{:S(2)}) collective-permute-start(f32[8,64,128]{2,1,0:T(8,128)S(1)} %get-tuple-element.62.own_ref.target_ref), channel_id=1, source_target_pairs={{0,31},{1,2},{2,1},{3,4},{4,3},{5,6},{6,5},{7,8},{8,7},{9,10},{10,... | collective-permute-start | bytes 786440 | tf_op jit(solution)/shard_map/ppermute | solution.py:179
  8.6 3.4 %rest.1 = (s32[64]{0:T(128)S(4)}, bf16[8,4,256,256]{3,2,1,0:T(8,128)(2,1)S(1)}, f32[8,64,128]{2,1,0:T(8,128)S(1)}, f32[8,64,128]{2,1,0:T(8,128)S(1)}) custom-call(s32[4,2,16]{2,1,0:T(2,128)S(4)} %get-tuple-element.58.columns_ref, s32[2048,128]{1,0:T(8,128)} %targets_ref.3, f32[2,16,2,128,128]{4,3,2,1,0:T(8,128)} %tiles_ref.1, ...), custom_call_target="tpu_custom_call" | custom-call | tf_op jit(solution)/shard_map/rest/pallas_call | solution.py:181
  12.7 0.8 sweep.24.own_ref
  13.6 6.0 %collective-permute-start.5 = (f32[8,64,128]{2,1,0:T(8,128)S(1)}, f32[8,64,128]{2,1,0:T(8,128)S(1)}, u32[]{:S(2)}, u32[]{:S(2)}) collective-permute-start(f32[8,64,128]{2,1,0:T(8,128)S(1)} %sweep.24.own_ref), channel_id=1, source_target_pairs={{0,31},{1,2},{2,1},{3,4},{4,3},{5,6},{6,5},{7,8},{8,7},{9,10},{10,... | collective-permute-start | bytes 786440 | tf_op jit(solution)/shard_map/ppermute | solution.py:218
  19.6 0.8 sweep.25.own_ref
  20.5 4.7 %collective-permute-start.4 = (f32[8,64,128]{2,1,0:T(8,128)S(1)}, f32[8,64,128]{2,1,0:T(8,128)S(1)}, u32[]{:S(2)}, u32[]{:S(2)}) collective-permute-start(f32[8,64,128]{2,1,0:T(8,128)S(1)} %sweep.25.own_ref), channel_id=1, source_target_pairs={{0,31},{1,2},{2,1},{3,4},{4,3},{5,6},{6,5},{7,8},{8,7},{9,10},{10,... | collective-permute-start | bytes 786440 | tf_op jit(solution)/shard_map/ppermute | solution.py:218
  25.2 0.8 sweep.26.own_ref
  26.7 4.1 %collective-permute-start.9 = (f32[8,64,128]{2,1,0:T(8,128)S(1)}, f32[8,64,128]{2,1,0:T(8,128)S(1)}, u32[]{:S(2)}, u32[]{:S(2)}) collective-permute-start(f32[8,64,128]{2,1,0:T(8,128)S(1)} %sweep.26.own_ref), channel_id=1, source_target_pairs={{0,31},{1,2},{2,1},{3,4},{4,3},{5,6},{6,5},{7,8},{8,7},{9,10},{10,... | collective-permute-start | bytes 786440 | tf_op jit(solution)/shard_map/ppermute | solution.py:218
  30.8 0.8 sweep.27.own_ref
  31.6 0.7 collective-permute-start.10
  32.4 4.1 %collective-permute-start.8 = (f32[8,64,128]{2,1,0:T(8,128)S(1)}, f32[8,64,128]{2,1,0:T(8,128)S(1)}, u32[]{:S(2)}, u32[]{:S(2)}) collective-permute-start(f32[8,64,128]{2,1,0:T(8,128)S(1)} %sweep.27.own_ref), channel_id=1, source_target_pairs={{0,31},{1,2},{2,1},{3,4},{4,3},{5,6},{6,5},{7,8},{8,7},{9,10},{10,... | collective-permute-start | bytes 786440 | tf_op jit(solution)/shard_map/ppermute | solution.py:218
  36.4 0.8 sweep.28.own_ref
  37.3 0.7 collective-permute-start.11
  38.0 4.1 %collective-permute-start.13 = (f32[8,64,128]{2,1,0:T(8,128)S(1)}, f32[8,64,128]{2,1,0:T(8,128)S(1)}, u32[]{:S(2)}, u32[]{:S(2)}) collective-permute-start(f32[8,64,128]{2,1,0:T(8,128)S(1)} %sweep.28.own_ref), channel_id=1, source_target_pairs={{0,31},{1,2},{2,1},{3,4},{4,3},{5,6},{6,5},{7,8},{8,7},{9,10},{10,... | collective-permute-start | bytes 786440 | tf_op jit(solution)/shard_map/ppermute | solution.py:218
  42.0 0.8 sweep.29.own_ref
  42.9 0.7 collective-permute-start.14
  43.6 4.1 %collective-permute-start.12 = (f32[8,64,128]{2,1,0:T(8,128)S(1)}, f32[8,64,128]{2,1,0:T(8,128)S(1)}, u32[]{:S(2)}, u32[]{:S(2)}) collective-permute-start(f32[8,64,128]{2,1,0:T(8,128)S(1)} %sweep.29.own_ref), channel_id=1, source_target_pairs={{0,31},{1,2},{2,1},{3,4},{4,3},{5,6},{6,5},{7,8},{8,7},{9,10},{10,... | collective-permute-start | bytes 786440 | tf_op jit(solution)/shard_map/ppermute | solution.py:218
  47.7 0.8 sweep.30.own_ref
  48.5 0.7 collective-permute-start.15
  49.2 4.1 %collective-permute-start.17 = (f32[8,64,128]{2,1,0:T(8,128)S(1)}, f32[8,64,128]{2,1,0:T(8,128)S(1)}, u32[]{:S(2)}, u32[]{:S(2)}) collective-permute-start(f32[8,64,128]{2,1,0:T(8,128)S(1)} %sweep.30.own_ref), channel_id=1, source_target_pairs={{0,31},{1,2},{2,1},{3,4},{4,3},{5,6},{6,5},{7,8},{8,7},{9,10},{10,... | collective-permute-start | bytes 786440 | tf_op jit(solution)/shard_map/ppermute | solution.py:218
  53.3 0.8 sweep.31.own_ref
  54.8 4.1 %collective-permute-start.16 = (f32[8,64,128]{2,1,0:T(8,128)S(1)}, f32[8,64,128]{2,1,0:T(8,128)S(1)}, u32[]{:S(2)}, u32[]{:S(2)}) collective-permute-start(f32[8,64,128]{2,1,0:T(8,128)S(1)} %sweep.31.own_ref), channel_id=1, source_target_pairs={{0,31},{1,2},{2,1},{3,4},{4,3},{5,6},{6,5},{7,8},{8,7},{9,10},{10,... | collective-permute-start | bytes 786440 | tf_op jit(solution)/shard_map/ppermute | solution.py:218
  58.9 0.8 sweep.32.own_ref
  59.7 0.7 collective-permute-start.19
  60.4 4.1 %collective-permute-start.21 = (f32[8,64,128]{2,1,0:T(8,128)S(1)}, f32[8,64,128]{2,1,0:T(8,128)S(1)}, u32[]{:S(2)}, u32[]{:S(2)}) collective-permute-start(f32[8,64,128]{2,1,0:T(8,128)S(1)} %sweep.32.own_ref), channel_id=1, source_target_pairs={{0,31},{1,2},{2,1},{3,4},{4,3},{5,6},{6,5},{7,8},{8,7},{9,10},{10,... | collective-permute-start | bytes 786440 | tf_op jit(solution)/shard_map/ppermute | solution.py:218
  64.5 0.8 sweep.33.own_ref
  66.1 4.1 %collective-permute-start.20 = (f32[8,64,128]{2,1,0:T(8,128)S(1)}, f32[8,64,128]{2,1,0:T(8,128)S(1)}, u32[]{:S(2)}, u32[]{:S(2)}) collective-permute-start(f32[8,64,128]{2,1,0:T(8,128)S(1)} %sweep.33.own_ref), channel_id=1, source_target_pairs={{0,31},{1,2},{2,1},{3,4},{4,3},{5,6},{6,5},{7,8},{8,7},{9,10},{10,... | collective-permute-start | bytes 786440 | tf_op jit(solution)/shard_map/ppermute | solution.py:218
  70.1 1.0 sweep.34.own_ref
  71.9 4.1 %collective-permute-start.25 = (f32[8,64,128]{2,1,0:T(8,128)S(1)}, f32[8,64,128]{2,1,0:T(8,128)S(1)}, u32[]{:S(2)}, u32[]{:S(2)}) collective-permute-start(f32[8,64,128]{2,1,0:T(8,128)S(1)} %sweep.34.own_ref), channel_id=1, source_target_pairs={{0,31},{1,2},{2,1},{3,4},{4,3},{5,6},{6,5},{7,8},{8,7},{9,10},{10,... | collective-permute-start | bytes 786440 | tf_op jit(solution)/shard_map/ppermute | solution.py:218
  75.9 0.8 sweep.35.own_ref
  77.3 4.1 %collective-permute-start.24 = (f32[8,64,128]{2,1,0:T(8,128)S(1)}, f32[8,64,128]{2,1,0:T(8,128)S(1)}, u32[]{:S(2)}, u32[]{:S(2)}) collective-permute-start(f32[8,64,128]{2,1,0:T(8,128)S(1)} %sweep.35.own_ref), channel_id=1, source_target_pairs={{0,31},{1,2},{2,1},{3,4},{4,3},{5,6},{6,5},{7,8},{8,7},{9,10},{10,... | collective-permute-start | bytes 786440 | tf_op jit(solution)/shard_map/ppermute | solution.py:218
  81.4 0.8 sweep.36.own_ref
  82.2 0.7 collective-permute-start.27
  82.9 4.1 %collective-permute-start.29 = (f32[8,64,128]{2,1,0:T(8,128)S(1)}, f32[8,64,128]{2,1,0:T(8,128)S(1)}, u32[]{:S(2)}, u32[]{:S(2)}) collective-permute-start(f32[8,64,128]{2,1,0:T(8,128)S(1)} %sweep.36.own_ref), channel_id=1, source_target_pairs={{0,31},{1,2},{2,1},{3,4},{4,3},{5,6},{6,5},{7,8},{8,7},{9,10},{10,... | collective-permute-start | bytes 786440 | tf_op jit(solution)/shard_map/ppermute | solution.py:218
  87.0 0.8 sweep.37.own_ref
  87.8 0.7 collective-permute-start.30
  88.5 4.1 %collective-permute-start.28 = (f32[8,64,128]{2,1,0:T(8,128)S(1)}, f32[8,64,128]{2,1,0:T(8,128)S(1)}, u32[]{:S(2)}, u32[]{:S(2)}) collective-permute-start(f32[8,64,128]{2,1,0:T(8,128)S(1)} %sweep.37.own_ref), channel_id=1, source_target_pairs={{0,31},{1,2},{2,1},{3,4},{4,3},{5,6},{6,5},{7,8},{8,7},{9,10},{10,... | collective-permute-start | bytes 786440 | tf_op jit(solution)/shard_map/ppermute | solution.py:218
  92.6 0.8 sweep.38.own_ref
  93.4 0.7 collective-permute-start.31
  94.1 4.1 %collective-permute-start.33 = (f32[8,64,128]{2,1,0:T(8,128)S(1)}, f32[8,64,128]{2,1,0:T(8,128)S(1)}, u32[]{:S(2)}, u32[]{:S(2)}) collective-permute-start(f32[8,64,128]{2,1,0:T(8,128)S(1)} %sweep.38.own_ref), channel_id=1, source_target_pairs={{0,31},{1,2},{2,1},{3,4},{4,3},{5,6},{6,5},{7,8},{8,7},{9,10},{10,... | collective-permute-start | bytes 786440 | tf_op jit(solution)/shard_map/ppermute | solution.py:218
  98.2 0.8 sweep.39.own_ref
  99.0 0.7 collective-permute-start.34
  99.8 4.1 %collective-permute-start.32 = (f32[8,64,128]{2,1,0:T(8,128)S(1)}, f32[8,64,128]{2,1,0:T(8,128)S(1)}, u32[]{:S(2)}, u32[]{:S(2)}) collective-permute-start(f32[8,64,128]{2,1,0:T(8,128)S(1)} %sweep.39.own_ref), channel_id=1, source_target_pairs={{0,31},{1,2},{2,1},{3,4},{4,3},{5,6},{6,5},{7,8},{8,7},{9,10},{10,... | collective-permute-start | bytes 786440 | tf_op jit(solution)/shard_map/ppermute | solution.py:218
  103.8 0.8 sweep.40.own_ref
  104.7 0.7 collective-permute-start.35
  105.4 4.1 %collective-permute-start.37 = (f32[8,64,128]{2,1,0:T(8,128)S(1)}, f32[8,64,128]{2,1,0:T(8,128)S(1)}, u32[]{:S(2)}, u32[]{:S(2)}) collective-permute-start(f32[8,64,128]{2,1,0:T(8,128)S(1)} %sweep.40.own_ref), channel_id=1, source_target_pairs={{0,31},{1,2},{2,1},{3,4},{4,3},{5,6},{6,5},{7,8},{8,7},{9,10},{10,... | collective-permute-start | bytes 786440 | tf_op jit(solution)/shard_map/ppermute | solution.py:218
  109.5 0.8 sweep.41.own_ref
  111.0 4.1 %collective-permute-start.36 = (f32[8,64,128]{2,1,0:T(8,128)S(1)}, f32[8,64,128]{2,1,0:T(8,128)S(1)}, u32[]{:S(2)}, u32[]{:S(2)}) collective-permute-start(f32[8,64,128]{2,1,0:T(8,128)S(1)} %sweep.41.own_ref), channel_id=1, source_target_pairs={{0,31},{1,2},{2,1},{3,4},{4,3},{5,6},{6,5},{7,8},{8,7},{9,10},{10,... | collective-permute-start | bytes 786440 | tf_op jit(solution)/shard_map/ppermute | solution.py:218
  115.1 0.8 sweep.42.own_ref
  115.9 0.7 collective-permute-start.39
  116.6 4.1 %collective-permute-start.41 = (f32[8,64,128]{2,1,0:T(8,128)S(1)}, f32[8,64,128]{2,1,0:T(8,128)S(1)}, u32[]{:S(2)}, u32[]{:S(2)}) collective-permute-start(f32[8,64,128]{2,1,0:T(8,128)S(1)} %sweep.42.own_ref), channel_id=1, source_target_pairs={{0,31},{1,2},{2,1},{3,4},{4,3},{5,6},{6,5},{7,8},{8,7},{9,10},{10,... | collective-permute-start | bytes 786440 | tf_op jit(solution)/shard_map/ppermute | solution.py:218
  120.7 0.8 sweep.43.own_ref
  122.2 4.1 %collective-permute-start.40 = (f32[8,64,128]{2,1,0:T(8,128)S(1)}, f32[8,64,128]{2,1,0:T(8,128)S(1)}, u32[]{:S(2)}, u32[]{:S(2)}) collective-permute-start(f32[8,64,128]{2,1,0:T(8,128)S(1)} %sweep.43.own_ref), channel_id=1, source_target_pairs={{0,31},{1,2},{2,1},{3,4},{4,3},{5,6},{6,5},{7,8},{8,7},{9,10},{10,... | collective-permute-start | bytes 786440 | tf_op jit(solution)/shard_map/ppermute | solution.py:218
  126.3 0.8 sweep.44.own_ref
  127.9 4.1 %collective-permute-start.45 = (f32[8,64,128]{2,1,0:T(8,128)S(1)}, f32[8,64,128]{2,1,0:T(8,128)S(1)}, u32[]{:S(2)}, u32[]{:S(2)}) collective-permute-start(f32[8,64,128]{2,1,0:T(8,128)S(1)} %sweep.44.own_ref), channel_id=1, source_target_pairs={{0,31},{1,2},{2,1},{3,4},{4,3},{5,6},{6,5},{7,8},{8,7},{9,10},{10,... | collective-permute-start | bytes 786440 | tf_op jit(solution)/shard_map/ppermute | solution.py:218
  131.9 0.8 sweep.45.own_ref
  132.8 0.7 collective-permute-start.46
  133.5 4.1 %collective-permute-start.44 = (f32[8,64,128]{2,1,0:T(8,128)S(1)}, f32[8,64,128]{2,1,0:T(8,128)S(1)}, u32[]{:S(2)}, u32[]{:S(2)}) collective-permute-start(f32[8,64,128]{2,1,0:T(8,128)S(1)} %sweep.45.own_ref), channel_id=1, source_target_pairs={{0,31},{1,2},{2,1},{3,4},{4,3},{5,6},{6,5},{7,8},{8,7},{9,10},{10,... | collective-permute-start | bytes 786440 | tf_op jit(solution)/shard_map/ppermute | solution.py:218
  137.5 0.8 sweep.46.refs_0_
  139.1 3.9 %collective-permute-done.44.ici_ref = f32[8,64,128]{2,1,0:T(8,128)S(1)} collective-permute-done((f32[8,64,128]{2,1,0:T(8,128)S(1)}, f32[8,64,128]{2,1,0:T(8,128)S(1)}, u32[]{:S(2)}, u32[]{:S(2)}) %collective-permute-start.44) | collective-permute-done | bytes 262176 | tf_op jit(solution)/shard_map/ppermute | solution.py:218
  143.0 0.8 sweep.47.refs_1_
  143.9 1.2 finish.2.refs_2_
  145.4 1.2 finish.3
  (62 shorter events, 8.0 us)
Async XLA Ops:
  0.0 8.6 %collective-permute-start = (f32[2,16,2,128,128]{4,3,2,1,0:T(8,128)}, f32[2,16,2,128,128]{4,3,2,1,0:T(8,128)S(1)}, u32[]{:S(2)}, u32[]{:S(2)}) collective-permute-start(f32[2,16,2,128,128]{4,3,2,1,0:T(8,128)} %tiles_ref.1), channel_id=1, source_target_pairs={{0,1},{1,0},{2,3},{3,2},{4,5},{5,4},{6,7},{7,6},{8,9},{9,8},{10,11... | collective-permute-start | bytes 12582920 | tf_op jit(solution)/shard_map/ppermute | solution.py:165
  1.8 10.8 %collective-permute-start.2 = (f32[8,64,128]{2,1,0:T(8,128)S(1)}, f32[8,64,128]{2,1,0:T(8,128)S(1)}, u32[]{:S(2)}, u32[]{:S(2)}) collective-permute-start(f32[8,64,128]{2,1,0:T(8,128)S(1)} %get-tuple-element.62.own_ref.target_ref), channel_id=1, source_target_pairs={{0,31},{1,2},{2,1},{3,4},{4,3},{5,6},{6,5},{7,8},{8,7},{9,10},{10,... | collective-permute-start | bytes 786440 | tf_op jit(solution)/shard_map/ppermute | solution.py:179
  8.5 11.1 %collective-permute-start.1 = (f32[8,64,128]{2,1,0:T(8,128)S(1)}, f32[8,64,128]{2,1,0:T(8,128)S(1)}, u32[]{:S(2)}, u32[]{:S(2)}) collective-permute-start(f32[8,64,128]{2,1,0:T(8,128)S(1)} %get-tuple-element.61.own_ref.target_ref), channel_id=1, source_target_pairs={{0,31},{1,2},{2,1},{3,4},{4,3},{5,6},{6,5},{7,8},{8,7},{9,10},{10,... | collective-permute-start | bytes 786440 | tf_op jit(solution)/shard_map/ppermute | solution.py:179
  13.5 6.1 %collective-permute-start.3 = (f32[8,64,128]{2,1,0:T(8,128)S(1)}, f32[8,64,128]{2,1,0:T(8,128)S(1)}, u32[]{:S(2)}, u32[]{:S(2)}) collective-permute-start(f32[8,64,128]{2,1,0:T(8,128)S(1)} %sweep.24.own_ref), channel_id=1, source_target_pairs={{0,1},{1,0},{2,3},{3,2},{4,5},{5,4},{6,7},{7,6},{8,9},{9,8},{10,11... | collective-permute-start | bytes 786440 | tf_op jit(solution)/shard_map/ppermute | solution.py:219
  13.6 11.6 %collective-permute-start.5 = (f32[8,64,128]{2,1,0:T(8,128)S(1)}, f32[8,64,128]{2,1,0:T(8,128)S(1)}, u32[]{:S(2)}, u32[]{:S(2)}) collective-permute-start(f32[8,64,128]{2,1,0:T(8,128)S(1)} %sweep.24.own_ref), channel_id=1, source_target_pairs={{0,31},{1,2},{2,1},{3,4},{4,3},{5,6},{6,5},{7,8},{8,7},{9,10},{10,... | collective-permute-start | bytes 786440 | tf_op jit(solution)/shard_map/ppermute | solution.py:218
  20.4 4.8 %collective-permute-start.6 = (f32[8,64,128]{2,1,0:T(8,128)S(1)}, f32[8,64,128]{2,1,0:T(8,128)S(1)}, u32[]{:S(2)}, u32[]{:S(2)}) collective-permute-start(f32[8,64,128]{2,1,0:T(8,128)S(1)} %sweep.25.own_ref), channel_id=1, source_target_pairs={{0,1},{1,0},{2,3},{3,2},{4,5},{5,4},{6,7},{7,6},{8,9},{9,8},{10,11... | collective-permute-start | bytes 786440 | tf_op jit(solution)/shard_map/ppermute | solution.py:219
  20.5 10.3 %collective-permute-start.4 = (f32[8,64,128]{2,1,0:T(8,128)S(1)}, f32[8,64,128]{2,1,0:T(8,128)S(1)}, u32[]{:S(2)}, u32[]{:S(2)}) collective-permute-start(f32[8,64,128]{2,1,0:T(8,128)S(1)} %sweep.25.own_ref), channel_id=1, source_target_pairs={{0,31},{1,2},{2,1},{3,4},{4,3},{5,6},{6,5},{7,8},{8,7},{9,10},{10,... | collective-permute-start | bytes 786440 | tf_op jit(solution)/shard_map/ppermute | solution.py:218
  26.1 4.7 %collective-permute-start.7 = (f32[8,64,128]{2,1,0:T(8,128)S(1)}, f32[8,64,128]{2,1,0:T(8,128)S(1)}, u32[]{:S(2)}, u32[]{:S(2)}) collective-permute-start(f32[8,64,128]{2,1,0:T(8,128)S(1)} %sweep.26.own_ref), channel_id=1, source_target_pairs={{0,1},{1,0},{2,3},{3,2},{4,5},{5,4},{6,7},{7,6},{8,9},{9,8},{10,11... | collective-permute-start | bytes 786440 | tf_op jit(solution)/shard_map/ppermute | solution.py:219
  26.7 9.7 %collective-permute-start.9 = (f32[8,64,128]{2,1,0:T(8,128)S(1)}, f32[8,64,128]{2,1,0:T(8,128)S(1)}, u32[]{:S(2)}, u32[]{:S(2)}) collective-permute-start(f32[8,64,128]{2,1,0:T(8,128)S(1)} %sweep.26.own_ref), channel_id=1, source_target_pairs={{0,31},{1,2},{2,1},{3,4},{4,3},{5,6},{6,5},{7,8},{8,7},{9,10},{10,... | collective-permute-start | bytes 786440 | tf_op jit(solution)/shard_map/ppermute | solution.py:218
  31.6 4.8 %collective-permute-start.10 = (f32[8,64,128]{2,1,0:T(8,128)S(1)}, f32[8,64,128]{2,1,0:T(8,128)S(1)}, u32[]{:S(2)}, u32[]{:S(2)}) collective-permute-start(f32[8,64,128]{2,1,0:T(8,128)S(1)} %sweep.27.own_ref), channel_id=1, source_target_pairs={{0,1},{1,0},{2,3},{3,2},{4,5},{5,4},{6,7},{7,6},{8,9},{9,8},{10,11... | collective-permute-start | bytes 786440 | tf_op jit(solution)/shard_map/ppermute | solution.py:219
  32.4 9.7 %collective-permute-start.8 = (f32[8,64,128]{2,1,0:T(8,128)S(1)}, f32[8,64,128]{2,1,0:T(8,128)S(1)}, u32[]{:S(2)}, u32[]{:S(2)}) collective-permute-start(f32[8,64,128]{2,1,0:T(8,128)S(1)} %sweep.27.own_ref), channel_id=1, source_target_pairs={{0,31},{1,2},{2,1},{3,4},{4,3},{5,6},{6,5},{7,8},{8,7},{9,10},{10,... | collective-permute-start | bytes 786440 | tf_op jit(solution)/shard_map/ppermute | solution.py:218
  37.3 4.8 %collective-permute-start.11 = (f32[8,64,128]{2,1,0:T(8,128)S(1)}, f32[8,64,128]{2,1,0:T(8,128)S(1)}, u32[]{:S(2)}, u32[]{:S(2)}) collective-permute-start(f32[8,64,128]{2,1,0:T(8,128)S(1)} %sweep.28.own_ref), channel_id=1, source_target_pairs={{0,1},{1,0},{2,3},{3,2},{4,5},{5,4},{6,7},{7,6},{8,9},{9,8},{10,11... | collective-permute-start | bytes 786440 | tf_op jit(solution)/shard_map/ppermute | solution.py:219
  38.0 9.7 %collective-permute-start.13 = (f32[8,64,128]{2,1,0:T(8,128)S(1)}, f32[8,64,128]{2,1,0:T(8,128)S(1)}, u32[]{:S(2)}, u32[]{:S(2)}) collective-permute-start(f32[8,64,128]{2,1,0:T(8,128)S(1)} %sweep.28.own_ref), channel_id=1, source_target_pairs={{0,31},{1,2},{2,1},{3,4},{4,3},{5,6},{6,5},{7,8},{8,7},{9,10},{10,... | collective-permute-start | bytes 786440 | tf_op jit(solution)/shard_map/ppermute | solution.py:218
  42.9 4.8 %collective-permute-start.14 = (f32[8,64,128]{2,1,0:T(8,128)S(1)}, f32[8,64,128]{2,1,0:T(8,128)S(1)}, u32[]{:S(2)}, u32[]{:S(2)}) collective-permute-start(f32[8,64,128]{2,1,0:T(8,128)S(1)} %sweep.29.own_ref), channel_id=1, source_target_pairs={{0,1},{1,0},{2,3},{3,2},{4,5},{5,4},{6,7},{7,6},{8,9},{9,8},{10,11... | collective-permute-start | bytes 786440 | tf_op jit(solution)/shard_map/ppermute | solution.py:219
  43.6 9.7 %collective-permute-start.12 = (f32[8,64,128]{2,1,0:T(8,128)S(1)}, f32[8,64,128]{2,1,0:T(8,128)S(1)}, u32[]{:S(2)}, u32[]{:S(2)}) collective-permute-start(f32[8,64,128]{2,1,0:T(8,128)S(1)} %sweep.29.own_ref), channel_id=1, source_target_pairs={{0,31},{1,2},{2,1},{3,4},{4,3},{5,6},{6,5},{7,8},{8,7},{9,10},{10,... | collective-permute-start | bytes 786440 | tf_op jit(solution)/shard_map/ppermute | solution.py:218
  48.5 4.8 %collective-permute-start.15 = (f32[8,64,128]{2,1,0:T(8,128)S(1)}, f32[8,64,128]{2,1,0:T(8,128)S(1)}, u32[]{:S(2)}, u32[]{:S(2)}) collective-permute-start(f32[8,64,128]{2,1,0:T(8,128)S(1)} %sweep.30.own_ref), channel_id=1, source_target_pairs={{0,1},{1,0},{2,3},{3,2},{4,5},{5,4},{6,7},{7,6},{8,9},{9,8},{10,11... | collective-permute-start | bytes 786440 | tf_op jit(solution)/shard_map/ppermute | solution.py:219
  49.2 9.7 %collective-permute-start.17 = (f32[8,64,128]{2,1,0:T(8,128)S(1)}, f32[8,64,128]{2,1,0:T(8,128)S(1)}, u32[]{:S(2)}, u32[]{:S(2)}) collective-permute-start(f32[8,64,128]{2,1,0:T(8,128)S(1)} %sweep.30.own_ref), channel_id=1, source_target_pairs={{0,31},{1,2},{2,1},{3,4},{4,3},{5,6},{6,5},{7,8},{8,7},{9,10},{10,... | collective-permute-start | bytes 786440 | tf_op jit(solution)/shard_map/ppermute | solution.py:218
  54.1 4.8 %collective-permute-start.18 = (f32[8,64,128]{2,1,0:T(8,128)S(1)}, f32[8,64,128]{2,1,0:T(8,128)S(1)}, u32[]{:S(2)}, u32[]{:S(2)}) collective-permute-start(f32[8,64,128]{2,1,0:T(8,128)S(1)} %sweep.31.own_ref), channel_id=1, source_target_pairs={{0,1},{1,0},{2,3},{3,2},{4,5},{5,4},{6,7},{7,6},{8,9},{9,8},{10,11... | collective-permute-start | bytes 786440 | tf_op jit(solution)/shard_map/ppermute | solution.py:219
  54.8 9.7 %collective-permute-start.16 = (f32[8,64,128]{2,1,0:T(8,128)S(1)}, f32[8,64,128]{2,1,0:T(8,128)S(1)}, u32[]{:S(2)}, u32[]{:S(2)}) collective-permute-start(f32[8,64,128]{2,1,0:T(8,128)S(1)} %sweep.31.own_ref), channel_id=1, source_target_pairs={{0,31},{1,2},{2,1},{3,4},{4,3},{5,6},{6,5},{7,8},{8,7},{9,10},{10,... | collective-permute-start | bytes 786440 | tf_op jit(solution)/shard_map/ppermute | solution.py:218
  59.7 4.8 %collective-permute-start.19 = (f32[8,64,128]{2,1,0:T(8,128)S(1)}, f32[8,64,128]{2,1,0:T(8,128)S(1)}, u32[]{:S(2)}, u32[]{:S(2)}) collective-permute-start(f32[8,64,128]{2,1,0:T(8,128)S(1)} %sweep.32.own_ref), channel_id=1, source_target_pairs={{0,1},{1,0},{2,3},{3,2},{4,5},{5,4},{6,7},{7,6},{8,9},{9,8},{10,11... | collective-permute-start | bytes 786440 | tf_op jit(solution)/shard_map/ppermute | solution.py:219
  60.4 9.7 %collective-permute-start.21 = (f32[8,64,128]{2,1,0:T(8,128)S(1)}, f32[8,64,128]{2,1,0:T(8,128)S(1)}, u32[]{:S(2)}, u32[]{:S(2)}) collective-permute-start(f32[8,64,128]{2,1,0:T(8,128)S(1)} %sweep.32.own_ref), channel_id=1, source_target_pairs={{0,31},{1,2},{2,1},{3,4},{4,3},{5,6},{6,5},{7,8},{8,7},{9,10},{10,... | collective-permute-start | bytes 786440 | tf_op jit(solution)/shard_map/ppermute | solution.py:218
  65.3 4.8 %collective-permute-start.22 = (f32[8,64,128]{2,1,0:T(8,128)S(1)}, f32[8,64,128]{2,1,0:T(8,128)S(1)}, u32[]{:S(2)}, u32[]{:S(2)}) collective-permute-start(f32[8,64,128]{2,1,0:T(8,128)S(1)} %sweep.33.own_ref), channel_id=1, source_target_pairs={{0,1},{1,0},{2,3},{3,2},{4,5},{5,4},{6,7},{7,6},{8,9},{9,8},{10,11... | collective-permute-start | bytes 786440 | tf_op jit(solution)/shard_map/ppermute | solution.py:219
  66.1 9.9 %collective-permute-start.20 = (f32[8,64,128]{2,1,0:T(8,128)S(1)}, f32[8,64,128]{2,1,0:T(8,128)S(1)}, u32[]{:S(2)}, u32[]{:S(2)}) collective-permute-start(f32[8,64,128]{2,1,0:T(8,128)S(1)} %sweep.33.own_ref), channel_id=1, source_target_pairs={{0,31},{1,2},{2,1},{3,4},{4,3},{5,6},{6,5},{7,8},{8,7},{9,10},{10,... | collective-permute-start | bytes 786440 | tf_op jit(solution)/shard_map/ppermute | solution.py:218
  71.1 4.8 %collective-permute-start.23 = (f32[8,64,128]{2,1,0:T(8,128)S(1)}, f32[8,64,128]{2,1,0:T(8,128)S(1)}, u32[]{:S(2)}, u32[]{:S(2)}) collective-permute-start(f32[8,64,128]{2,1,0:T(8,128)S(1)} %sweep.34.own_ref), channel_id=1, source_target_pairs={{0,1},{1,0},{2,3},{3,2},{4,5},{5,4},{6,7},{7,6},{8,9},{9,8},{10,11... | collective-permute-start | bytes 786440 | tf_op jit(solution)/shard_map/ppermute | solution.py:219
  71.9 9.5 %collective-permute-start.25 = (f32[8,64,128]{2,1,0:T(8,128)S(1)}, f32[8,64,128]{2,1,0:T(8,128)S(1)}, u32[]{:S(2)}, u32[]{:S(2)}) collective-permute-start(f32[8,64,128]{2,1,0:T(8,128)S(1)} %sweep.34.own_ref), channel_id=1, source_target_pairs={{0,31},{1,2},{2,1},{3,4},{4,3},{5,6},{6,5},{7,8},{8,7},{9,10},{10,... | collective-permute-start | bytes 786440 | tf_op jit(solution)/shard_map/ppermute | solution.py:218
  76.8 4.6 %collective-permute-start.26 = (f32[8,64,128]{2,1,0:T(8,128)S(1)}, f32[8,64,128]{2,1,0:T(8,128)S(1)}, u32[]{:S(2)}, u32[]{:S(2)}) collective-permute-start(f32[8,64,128]{2,1,0:T(8,128)S(1)} %sweep.35.own_ref), channel_id=1, source_target_pairs={{0,1},{1,0},{2,3},{3,2},{4,5},{5,4},{6,7},{7,6},{8,9},{9,8},{10,11... | collective-permute-start | bytes 786440 | tf_op jit(solution)/shard_map/ppermute | solution.py:219
  77.3 9.7 %collective-permute-start.24 = (f32[8,64,128]{2,1,0:T(8,128)S(1)}, f32[8,64,128]{2,1,0:T(8,128)S(1)}, u32[]{:S(2)}, u32[]{:S(2)}) collective-permute-start(f32[8,64,128]{2,1,0:T(8,128)S(1)} %sweep.35.own_ref), channel_id=1, source_target_pairs={{0,31},{1,2},{2,1},{3,4},{4,3},{5,6},{6,5},{7,8},{8,7},{9,10},{10,... | collective-permute-start | bytes 786440 | tf_op jit(solution)/shard_map/ppermute | solution.py:218
  82.2 4.8 %collective-permute-start.27 = (f32[8,64,128]{2,1,0:T(8,128)S(1)}, f32[8,64,128]{2,1,0:T(8,128)S(1)}, u32[]{:S(2)}, u32[]{:S(2)}) collective-permute-start(f32[8,64,128]{2,1,0:T(8,128)S(1)} %sweep.36.own_ref), channel_id=1, source_target_pairs={{0,1},{1,0},{2,3},{3,2},{4,5},{5,4},{6,7},{7,6},{8,9},{9,8},{10,11... | collective-permute-start | bytes 786440 | tf_op jit(solution)/shard_map/ppermute | solution.py:219
  82.9 9.7 %collective-permute-start.29 = (f32[8,64,128]{2,1,0:T(8,128)S(1)}, f32[8,64,128]{2,1,0:T(8,128)S(1)}, u32[]{:S(2)}, u32[]{:S(2)}) collective-permute-start(f32[8,64,128]{2,1,0:T(8,128)S(1)} %sweep.36.own_ref), channel_id=1, source_target_pairs={{0,31},{1,2},{2,1},{3,4},{4,3},{5,6},{6,5},{7,8},{8,7},{9,10},{10,... | collective-permute-start | bytes 786440 | tf_op jit(solution)/shard_map/ppermute | solution.py:218
  87.8 4.8 %collective-permute-start.30 = (f32[8,64,128]{2,1,0:T(8,128)S(1)}, f32[8,64,128]{2,1,0:T(8,128)S(1)}, u32[]{:S(2)}, u32[]{:S(2)}) collective-permute-start(f32[8,64,128]{2,1,0:T(8,128)S(1)} %sweep.37.own_ref), channel_id=1, source_target_pairs={{0,1},{1,0},{2,3},{3,2},{4,5},{5,4},{6,7},{7,6},{8,9},{9,8},{10,11... | collective-permute-start | bytes 786440 | tf_op jit(solution)/shard_map/ppermute | solution.py:219
  88.5 9.7 %collective-permute-start.28 = (f32[8,64,128]{2,1,0:T(8,128)S(1)}, f32[8,64,128]{2,1,0:T(8,128)S(1)}, u32[]{:S(2)}, u32[]{:S(2)}) collective-permute-start(f32[8,64,128]{2,1,0:T(8,128)S(1)} %sweep.37.own_ref), channel_id=1, source_target_pairs={{0,31},{1,2},{2,1},{3,4},{4,3},{5,6},{6,5},{7,8},{8,7},{9,10},{10,... | collective-permute-start | bytes 786440 | tf_op jit(solution)/shard_map/ppermute | solution.py:218
  93.4 4.8 %collective-permute-start.31 = (f32[8,64,128]{2,1,0:T(8,128)S(1)}, f32[8,64,128]{2,1,0:T(8,128)S(1)}, u32[]{:S(2)}, u32[]{:S(2)}) collective-permute-start(f32[8,64,128]{2,1,0:T(8,128)S(1)} %sweep.38.own_ref), channel_id=1, source_target_pairs={{0,1},{1,0},{2,3},{3,2},{4,5},{5,4},{6,7},{7,6},{8,9},{9,8},{10,11... | collective-permute-start | bytes 786440 | tf_op jit(solution)/shard_map/ppermute | solution.py:219
  94.1 9.7 %collective-permute-start.33 = (f32[8,64,128]{2,1,0:T(8,128)S(1)}, f32[8,64,128]{2,1,0:T(8,128)S(1)}, u32[]{:S(2)}, u32[]{:S(2)}) collective-permute-start(f32[8,64,128]{2,1,0:T(8,128)S(1)} %sweep.38.own_ref), channel_id=1, source_target_pairs={{0,31},{1,2},{2,1},{3,4},{4,3},{5,6},{6,5},{7,8},{8,7},{9,10},{10,... | collective-permute-start | bytes 786440 | tf_op jit(solution)/shard_map/ppermute | solution.py:218
  99.0 4.8 %collective-permute-start.34 = (f32[8,64,128]{2,1,0:T(8,128)S(1)}, f32[8,64,128]{2,1,0:T(8,128)S(1)}, u32[]{:S(2)}, u32[]{:S(2)}) collective-permute-start(f32[8,64,128]{2,1,0:T(8,128)S(1)} %sweep.39.own_ref), channel_id=1, source_target_pairs={{0,1},{1,0},{2,3},{3,2},{4,5},{5,4},{6,7},{7,6},{8,9},{9,8},{10,11... | collective-permute-start | bytes 786440 | tf_op jit(solution)/shard_map/ppermute | solution.py:219
  99.8 9.7 %collective-permute-start.32 = (f32[8,64,128]{2,1,0:T(8,128)S(1)}, f32[8,64,128]{2,1,0:T(8,128)S(1)}, u32[]{:S(2)}, u32[]{:S(2)}) collective-permute-start(f32[8,64,128]{2,1,0:T(8,128)S(1)} %sweep.39.own_ref), channel_id=1, source_target_pairs={{0,31},{1,2},{2,1},{3,4},{4,3},{5,6},{6,5},{7,8},{8,7},{9,10},{10,... | collective-permute-start | bytes 786440 | tf_op jit(solution)/shard_map/ppermute | solution.py:218
  104.7 4.8 %collective-permute-start.35 = (f32[8,64,128]{2,1,0:T(8,128)S(1)}, f32[8,64,128]{2,1,0:T(8,128)S(1)}, u32[]{:S(2)}, u32[]{:S(2)}) collective-permute-start(f32[8,64,128]{2,1,0:T(8,128)S(1)} %sweep.40.own_ref), channel_id=1, source_target_pairs={{0,1},{1,0},{2,3},{3,2},{4,5},{5,4},{6,7},{7,6},{8,9},{9,8},{10,11... | collective-permute-start | bytes 786440 | tf_op jit(solution)/shard_map/ppermute | solution.py:219
  105.4 9.7 %collective-permute-start.37 = (f32[8,64,128]{2,1,0:T(8,128)S(1)}, f32[8,64,128]{2,1,0:T(8,128)S(1)}, u32[]{:S(2)}, u32[]{:S(2)}) collective-permute-start(f32[8,64,128]{2,1,0:T(8,128)S(1)} %sweep.40.own_ref), channel_id=1, source_target_pairs={{0,31},{1,2},{2,1},{3,4},{4,3},{5,6},{6,5},{7,8},{8,7},{9,10},{10,... | collective-permute-start | bytes 786440 | tf_op jit(solution)/shard_map/ppermute | solution.py:218
  110.3 4.8 %collective-permute-start.38 = (f32[8,64,128]{2,1,0:T(8,128)S(1)}, f32[8,64,128]{2,1,0:T(8,128)S(1)}, u32[]{:S(2)}, u32[]{:S(2)}) collective-permute-start(f32[8,64,128]{2,1,0:T(8,128)S(1)} %sweep.41.own_ref), channel_id=1, source_target_pairs={{0,1},{1,0},{2,3},{3,2},{4,5},{5,4},{6,7},{7,6},{8,9},{9,8},{10,11... | collective-permute-start | bytes 786440 | tf_op jit(solution)/shard_map/ppermute | solution.py:219
  111.0 9.7 %collective-permute-start.36 = (f32[8,64,128]{2,1,0:T(8,128)S(1)}, f32[8,64,128]{2,1,0:T(8,128)S(1)}, u32[]{:S(2)}, u32[]{:S(2)}) collective-permute-start(f32[8,64,128]{2,1,0:T(8,128)S(1)} %sweep.41.own_ref), channel_id=1, source_target_pairs={{0,31},{1,2},{2,1},{3,4},{4,3},{5,6},{6,5},{7,8},{8,7},{9,10},{10,... | collective-permute-start | bytes 786440 | tf_op jit(solution)/shard_map/ppermute | solution.py:218
  115.9 4.8 %collective-permute-start.39 = (f32[8,64,128]{2,1,0:T(8,128)S(1)}, f32[8,64,128]{2,1,0:T(8,128)S(1)}, u32[]{:S(2)}, u32[]{:S(2)}) collective-permute-start(f32[8,64,128]{2,1,0:T(8,128)S(1)} %sweep.42.own_ref), channel_id=1, source_target_pairs={{0,1},{1,0},{2,3},{3,2},{4,5},{5,4},{6,7},{7,6},{8,9},{9,8},{10,11... | collective-permute-start | bytes 786440 | tf_op jit(solution)/shard_map/ppermute | solution.py:219
  116.6 9.7 %collective-permute-start.41 = (f32[8,64,128]{2,1,0:T(8,128)S(1)}, f32[8,64,128]{2,1,0:T(8,128)S(1)}, u32[]{:S(2)}, u32[]{:S(2)}) collective-permute-start(f32[8,64,128]{2,1,0:T(8,128)S(1)} %sweep.42.own_ref), channel_id=1, source_target_pairs={{0,31},{1,2},{2,1},{3,4},{4,3},{5,6},{6,5},{7,8},{8,7},{9,10},{10,... | collective-permute-start | bytes 786440 | tf_op jit(solution)/shard_map/ppermute | solution.py:218
  121.5 4.8 %collective-permute-start.42 = (f32[8,64,128]{2,1,0:T(8,128)S(1)}, f32[8,64,128]{2,1,0:T(8,128)S(1)}, u32[]{:S(2)}, u32[]{:S(2)}) collective-permute-start(f32[8,64,128]{2,1,0:T(8,128)S(1)} %sweep.43.own_ref), channel_id=1, source_target_pairs={{0,1},{1,0},{2,3},{3,2},{4,5},{5,4},{6,7},{7,6},{8,9},{9,8},{10,11... | collective-permute-start | bytes 786440 | tf_op jit(solution)/shard_map/ppermute | solution.py:219
  122.2 9.7 %collective-permute-start.40 = (f32[8,64,128]{2,1,0:T(8,128)S(1)}, f32[8,64,128]{2,1,0:T(8,128)S(1)}, u32[]{:S(2)}, u32[]{:S(2)}) collective-permute-start(f32[8,64,128]{2,1,0:T(8,128)S(1)} %sweep.43.own_ref), channel_id=1, source_target_pairs={{0,31},{1,2},{2,1},{3,4},{4,3},{5,6},{6,5},{7,8},{8,7},{9,10},{10,... | collective-permute-start | bytes 786440 | tf_op jit(solution)/shard_map/ppermute | solution.py:218
  127.1 4.8 %collective-permute-start.43 = (f32[8,64,128]{2,1,0:T(8,128)S(1)}, f32[8,64,128]{2,1,0:T(8,128)S(1)}, u32[]{:S(2)}, u32[]{:S(2)}) collective-permute-start(f32[8,64,128]{2,1,0:T(8,128)S(1)} %sweep.44.own_ref), channel_id=1, source_target_pairs={{0,1},{1,0},{2,3},{3,2},{4,5},{5,4},{6,7},{7,6},{8,9},{9,8},{10,11... | collective-permute-start | bytes 786440 | tf_op jit(solution)/shard_map/ppermute | solution.py:219
  127.9 9.7 %collective-permute-start.45 = (f32[8,64,128]{2,1,0:T(8,128)S(1)}, f32[8,64,128]{2,1,0:T(8,128)S(1)}, u32[]{:S(2)}, u32[]{:S(2)}) collective-permute-start(f32[8,64,128]{2,1,0:T(8,128)S(1)} %sweep.44.own_ref), channel_id=1, source_target_pairs={{0,31},{1,2},{2,1},{3,4},{4,3},{5,6},{6,5},{7,8},{8,7},{9,10},{10,... | collective-permute-start | bytes 786440 | tf_op jit(solution)/shard_map/ppermute | solution.py:218
  132.8 4.8 %collective-permute-start.46 = (f32[8,64,128]{2,1,0:T(8,128)S(1)}, f32[8,64,128]{2,1,0:T(8,128)S(1)}, u32[]{:S(2)}, u32[]{:S(2)}) collective-permute-start(f32[8,64,128]{2,1,0:T(8,128)S(1)} %sweep.45.own_ref), channel_id=1, source_target_pairs={{0,1},{1,0},{2,3},{3,2},{4,5},{5,4},{6,7},{7,6},{8,9},{9,8},{10,11... | collective-permute-start | bytes 786440 | tf_op jit(solution)/shard_map/ppermute | solution.py:219
  133.5 9.5 %collective-permute-start.44 = (f32[8,64,128]{2,1,0:T(8,128)S(1)}, f32[8,64,128]{2,1,0:T(8,128)S(1)}, u32[]{:S(2)}, u32[]{:S(2)}) collective-permute-start(f32[8,64,128]{2,1,0:T(8,128)S(1)} %sweep.45.own_ref), channel_id=1, source_target_pairs={{0,31},{1,2},{2,1},{3,4},{4,3},{5,6},{6,5},{7,8},{8,7},{9,10},{10,... | collective-permute-start | bytes 786440 | tf_op jit(solution)/shard_map/ppermute | solution.py:218
  138.4 4.6 %collective-permute-start.47 = (f32[8,64,128]{2,1,0:T(8,128)S(1)}, f32[8,64,128]{2,1,0:T(8,128)S(1)}, u32[]{:S(2)}, u32[]{:S(2)}) collective-permute-start(f32[8,64,128]{2,1,0:T(8,128)S(1)} %sweep.46.refs_0_), channel_id=1, source_target_pairs={{0,1},{1,0},{2,3},{3,2},{4,5},{5,4},{6,7},{7,6},{8,9},{9,8},{10,11... | collective-permute-start | bytes 786440 | tf_op jit(solution)/shard_map/ppermute | solution.py:219
  143.8 1.6 %collective-permute-start.48 = (f32[8,64,128]{2,1,0:T(8,128)S(1)}, f32[8,64,128]{2,1,0:T(8,128)S(1)}, u32[]{:S(2)}, u32[]{:S(2)}) collective-permute-start(f32[8,64,128]{2,1,0:T(8,128)S(1)} %sweep.47.refs_1_), channel_id=1, source_target_pairs={{0,1},{1,0},{2,3},{3,2},{4,5},{5,4},{6,7},{7,6},{8,9},{9,8},{10,11... | collective-permute-start | bytes 786440 | tf_op jit(solution)/shard_map/ppermute | solution.py:219
